TPU v7x, 32 devices: a whole 2x2x4 slice. The times are simulated.
32 devices in a mesh: dp: 16 (over z, y, x), tensor: 2 (over core).
Axes of the slice: x: 2, y: 2, z: 4, core: 2. Of those that a mesh axis runs over, the one named last changes fastest.
Arguments:
- stream: bfloat16 [10240, 1024], P(('dp', 'tensor')), may hold values from -24 to 24
- counts: int32 [32], P('dp'), may hold values from 16 to 256
- cotangent: bfloat16 [10240, 1024], P(('dp', 'tensor')), may hold values from -6 to 6
- w_qkv: bfloat16 [3, 1024, 1024], P(None, 'dp', 'tensor'), may hold values from -0.1875 to 0.1875
- b_qv: float32 [2, 1024], replicated, may hold values from -1.5 to 1.5
- w_out: bfloat16 [1024, 1024], P('tensor', 'dp'), may hold values from -0.75 to 0.75
- b_out: float32 [1024], replicated, may hold values from -1.8 to 1.8
- w_fc1: bfloat16 [1024, 4096], P('dp', 'tensor'), may hold values from -0.35 to 0.35
- b_fc1: float32 [4096], replicated, may hold values from -3 to 3
- w_fc2: bfloat16 [4096, 1024], P('tensor', 'dp'), may hold values from -0.09375 to 0.09375
- b_fc2: float32 [1024], replicated, may hold values from -1.8 to 1.8
- gain_one: float32 [1024], replicated, may hold values from 0.25 to 1.75
- shift_one: float32 [1024], replicated, may hold values from -1.8 to 1.8
- gain_two: float32 [1024], replicated, may hold values from 0.25 to 1.75
- shift_two: float32 [1024], replicated, may hold values from -1.8 to 1.8
Outputs:
- activations: bfloat16 [10240, 1024], P(('dp', 'tensor'))
- grad_input: float32 [10240, 1024], P(('dp', 'tensor'))
- grad_w_qkv: float32 [3, 1024, 1024], P(None, 'dp', 'tensor')
- grad_b_qv: float32 [2, 1024], P(None, ('dp', 'tensor'))
- grad_w_out: float32 [1024, 1024], P('tensor', 'dp')
- grad_b_out: float32 [1024], P(('dp', 'tensor'))
- grad_w_fc1: float32 [1024, 4096], P('dp', 'tensor')
- grad_b_fc1: float32 [4096], P(('dp', 'tensor'))
- grad_w_fc2: float32 [4096, 1024], P('tensor', 'dp')
- grad_b_fc2: float32 [1024], P(('dp', 'tensor'))
- grad_gain_one: float32 [1024], P(('dp', 'tensor'))
- grad_shift_one: float32 [1024], P(('dp', 'tensor'))
- grad_gain_two: float32 [1024], P(('dp', 'tensor'))
- grad_shift_two: float32 [1024], P(('dp', 'tensor'))
- rms_stats: float32 [5], replicated
All inputs are finite; a program needn't handle non-finite values.
Results may differ from a plain program's by a relative error of at most 0.02.
Values may be sent and summed in bfloat16 or wider, within the bound.
A program may use at most 128 MiB of HBM per device.

v0:
```python
import jax
import jax.numpy as jnp
from jax import lax
from jax.sharding import PartitionSpec as P

HD = 64
BUFFER = 64
SLOTS = 320


eps_norm = 1e-06


def layer_norm(values, gain, shift):
    centre = jnp.mean(values, axis=-1, keepdims=True)
    offset = values - centre
    spread = jnp.mean(offset * offset, axis=-1, keepdims=True)
    return offset * lax.rsqrt(spread + eps_norm) * gain + shift


def gelu_exact(values):
    return jax.nn.gelu(values, approximate=False)


def masked_scores(queries, key_rows, validity):
    scores = jnp.einsum(
        "bqhd,bkhd->bhqk", queries, key_rows, preferred_element_type=jnp.float32
    ) * HD ** (-0.5)
    return jnp.where(validity[:, None, None, :] > 0, scores, -1e30)


def attend_block(members):
    queries, key_rows, values, validity = members
    scores = masked_scores(queries, key_rows, validity)
    highest = jnp.max(scores, axis=-1, keepdims=True)
    expo_terms = jnp.exp(scores - highest)
    totals = jnp.sum(expo_terms, axis=-1, keepdims=True)
    weights = (expo_terms / totals).astype(jnp.bfloat16)
    mixture = jnp.einsum("bhqk,bkhd->bqhd", weights, values, preferred_element_type=jnp.float32)
    return (mixture.astype(jnp.bfloat16), (highest + jnp.log(totals))[..., 0])


def attend_back(members):
    queries, key_rows, values, validity, log_total, d_mixture = members
    scores = masked_scores(queries, key_rows, validity)
    probs = jnp.exp(scores - log_total[..., None])
    d_values = jnp.einsum(
        "bhqk,bqhd->bkhd", probs.astype(jnp.bfloat16), d_mixture, preferred_element_type=jnp.float32
    )
    d_probs = jnp.einsum("bqhd,bkhd->bhqk", d_mixture, values, preferred_element_type=jnp.float32)
    d_scores = (probs * (d_probs - jnp.sum(probs * d_probs, axis=-1, keepdims=True))).astype(
        jnp.bfloat16
    )
    d_queries = jnp.einsum(
        "bhqk,bkhd->bqhd", d_scores, key_rows, preferred_element_type=jnp.float32
    ) * HD ** (-0.5)
    d_keys = jnp.einsum(
        "bhqk,bqhd->bkhd", d_scores, queries, preferred_element_type=jnp.float32
    ) * HD ** (-0.5)
    return (
        d_queries.astype(jnp.bfloat16),
        d_keys.astype(jnp.bfloat16),
        d_values.astype(jnp.bfloat16),
    )


def local(
    stream,
    counts,
    cotangent,
    w_qkv,
    b_qv,
    w_out,
    b_out,
    w_fc1,
    b_fc1,
    w_fc2,
    b_fc2,
    gain_one,
    shift_one,
    gain_two,
    shift_two,
):
    tensor_pos = lax.axis_index("tensor")
    own_rows = stream.shape[0]
    width = stream.shape[1]
    own_images = own_rows // SLOTS
    slot_index = jnp.arange(SLOTS, dtype=jnp.int32)
    validity_all = (slot_index[None, :] < (BUFFER + counts)[:, None]).astype(jnp.float32)
    own_validity = lax.dynamic_slice_in_dim(validity_all, tensor_pos * own_images, own_images, 0)
    own_valid = own_validity.reshape(own_rows, 1)
    qkv_full, out_full, up_full, down_full = (
        lax.all_gather(w_qkv, "dp", axis=1, tiled=True),
        lax.all_gather(w_out, "dp", axis=1, tiled=True),
        lax.all_gather(w_fc1[None], "dp", axis=1, tiled=True),
        lax.all_gather(w_fc2, "dp", axis=1, tiled=True),
    )
    head_width = w_qkv.shape[2]
    unit_width = w_fc1.shape[1]
    bias_query = lax.dynamic_slice_in_dim(b_qv[0], tensor_pos * head_width, head_width, 0)
    bias_value = lax.dynamic_slice_in_dim(b_qv[1], tensor_pos * head_width, head_width, 0)
    bias_up = lax.dynamic_slice_in_dim(b_fc1, tensor_pos * unit_width, unit_width, 0)
    up_full = up_full[0]
    group_images = validity_all.shape[0]
    group_rows = group_images * SLOTS
    local_heads = head_width // HD
    pairing = 2
    block_count = group_images // pairing
    blocked_valid = validity_all.reshape(block_count, pairing, SLOTS)
    stream_f = stream.astype(jnp.float32)
    normed_one = layer_norm(stream_f, gain_one, shift_one).astype(jnp.bfloat16)
    first_rows = lax.all_gather(normed_one, "tensor", axis=0, tiled=True)
    projected = jnp.einsum("rd,cde->rce", first_rows, qkv_full, preferred_element_type=jnp.float32)
    shape_heads = (block_count, pairing, SLOTS, local_heads, HD)
    queries = (projected[:, 0] + bias_query).astype(jnp.bfloat16).reshape(shape_heads)
    key_rows = projected[:, 1].astype(jnp.bfloat16).reshape(shape_heads)
    values = (projected[:, 2] + bias_value).astype(jnp.bfloat16).reshape(shape_heads)
    mixture, log_total = lax.map(attend_block, (queries, key_rows, values, blocked_valid))
    attn_heads = mixture.reshape(group_rows, head_width)
    taken = attn_heads
    attn_total = lax.psum_scatter(
        jnp.dot(taken, out_full, preferred_element_type=jnp.float32).astype(jnp.bfloat16),
        "tensor",
        scatter_dimension=0,
        tiled=True,
    ).astype(jnp.float32)
    branch = attn_total + b_out
    middle = stream_f + branch
    normed_two = layer_norm(middle, gain_two, shift_two).astype(jnp.bfloat16)
    second_rows = lax.all_gather(normed_two, "tensor", axis=0, tiled=True)
    hidden_pre = jnp.dot(second_rows, up_full, preferred_element_type=jnp.float32) + bias_up
    hidden_act = gelu_exact(hidden_pre).astype(jnp.bfloat16)
    taken = hidden_act
    mlp_total = lax.psum_scatter(
        jnp.dot(taken, down_full, preferred_element_type=jnp.float32).astype(jnp.bfloat16),
        "tensor",
        scatter_dimension=0,
        tiled=True,
    ).astype(jnp.float32)
    feed = mlp_total + b_fc2
    result = middle + feed
    activations = (result * own_valid).astype(jnp.bfloat16)
    squares = jnp.stack(
        [
            jnp.sum(own_valid * member * member)
            for member in (stream_f, middle, result, branch, feed)
        ]
    )
    square_sums, valid_count = lax.psum((squares, jnp.sum(own_valid)), ("dp", "tensor"))
    rms_stats = jnp.sqrt(square_sums / (valid_count * width))
    d_result = cotangent.astype(jnp.float32) * own_valid
    d_feed_low = d_result.astype(jnp.bfloat16)
    d_feed_rows = lax.all_gather(d_feed_low, "tensor", axis=0, tiled=True)
    d_act = jnp.einsum("rd,ud->ru", d_feed_rows, down_full, preferred_element_type=jnp.float32)
    unused_act, gelu_pullback = jax.vjp(gelu_exact, hidden_pre)
    d_pre = gelu_pullback(d_act)[0].astype(jnp.bfloat16)
    grad_down = jnp.einsum("ru,rd->ud", hidden_act, d_feed_rows, preferred_element_type=jnp.float32)
    grad_up = jnp.einsum("rd,ru->du", second_rows, d_pre, preferred_element_type=jnp.float32)
    grad_bias_up = jnp.sum(d_pre, axis=0, dtype=jnp.float32)
    grad_bias_down = jnp.sum(d_feed_low, axis=0, dtype=jnp.float32)
    taken = d_pre
    d_normed_two = lax.psum_scatter(
        jnp.einsum("ru,du->rd", taken, up_full, preferred_element_type=jnp.float32).astype(
            jnp.bfloat16
        ),
        "tensor",
        scatter_dimension=0,
        tiled=True,
    ).astype(jnp.float32)
    unused_two, norm_two_pullback = jax.vjp(layer_norm, middle, gain_two, shift_two)
    d_middle_norm, grad_gain_two, grad_shift_two = norm_two_pullback(d_normed_two)
    d_middle = d_result + d_middle_norm
    d_branch_low = d_middle.astype(jnp.bfloat16)
    grad_bias_out = jnp.sum(d_branch_low, axis=0, dtype=jnp.float32)
    d_branch_rows = lax.all_gather(d_branch_low, "tensor", axis=0, tiled=True)
    d_attn = jnp.einsum(
        "rd,hd->rh", d_branch_rows, out_full, preferred_element_type=jnp.float32
    ).astype(jnp.bfloat16)
    grad_out = jnp.einsum(
        "rh,rd->hd", attn_heads, d_branch_rows, preferred_element_type=jnp.float32
    )
    d_queries, d_keys, d_values = lax.map(
        attend_back,
        (queries, key_rows, values, blocked_valid, log_total, d_attn.reshape(shape_heads)),
    )
    d_projected = jnp.stack(
        [
            d_queries.reshape(group_rows, head_width),
            d_keys.reshape(group_rows, head_width),
            d_values.reshape(group_rows, head_width),
        ],
        axis=1,
    )
    grad_qkv = jnp.einsum(
        "rd,rce->cde", first_rows, d_projected, preferred_element_type=jnp.float32
    )
    bias_terms = jnp.sum(d_projected, axis=0, dtype=jnp.float32)
    taken = d_projected
    d_normed_one = lax.psum_scatter(
        jnp.einsum("rce,cde->rd", taken, qkv_full, preferred_element_type=jnp.float32).astype(
            jnp.bfloat16
        ),
        "tensor",
        scatter_dimension=0,
        tiled=True,
    ).astype(jnp.float32)
    unused_one, norm_one_pullback = jax.vjp(layer_norm, stream_f, gain_one, shift_one)
    d_stream_norm, grad_gain_one, grad_shift_one = norm_one_pullback(d_normed_one)
    grad_input = d_middle + d_stream_norm
    grad_up = grad_up[None]
    bias_qv_full = lax.dynamic_update_slice(
        jnp.zeros((2, width), jnp.float32),
        jnp.stack([bias_terms[0], bias_terms[2]]),
        (jnp.int32(0), tensor_pos * head_width),
    )
    bias_up_full = lax.dynamic_update_slice(
        jnp.zeros((b_fc1.shape[0],), jnp.float32), grad_bias_up, (tensor_pos * unit_width,)
    )
    qkv_part, out_part, up_part, down_part = (
        lax.psum_scatter(
            grad_qkv.astype(jnp.bfloat16), "dp", scatter_dimension=1, tiled=True
        ).astype(jnp.float32),
        lax.psum_scatter(
            grad_out.astype(jnp.bfloat16), "dp", scatter_dimension=1, tiled=True
        ).astype(jnp.float32),
        lax.psum_scatter(
            grad_up.astype(jnp.bfloat16), "dp", scatter_dimension=1, tiled=True
        ).astype(jnp.float32),
        lax.psum_scatter(
            grad_down.astype(jnp.bfloat16), "dp", scatter_dimension=1, tiled=True
        ).astype(jnp.float32),
    )
    small_parts = (
        lax.psum_scatter(bias_qv_full, ("dp", "tensor"), scatter_dimension=1, tiled=True),
        lax.psum_scatter(grad_bias_out, ("dp", "tensor"), scatter_dimension=0, tiled=True),
        lax.psum_scatter(bias_up_full, ("dp", "tensor"), scatter_dimension=0, tiled=True),
        lax.psum_scatter(grad_bias_down, ("dp", "tensor"), scatter_dimension=0, tiled=True),
        lax.psum_scatter(grad_gain_one, ("dp", "tensor"), scatter_dimension=0, tiled=True),
        lax.psum_scatter(grad_shift_one, ("dp", "tensor"), scatter_dimension=0, tiled=True),
        lax.psum_scatter(grad_gain_two, ("dp", "tensor"), scatter_dimension=0, tiled=True),
        lax.psum_scatter(grad_shift_two, ("dp", "tensor"), scatter_dimension=0, tiled=True),
    )
    return (
        activations,
        grad_input,
        qkv_part,
        small_parts[0],
        out_part,
        small_parts[1],
        up_part[0],
        small_parts[2],
        down_part,
        small_parts[3],
        small_parts[4],
        small_parts[5],
        small_parts[6],
        small_parts[7],
        rms_stats,
    )


def solution(mesh):
    return jax.shard_map(
        local,
        mesh=mesh,
        in_specs=(
            P(("dp", "tensor"), None),
            P("dp"),
            P(("dp", "tensor"), None),
            P(None, "dp", "tensor"),
            P(),
            P("tensor", "dp"),
            P(),
            P("dp", "tensor"),
            P(),
            P("tensor", "dp"),
            P(),
            P(),
            P(),
            P(),
            P(),
        ),
        out_specs=(
            P(("dp", "tensor"), None),
            P(("dp", "tensor"), None),
            P(None, "dp", "tensor"),
            P(None, ("dp", "tensor")),
            P("tensor", "dp"),
            P(("dp", "tensor")),
            P("dp", "tensor"),
            P(("dp", "tensor")),
            P("tensor", "dp"),
            P(("dp", "tensor")),
            P(("dp", "tensor")),
            P(("dp", "tensor")),
            P(("dp", "tensor")),
            P(("dp", "tensor")),
            P(),
        ),
        check_vma=False,
    )
```

profile of v0, /device:TPU:0, one launch (start us, length us, event | category | flops | bytes accessed | tf_op | source)
XLA Modules:
  0.0 1049.0 jit_solution(8814430301375439884)
XLA Ops:
  10.0 2.3 fusion.26
  14.7 9.8 all-gather.10.cloned.1.call-done
  24.5 71.6 %all-gather.12.cloned.1.call-done = bf16[3,1024,512]{2,1,0:T(8,128)(2,1)} async-done(((bf16[3,64,512]{2,1,0:T(8,128)(2,1)}), bf16[3,1024,512]{2,1,0:T(8,128)(2,1)}) %all-gather.12.cloned.1.call-update) | async-done | bytes 3145744 | tf_op jit(solution)/shard_map/all_gather | solution.py:93
  96.1 4.5 fusion.38
  103.8 2.0 copy.98
  105.8 2.0 reshape.163
  107.9 2.3 copy.96
  110.1 5.3 fusion.12
  115.4 2.9 reshape.162
  118.4 3.1 copy.94
  121.5 4.8 fusion
  127.1 3.7 fusion.42
  133.1 20.2 %all-gather.14.cloned.1.call-done = bf16[512,1024]{0,1:T(8,128)(2,1)} async-done(((bf16[512,64]{0,1:T(8,128)(2,1)}), bf16[512,1024]{0,1:T(8,128)(2,1)}) %all-gather.14.cloned.1.call-update) | async-done | bytes 1048592 | tf_op jit(solution)/shard_map/all_gather | solution.py:94
  153.2 3.4 convolution_convert_fusion.3
  157.3 7.1 reduce-scatter.11.cloned.1.call-done
  168.6 1.9 add_convert_fusion.3
  176.0 68.7 %all-gather.24.cloned.1.call-done = bf16[1024,2048]{1,0:T(8,128)(2,1)} async-done(((bf16[64,2048]{1,0:T(8,128)(2,1)}), bf16[1024,2048]{1,0:T(8,128)(2,1)}) %all-gather.24.cloned.1.call-update) | async-done | bytes 4194320 | tf_op jit(solution)/shard_map/all_gather | solution.py:95
  244.7 10.1 all-gather.16.cloned.1.call-done
  254.8 7.8 fusion.68
  262.6 5.0 all-gather.20.cloned.1.call-done
  267.6 80.4 %all-gather.18.cloned.1.call-done = bf16[2048,1024]{0,1:T(8,128)(2,1)} async-done(((bf16[2048,64]{0,1:T(8,128)(2,1)}), bf16[2048,1024]{0,1:T(8,128)(2,1)}) %all-gather.18.cloned.1.call-update) | async-done | bytes 4194320 | tf_op jit(solution)/shard_map/all_gather | solution.py:96
  348.0 18.7 %convert_reduce_fusion = (f32[2048]{0:T(1024)}, bf16[640,2048]{1,0:T(8,128)(2,1)}, f32[640,2048]{1,0:T(8,128)S(1)}) fusion(f32[640,2048]{1,0:T(8,128)} %fusion.68, f32[2048]{0:T(1024)} %dynamic_slice.37, bf16[640,1024]{1,0:T(8,128)(2,1)} %all-gather.20.cloned.1.call-done, bf16[2048,1024]{0,1:T(8,128)(2,1)} %all-gather.18.cloned.1.call-done), kind=kOutput, calls=%fused_computation.10 | convolution fusion | flops 2782656512 | bytes 18628608 | tf_op jit(solution)/shard_map/rd,ud->ru/dot_general | solution.py:154
  369.6 4.0 convolution_convert_fusion.2
  373.7 7.0 convolution_convert_fusion.1
  381.2 12.1 %reduce-scatter.15.cloned.1.call-done = bf16[320,1024]{1,0:T(8,128)(2,1)} async-done(((bf16[640,1024]{1,0:T(8,128)(2,1)}), bf16[320,1024]{1,0:T(8,128)(2,1)}) %reduce-scatter.15.cloned.1.call-update) | async-done | bytes 655376 | tf_op jit(solution)/shard_map/reduce_scatter | solution.py:162
  393.3 4.5 fusion.28
  403.3 10.1 all-gather.22.cloned.1.call-done
  413.4 2.5 convolution_convert_fusion.5
  417.6 2.5 copy.102
  420.2 6.4 fusion.43
  426.6 6.2 multiply_reduce_fusion
  432.9 2.4 multiply_convert_fusion
  435.3 2.2 fusion.47
  452.0 3.5 convolution_convert_fusion.4
  455.6 5.2 bitcast_convert_fusion
  460.9 5.4 convert_bitcast_fusion.1
  466.2 7.6 copy.115
  475.2 6.8 convolution_convert_fusion
  483.3 6.8 convert_bitcast_fusion
  492.3 3.3 stack.31
  495.6 91.5 %reduce-scatter.25.cloned.1.call-done = f32[32,2]{1,0:T(8,128)} async-done(((f32[1024,2]{1,0:T(8,128)}), f32[32,2]{1,0:T(8,128)}) %reduce-scatter.25.cloned.1.call-update) | async-done | bytes 272
  588.5 74.4 %reduce-scatter.19.cloned.1.call-done = bf16[512,64]{0,1:T(8,128)(2,1)} async-done(((bf16[512,1024]{0,1:T(8,128)(2,1)}), bf16[512,64]{0,1:T(8,128)(2,1)}) %reduce-scatter.19.cloned.1.call-update) | async-done | bytes 65552 | tf_op jit(solution)/shard_map/reduce_scatter | solution.py:223
  664.4 6.7 reduce-scatter.17.cloned.1.call-done
  672.8 1.9 fusion.30
  674.7 44.3 %all-reduce.8 = (f32[1024]{0:T(1024)S(1)}, f32[4096]{0:T(1024)S(1)}, f32[1024]{0:T(1024)S(1)}, f32[1024]{0:T(1024)S(1)}, f32[1024]{0:T(1024)S(1)}, /*index=5*/f3...) all-reduce(f32[1024]{0:T(1024)S(1)} %copy-done.42, ...), channel_id=10, replica_groups=mesh['dp'=16,'tensor'=2] {'dp','tensor'}, use_global_device_ids=true, to_apply=%region_20.21.clone | all-reduce | flops 10246 | bytes 81968
  726.1 121.1 %all-reduce.11.cloned.1.call-done = bf16[3,1024,512]{2,0,1:T(4,128)(2,1)} async-done(((bf16[3,1024,512]{2,0,1:T(4,128)(2,1)}), bf16[3,1024,512]{2,0,1:T(4,128)(2,1)}) %all-reduce.11.cloned.1.call-update) | async-done | bytes 3145744
  849.0 94.5 %reduce-scatter.23.cloned.1.call-done = bf16[2048,64]{0,1:T(8,128)(2,1)} async-done(((bf16[2048,1024]{0,1:T(8,128)(2,1)}), bf16[2048,64]{0,1:T(8,128)(2,1)}) %reduce-scatter.23.cloned.1.call-update) | async-done | bytes 262160 | tf_op jit(solution)/shard_map/reduce_scatter | solution.py:229
  945.3 95.2 %reduce-scatter.21.cloned.1.call-done = bf16[1,64,2048]{2,1,0:T(8,128)(2,1)} async-done(((bf16[1,1024,2048]{2,1,0:T(8,128)(2,1)}), bf16[1,64,2048]{2,1,0:T(8,128)(2,1)}) %reduce-scatter.21.cloned.1.call-update) | async-done | bytes 262160 | tf_op jit(solution)/shard_map/reduce_scatter | solution.py:226
  (206 shorter events, 67.2 us)
Async XLA Ops:
  7.2 6.6 copy-start.48
  7.2 7.3 copy-start.43
  7.2 17.3 %all-gather.10.cloned.1.call-start = ((), (), s32[]{:S(2)}) async-start(), calls=%async_computation.8 | async-start | bytes 1966080 | tf_op jit(solution)/shard_map/all_gather | solution.py:112
  8.5 87.6 %copy-start.23 = (f32[320]{0:T(512)}, f32[320]{0:T(512)S(1)}, u32[]{:S(2)}) copy-start(f32[320]{0:T(512)S(1)} %broadcast_multiply_fusion.1) | copy-start | bytes 3844
  9.9 86.1 %copy-start.36 = (f32[320]{0:T(512)}, f32[320]{0:T(512)S(1)}, u32[]{:S(2)}) copy-start(f32[320]{0:T(512)S(1)} %fusion.34) | copy-start | bytes 3844
  10.0 86.1 %copy-start.30 = (f32[320]{0:T(512)}, f32[320]{0:T(512)S(1)}, u32[]{:S(2)}) copy-start(f32[320]{0:T(512)S(1)} %fusion.53) | copy-start | bytes 3844
  12.3 83.8 %all-gather.12.cloned.1.call-start = ((), (), s32[]{:S(2)}) async-start(), calls=%async_computation.9 | async-start | bytes 3342336 | tf_op jit(solution)/shard_map/all_gather | solution.py:93
  13.0 140.2 %all-gather.14.cloned.1.call-start = ((), (), s32[]{:S(2)}) async-start(), calls=%async_computation.10 | async-start | bytes 1114112 | tf_op jit(solution)/shard_map/all_gather | solution.py:94
  13.7 150.7 %reduce-scatter.11.cloned.1.call-start = ((), (), s32[]{:S(2)}) async-start(), calls=%async_computation.11 | async-start | bytes 1966080 | tf_op jit(solution)/shard_map/reduce_scatter | solution.py:121
  14.6 111.7 %copy-start.28 = (f32[8,64]{1,0:T(8,128)}, f32[8,64]{1,0:T(8,128)S(1)}, u32[]{:S(2)}) copy-start(f32[8,64]{1,0:T(8,128)S(1)} %add.165) | copy-start | bytes 6148
  115.4 10.9 %copy-start.17 = (f32[2,8,320]{2,1,0:T(8,128)}, f32[2,8,320]{2,1,0:T(8,128)S(1)}, u32[]{:S(2)}) copy-start(f32[2,8,320]{2,1,0:T(8,128)S(1)} %get-tuple-element.169) | copy-start | bytes 61444
  133.1 31.3 %copy-start.1 = (bf16[320,1024]{1,0:T(8,128)(2,1)S(1)}, bf16[320,1024]{1,0:T(8,128)(2,1)}, u32[]{:S(2)}) copy-start(bf16[320,1024]{1,0:T(8,128)(2,1)} %param.15) | copy-start | bytes 1966084
  133.1 31.3 %copy-start.20 = (f32[1024]{0:T(1024)S(1)}, f32[1024]{0:T(1024)}, u32[]{:S(2)}) copy-start(f32[1024]{0:T(1024)} %param.21) | copy-start | bytes 12292
  156.6 12.0 %copy-start.27 = (f32[1024]{0:T(1024)S(1)}, f32[1024]{0:T(1024)}, u32[]{:S(2)}) copy-start(f32[1024]{0:T(1024)} %param.28) | copy-start | bytes 12292
  156.6 88.0 %all-gather.24.cloned.1.call-start = ((), (), s32[]{:S(2)}) async-start(), calls=%async_computation.22 | async-start | bytes 4456448 | tf_op jit(solution)/shard_map/all_gather | solution.py:95
  157.2 14.6 %copy-start.8 = (bf16[320,1024]{1,0:T(8,128)(2,1)S(1)}, bf16[320,1024]{1,0:T(8,128)(2,1)}, u32[]{:S(2)}) copy-start(bf16[320,1024]{1,0:T(8,128)(2,1)} %param.17) | copy-start | bytes 1966084
  157.3 97.5 %all-gather.16.cloned.1.call-start = ((), (), s32[]{:S(2)}) async-start(), calls=%async_computation.12 | async-start | bytes 1966080 | tf_op jit(solution)/shard_map/all_gather | solution.py:130
  170.5 97.1 %all-gather.20.cloned.1.call-start = ((), (), s32[]{:S(2)}) async-start(), calls=%async_computation.15 | async-start | bytes 1966080 | tf_op jit(solution)/shard_map/all_gather | solution.py:153
  173.5 174.5 %all-gather.18.cloned.1.call-start = ((), (), s32[]{:S(2)}) async-start(), calls=%async_computation.13 | async-start | bytes 4456448 | tf_op jit(solution)/shard_map/all_gather | solution.py:96
  174.3 206.9 %reduce-scatter.13.cloned.1.call-start = ((), (), s32[]{:S(2)}) async-start(), calls=%async_computation.14 | async-start | bytes 1966080 | tf_op jit(solution)/shard_map/reduce_scatter | solution.py:134
  348.0 18.7 %copy-start.10 = (f32[640,2048]{1,0:T(8,128)S(1)}, f32[640,2048]{1,0:T(8,128)}, u32[]{:S(2)}) copy-start(f32[640,2048]{1,0:T(8,128)} %fusion.68) | copy-start | bytes 15728644
  348.0 18.7 %copy-start.33 = (f32[2048]{0:T(1024)S(1)}, f32[2048]{0:T(1024)}, u32[]{:S(2)}) copy-start(f32[2048]{0:T(1024)} %dynamic_slice.37) | copy-start | bytes 24580
  373.6 19.6 %reduce-scatter.15.cloned.1.call-start = ((), (), s32[]{:S(2)}) async-start(), calls=%async_computation.16 | async-start | bytes 1966080 | tf_op jit(solution)/shard_map/reduce_scatter | solution.py:162
  380.7 32.7 %all-gather.22.cloned.1.call-start = ((), (), s32[]{:S(2)}) async-start(), calls=%async_computation.17 | async-start | bytes 1966080 | tf_op jit(solution)/shard_map/all_gather | solution.py:175
  399.8 16.1 %copy-start.34 = (f32[320]{0:T(512)}, f32[320]{0:T(512)S(1)}, u32[]{:S(2)}) copy-start(f32[320]{0:T(512)S(1)} %negate_multiply_fusion.2) | copy-start | bytes 3844
  402.6 184.5 %reduce-scatter.25.cloned.1.call-start = ((), (), s32[]{:S(2)}) async-start(), calls=%async_computation.23 | async-start | bytes 540672
  420.1 6.4 copy-start.7
  420.1 6.4 copy-start.12
  420.1 6.4 copy-start.19
  420.1 6.4 copy-start.29
  420.2 12.7 %slice-start = ((s8[7864320]{0:T(1024)(128)(4,1)}), s8[4194304]{0:T(1024)(128)(4,1)S(1)}, s32[]{:S(2)}) async-start(s8[7864320]{0:T(1024)(128)(4,1)} %bitcast.72), calls=%async_computation.25 | async-start | bytes 8388608
  426.6 6.3 slice-start.1
  451.8 211.1 %reduce-scatter.19.cloned.1.call-start = ((), (), s32[]{:S(2)}) async-start(), calls=%async_computation.19 | async-start | bytes 1114112 | tf_op jit(solution)/shard_map/reduce_scatter | solution.py:223
  455.6 215.6 %reduce-scatter.17.cloned.1.call-start = ((), (), s32[]{:S(2)}) async-start(), calls=%async_computation.18 | async-start | bytes 1966080 | tf_op jit(solution)/shard_map/reduce_scatter | solution.py:199
  460.8 386.3 %all-reduce.11.cloned.1.call-start = ((), (), s32[]{:S(2)}) async-start(), calls=%async_computation.24 | async-start | bytes 8388608
  473.9 469.6 %reduce-scatter.23.cloned.1.call-start = ((), (), s32[]{:S(2)}) async-start(), calls=%async_computation.21 | async-start | bytes 4456448 | tf_op jit(solution)/shard_map/reduce_scatter | solution.py:229
  482.0 558.5 %reduce-scatter.21.cloned.1.call-start = ((), (), s32[]{:S(2)}) async-start(), calls=%async_computation.20 | async-start | bytes 4456448 | tf_op jit(solution)/shard_map/reduce_scatter | solution.py:226
  490.0 181.1 %copy-start.24 = (f32[320]{0:T(512)S(1)}, f32[320]{0:T(512)}, u32[]{:S(2)}) copy-start(f32[320]{0:T(512)} %copy-done.23) | copy-start | bytes 3844
  490.0 181.1 %copy-start.25 = (f32[1024]{0:T(1024)S(1)}, f32[1024]{0:T(1024)}, u32[]{:S(2)}) copy-start(f32[1024]{0:T(1024)} %param.26) | copy-start | bytes 12292
  490.1 182.7 %copy-start.37 = (f32[320]{0:T(512)S(1)}, f32[320]{0:T(512)}, u32[]{:S(2)}) copy-start(f32[320]{0:T(512)} %copy-done.36) | copy-start | bytes 3844
  490.1 182.7 %copy-start.31 = (f32[320]{0:T(512)S(1)}, f32[320]{0:T(512)}, u32[]{:S(2)}) copy-start(f32[320]{0:T(512)} %copy-done.30) | copy-start | bytes 3844
  490.1 184.6 %copy-start.39 = (f32[1024]{0:T(1024)S(1)}, f32[1024]{0:T(1024)}, u32[]{:S(2)}) copy-start(f32[1024]{0:T(1024)} %get-tuple-element.151) | copy-start | bytes 12292
  490.1 184.6 %copy-start.40 = (f32[1024]{0:T(1024)S(1)}, f32[1024]{0:T(1024)}, u32[]{:S(2)}) copy-start(f32[1024]{0:T(1024)} %get-tuple-element.131) | copy-start | bytes 12292
  490.1 184.6 %copy-start.41 = (f32[1024]{0:T(1024)S(1)}, f32[1024]{0:T(1024)}, u32[]{:S(2)}) copy-start(f32[1024]{0:T(1024)} %get-tuple-element.137) | copy-start | bytes 12292
  490.1 184.6 %copy-start.42 = (f32[1024]{0:T(1024)S(1)}, f32[1024]{0:T(1024)}, u32[]{:S(2)}) copy-start(f32[1024]{0:T(1024)} %get-tuple-element.156) | copy-start | bytes 12292
  490.1 234.2 %copy-start.4 = (f32[320,1024]{1,0:T(8,128)S(1)}, f32[320,1024]{1,0:T(8,128)}, u32[]{:S(2)}) copy-start(f32[320,1024]{1,0:T(8,128)} %copy-done.3) | copy-start | bytes 3932164
  490.1 234.2 %copy-start.35 = (f32[320]{0:T(512)S(1)}, f32[320]{0:T(512)}, u32[]{:S(2)}) copy-start(f32[320]{0:T(512)} %copy-done.34) | copy-start | bytes 3844
  671.1 53.2 %copy-start.9 = (bf16[320,1024]{1,0:T(8,128)(2,1)S(1)}, bf16[320,1024]{1,0:T(8,128)(2,1)}, u32[]{:S(2)}) copy-start(bf16[320,1024]{1,0:T(8,128)(2,1)} %reduce-scatter.17.cloned.1.call-done) | copy-start | bytes 1966084
  (21 other events, 54.2 us)
Sparse Core Ops, SparseCore 0:
  12.4 12.1 all-gather.9
  27.3 68.7 all-gather.11
  98.8 54.3 all-gather.13
  156.8 7.5 reduce-scatter.10
  167.4 77.2 all-gather.23
  246.7 8.0 all-gather.15
  257.0 10.5 all-gather.19
  270.8 77.2 all-gather.17
  373.8 7.3 reduce-scatter.12
  383.3 9.9 reduce-scatter.14
  402.7 10.6 all-gather.21
  451.9 135.1 reduce-scatter.24
  589.4 73.4 reduce-scatter.18
  665.7 5.4 reduce-scatter.16
  676.6 170.4 all-reduce.10
  849.4 94.0 reduce-scatter.22
  945.8 94.7 reduce-scatter.20
where the time goes:
time: 1050 us
  waiting for transfers between devices  782 us (74%)
  matrix products  101 us (10%)
  local copies, waits for them, and re-layouts  61.5 us (6%)
  blocking collectives  44.3 us (4%)
  other arithmetic  42.9 us (4%)
  between operations  16.1 us (2%)
    unnamed x19, waiting for transfers between devices  215 us
    reduce_scatter x1, waiting for transfers between devices, local(): lax.psum_scatter(grad_up.astype(jnp.bfloat16), 'dp', scatter_dimension=1,...  95.2 us
    reduce_scatter x1, waiting for transfers between devices, local(): lax.psum_scatter(grad_down.astype(jnp.bfloat16), 'dp', scatter_dimension=...  94.5 us
    all_gather x1, waiting for transfers between devices, local(): lax.all_gather(w_fc2, 'dp', axis=1, tiled=True)  80.4 us
    reduce_scatter x1, waiting for transfers between devices, local(): lax.psum_scatter(grad_out.astype(jnp.bfloat16), 'dp', scatter_dimension=1...  74.4 us
    all_gather x1, waiting for transfers between devices, local(): lax.all_gather(w_qkv, 'dp', axis=1, tiled=True)  71.6 us
    all_gather x1, waiting for transfers between devices, local(): lax.all_gather(w_fc1[None], 'dp', axis=1, tiled=True)  68.7 us
    unnamed x1, blocking collectives  44.3 us
  transfers between devices with their start and end apart: 17, of which 17 were waited for; matrix products, arithmetic and copies ran while one was open for 11% of the time, Pallas kernels for 0%

commit v1 on v0

--- a/solution.py
+++ b/solution.py
@@ -1,7 +1,408 @@
 import jax
 import jax.numpy as jnp
 from jax import lax
+from jax.experimental import pallas as pl
+from jax.experimental.pallas import tpu as pltpu
 from jax.sharding import PartitionSpec as P
+
+MESH = pl.DeviceIdType.MESH
+
+
+class Place:
+    def __init__(self):
+        dp = lax.axis_index("dp")
+        self.t = lax.axis_index("tensor")
+        self.z, self.y, self.x = dp // 4, (dp // 2) % 2, dp % 2
+        self.side = self.z // 2
+        self.w = self.z + self.side * (3 - 2 * self.z)
+        self.step = 1 - 2 * self.side
+        self.dp = dp
+
+    def order(self, k):
+        o = (self.w, 1 - self.w, 2, 3)[k]
+        return 3 * self.side + self.step * o
+
+    def chip(self, z, y, x):
+        return z * 4 + y * 2 + x
+
+    def inward(self):
+        return (self.chip(self.z + self.step, self.y, self.x), self.t)
+
+    def outward(self):
+        return (self.chip(self.z - self.step, self.y, self.x), self.t)
+
+    def across_x(self):
+        return (self.chip(self.z, self.y, 1 - self.x), self.t)
+
+    def across_y(self):
+        return (self.chip(self.z, 1 - self.y, self.x), self.t)
+
+    def twin(self):
+        return (self.dp, 1 - self.t)
+
+
+def enter(at):
+    barrier = pltpu.get_barrier_semaphore()
+    for other in (at.across_x(), at.across_y(), at.inward(), at.twin()):
+        pl.semaphore_signal(barrier, inc=1, device_id=other, device_id_type=MESH)
+
+    @pl.when(at.w == 1)
+    def _():
+        pl.semaphore_signal(barrier, inc=1, device_id=at.outward(), device_id_type=MESH)
+
+    pl.semaphore_wait(barrier, 4 + at.w)
+
+
+class Gather:
+    def __init__(self, at, full, shard, pieces, send, recv):
+        self.at, self.full, self.shard, self.pieces, self.send, self.recv = at, full, shard, pieces, send, recv
+
+    def rows(self, p, z, y, x, part=None):
+        c0, c1 = self.pieces[p]
+        start, size = self.at.chip(z, y, x) * self.shard, self.shard
+        if part is not None:
+            size = self.shard // 2
+            start = start + part * size
+        return self.full.at[pl.ds(pl.multiple_of(start, size), size), pl.ds(c0, c1 - c0)]
+
+    def copy(self, p, ref, s, r, other):
+        return pltpu.make_async_remote_copy(
+            src_ref=ref,
+            dst_ref=ref,
+            send_sem=self.send.at[p, s[0], s[1]],
+            recv_sem=self.recv.at[p, r[0], r[1]],
+            device_id=other,
+            device_id_type=MESH,
+        )
+
+    def z_in(self, p, z):
+        return self.copy(p, self.rows(p, z, self.at.y, self.at.x), (0, z), (0, z), self.at.inward())
+
+    def z_out(self, p, z):
+        return self.copy(p, self.rows(p, z, self.at.y, self.at.x), (5, z), (0, z), self.at.outward())
+
+    def x_full(self, p, z):
+        return self.copy(p, self.rows(p, z, self.at.y, self.at.x), (1, z), (1, z), self.at.across_x())
+
+    def y_full(self, p, z):
+        return self.copy(p, self.rows(p, z, self.at.y, self.at.x), (2, z), (2, z), self.at.across_y())
+
+    def x_half(self, p, z):
+        return self.copy(p, self.rows(p, z, 1 - self.at.y, self.at.x, 1), (3, z), (3, z), self.at.across_x())
+
+    def y_half(self, p, z):
+        return self.copy(p, self.rows(p, z, self.at.y, 1 - self.at.x, 0), (4, z), (4, z), self.at.across_y())
+
+    def arrived(self, p, kind, z):
+        at = self.at
+        ref = (
+            lambda: self.rows(p, z, at.y, at.x),
+            lambda: self.rows(p, z, at.y, 1 - at.x),
+            lambda: self.rows(p, z, 1 - at.y, at.x),
+            lambda: self.rows(p, z, 1 - at.y, 1 - at.x, 1),
+            lambda: self.rows(p, z, 1 - at.y, 1 - at.x, 0),
+        )[kind]()
+        self.copy(p, ref, (kind, z), (kind, z), at.across_x()).wait_recv()
+
+    def line(self, p, k):
+        at = self.at
+        z = at.order(k)
+        if k > 0:
+            self.arrived(p, 0, z)
+        if k == 0:
+            self.z_in(p, z).start()
+        if k == 1:
+
+            @pl.when(at.w == 1)
+            def _():
+                self.z_in(p, z).start()
+
+        else:
+
+            @pl.when(at.w == 1)
+            def _():
+                self.z_out(p, z).start()
+
+        self.x_full(p, z).start()
+        self.y_full(p, z).start()
+
+    def plane(self, p, k):
+        z = self.at.order(k)
+        self.arrived(p, 1, z)
+        self.y_half(p, z).start()
+        self.arrived(p, 2, z)
+        self.x_half(p, z).start()
+
+    def finish(self, p):
+        for k in range(4):
+            z = self.at.order(k)
+            self.arrived(p, 3, z)
+            self.arrived(p, 4, z)
+
+    def drain(self, p):
+        at = self.at
+        for k in range(4):
+            z = at.order(k)
+            if k == 0:
+                self.z_in(p, z).wait_send()
+            if k == 1:
+
+                @pl.when(at.w == 1)
+                def _(z=z):
+                    self.z_in(p, z).wait_send()
+
+            else:
+
+                @pl.when(at.w == 1)
+                def _(z=z):
+                    self.z_out(p, z).wait_send()
+
+            self.x_full(p, z).wait_send()
+            self.y_full(p, z).wait_send()
+            self.x_half(p, z).wait_send()
+            self.y_half(p, z).wait_send()
+
+
+class Scatter:
+    def __init__(self, at, full, shard, pieces, xh, yh, xf, yf, zl, send, recv):
+        self.at, self.full, self.shard, self.pieces = at, full, shard, pieces
+        self.xh, self.yh, self.xf, self.yf, self.zl = xh, yh, xf, yf, zl
+        self.send, self.recv = send, recv
+
+    def cols(self, p):
+        c0, c1 = self.pieces[p]
+        return pl.ds(c0, c1 - c0)
+
+    def rows(self, p, z, y, x, part=None):
+        start, size = self.at.chip(z, y, x) * self.shard, self.shard
+        if part is not None:
+            size = self.shard // 2
+            start = start + part * size
+        ref, c0, c1 = self.full(p)
+        return ref.at[pl.ds(pl.multiple_of(start, size), size), pl.ds(c0, c1 - c0)]
+
+    def copy(self, p, src, dst, s, r, other):
+        return pltpu.make_async_remote_copy(
+            src_ref=src,
+            dst_ref=dst,
+            send_sem=self.send.at[p, s[0], s[1]],
+            recv_sem=self.recv.at[p, r[0], r[1]],
+            device_id=other,
+            device_id_type=MESH,
+        )
+
+    def x_half(self, p, z):
+        at = self.at
+        return self.copy(
+            p, self.rows(p, z, 1 - at.y, 1 - at.x, 0), self.xh.at[z, :, self.cols(p)], (1, z), (1, z), at.across_x()
+        )
+
+    def y_half(self, p, z):
+        at = self.at
+        return self.copy(
+            p, self.rows(p, z, 1 - at.y, 1 - at.x, 1), self.yh.at[z, :, self.cols(p)], (2, z), (2, z), at.across_y()
+        )
+
+    def x_full(self, p, z):
+        at = self.at
+        return self.copy(
+            p, self.rows(p, z, at.y, 1 - at.x), self.xf.at[z, :, self.cols(p)], (3, z), (3, z), at.across_x()
+        )
+
+    def y_full(self, p, z):
+        at = self.at
+        return self.copy(
+            p, self.rows(p, z, 1 - at.y, at.x), self.yf.at[z, :, self.cols(p)], (4, z), (4, z), at.across_y()
+        )
+
+    def z_in(self, p, z, slot):
+        at = self.at
+        return self.copy(
+            p, self.rows(p, z, at.y, at.x), self.zl.at[slot, :, self.cols(p)], (0, z), (0, slot), at.inward()
+        )
+
+    def z_out(self, p, z, slot):
+        at = self.at
+        return self.copy(
+            p, self.rows(p, z, at.y, at.x), self.zl.at[slot, :, self.cols(p)], (0, z), (0, slot), at.outward()
+        )
+
+    def begin(self, p):
+        for k in (3, 2, 1, 0):
+            z = self.at.order(k)
+            self.x_half(p, z).start()
+            self.y_half(p, z).start()
+
+    def plane(self, p, k):
+        at = self.at
+        z = at.order(k)
+        self.x_half(p, z).wait_recv()
+        ref = self.rows(p, z, 1 - at.y, at.x, 0)
+        ref[...] = ref[...] + self.xh[z, :, self.cols(p)]
+        self.y_full(p, z).start()
+        self.y_half(p, z).wait_recv()
+        ref = self.rows(p, z, at.y, 1 - at.x, 1)
+        ref[...] = ref[...] + self.yh[z, :, self.cols(p)]
+        self.x_full(p, z).start()
+
+    def wait_line(self, p, z, slot):
+        self.z_in(p, z, slot).wait_recv()
+
+    def line(self, p, k, out=None):
+        at = self.at
+        z = at.order(k)
+        self.x_full(p, z).wait_recv()
+        self.y_full(p, z).wait_recv()
+        ref = self.rows(p, z, at.y, at.x)
+        total = (
+            ref[...].astype(jnp.float32)
+            + self.xf[z, :, self.cols(p)].astype(jnp.float32)
+            + self.yf[z, :, self.cols(p)].astype(jnp.float32)
+        )
+        if k > 0:
+
+            @pl.when(at.w == 0)
+            def _():
+                ref[...] = total.astype(jnp.bfloat16)
+                self.z_in(p, z, z).start()
+
+            @pl.when(at.w == 1)
+            def _():
+                self.wait_line(p, z, z)
+                ref[...] = (total + self.zl[z, :, self.cols(p)].astype(jnp.float32)).astype(jnp.bfloat16)
+                if k == 3:
+                    self.z_in(p, z, z).start()
+                elif k == 2:
+                    self.z_in(p, z, 4).start()
+                else:
+                    self.z_out(p, z, 4).start()
+
+        else:
+            self.wait_line(p, z, 4)
+            total = total + self.zl[4, :, self.cols(p)].astype(jnp.float32)
+
+            @pl.when(at.w == 0)
+            def _():
+                out[...] = total
+
+            @pl.when(at.w == 1)
+            def _():
+                self.wait_line(p, z, z)
+                out[...] = total + self.zl[z, :, self.cols(p)].astype(jnp.float32)
+
+    def drain(self, p):
+        at = self.at
+        for k in range(4):
+            z = at.order(k)
+            for c in (self.x_half(p, z), self.y_half(p, z), self.x_full(p, z), self.y_full(p, z)):
+                c.wait_send()
+            if k > 0:
+                self.z_in(p, z, z).wait_send()
+
+WIDTHS = (1536, 512, 1024, 1024, 1024, 1024)
+
+
+def pieces_of():
+    out, c = [], 0
+    for n in WIDTHS:
+        out.append((c, c + n))
+        c += n
+    return out
+
+
+def gather_kernel(own_ref, full_ref, held, sem, send, recv):
+    at = Place()
+    shard = own_ref.shape[0]
+    enter(at)
+    pieces = pieces_of()
+    g = Gather(at, held, shard, pieces, send, recv)
+    cp = pltpu.make_async_copy(own_ref, held.at[pl.ds(pl.multiple_of(at.dp * shard, shard), shard), :], sem)
+    cp.start()
+    cp.wait()
+    n = len(pieces)
+    g.line(0, 0)
+    for p in range(n):
+        for k in range(1, 4):
+            g.line(p, k)
+            g.plane(p, k - 1)
+            if k == 2 and p + 1 < n:
+                g.line(p + 1, 0)
+        g.plane(p, 3)
+    for p in range(n):
+        g.finish(p)
+        g.drain(p)
+    cp = pltpu.make_async_copy(held, full_ref, sem)
+    cp.start()
+    cp.wait()
+
+
+def scatter_kernel(g_ref, out_ref, held, xh, yh, xf, yf, zl, sem, send, recv):
+    at = Place()
+    shard = out_ref.shape[0]
+    enter(at)
+    pieces = pieces_of()
+    cp = pltpu.make_async_copy(g_ref, held, sem)
+    cp.start()
+    cp.wait()
+    s = Scatter(at, lambda p: (held,) + pieces[p], shard, pieces, xh, yh, xf, yf, zl, send, recv)
+    n = len(pieces)
+    s.begin(0)
+    for p in range(n):
+        if p + 1 < n:
+            s.begin(p + 1)
+        for k in (3, 2, 1, 0):
+            s.plane(p, k)
+        if p > 0:
+            for k in (3, 2, 1, 0):
+                s.line(p - 1, k, out_ref.at[:, s.cols(p - 1)])
+    for k in (3, 2, 1, 0):
+        s.line(n - 1, k, out_ref.at[:, s.cols(n - 1)])
+    for p in range(n):
+        s.drain(p)
+
+
+def gather_all(own):
+    shard, cols = own.shape
+    n = len(WIDTHS)
+    return pl.pallas_call(
+        gather_kernel,
+        out_shape=jax.ShapeDtypeStruct((16 * shard, cols), jnp.bfloat16),
+        in_specs=[pl.BlockSpec(memory_space=pl.ANY)],
+        out_specs=pl.BlockSpec(memory_space=pl.ANY),
+        scratch_shapes=[
+            pltpu.VMEM((16 * shard, cols), jnp.bfloat16),
+            pltpu.SemaphoreType.DMA,
+            pltpu.SemaphoreType.DMA((n, 6, 4)),
+            pltpu.SemaphoreType.DMA((n, 5, 4)),
+        ],
+        compiler_params=pltpu.CompilerParams(collective_id=1, has_side_effects=True, vmem_limit_bytes=48 << 20),
+    )(own)
+
+
+def scatter_all(grads):
+    rows, cols = grads.shape
+    shard = rows // 16
+    n = len(WIDTHS)
+    bf = jnp.bfloat16
+    return pl.pallas_call(
+        scatter_kernel,
+        out_shape=jax.ShapeDtypeStruct((shard, cols), jnp.float32),
+        in_specs=[pl.BlockSpec(memory_space=pl.ANY)],
+        out_specs=pl.BlockSpec(memory_space=pltpu.VMEM),
+        scratch_shapes=[
+            pltpu.VMEM((rows, cols), bf),
+            pltpu.VMEM((4, shard // 2, cols), bf),
+            pltpu.VMEM((4, shard // 2, cols), bf),
+            pltpu.VMEM((4, shard, cols), bf),
+            pltpu.VMEM((4, shard, cols), bf),
+            pltpu.VMEM((5, shard, cols), bf),
+            pltpu.SemaphoreType.DMA,
+            pltpu.SemaphoreType.DMA((n, 5, 4)),
+            pltpu.SemaphoreType.DMA((n, 5, 5)),
+        ],
+        compiler_params=pltpu.CompilerParams(collective_id=2, has_side_effects=True, vmem_limit_bytes=48 << 20),
+    )(grads)
+
 
 HD = 64
 BUFFER = 64
@@ -89,12 +490,21 @@
     validity_all = (slot_index[None, :] < (BUFFER + counts)[:, None]).astype(jnp.float32)
     own_validity = lax.dynamic_slice_in_dim(validity_all, tensor_pos * own_images, own_images, 0)
     own_valid = own_validity.reshape(own_rows, 1)
-    qkv_full, out_full, up_full, down_full = (
-        lax.all_gather(w_qkv, "dp", axis=1, tiled=True),
-        lax.all_gather(w_out, "dp", axis=1, tiled=True),
-        lax.all_gather(w_fc1[None], "dp", axis=1, tiled=True),
-        lax.all_gather(w_fc2, "dp", axis=1, tiled=True),
-    )
+    fast = lax.axis_size("dp") == 16 and lax.axis_size("tensor") == 2
+    if fast:
+        own = jnp.concatenate([w_qkv[0], w_qkv[1], w_qkv[2], w_out.T, w_fc1, w_fc2.T], axis=1)
+        full = gather_all(own)
+        qkv_full = jnp.stack([full[:, 0:512], full[:, 512:1024], full[:, 1024:1536]])
+        out_full = full[:, 1536:2048].T
+        up_full = full[None, :, 2048:4096]
+        down_full = full[:, 4096:6144].T
+    else:
+        qkv_full, out_full, up_full, down_full = (
+            lax.all_gather(w_qkv, "dp", axis=1, tiled=True),
+            lax.all_gather(w_out, "dp", axis=1, tiled=True),
+            lax.all_gather(w_fc1[None], "dp", axis=1, tiled=True),
+            lax.all_gather(w_fc2, "dp", axis=1, tiled=True),
+        )
     head_width = w_qkv.shape[2]
     unit_width = w_fc1.shape[1]
     bias_query = lax.dynamic_slice_in_dim(b_qv[0], tensor_pos * head_width, head_width, 0)
@@ -216,20 +626,32 @@
     bias_up_full = lax.dynamic_update_slice(
         jnp.zeros((b_fc1.shape[0],), jnp.float32), grad_bias_up, (tensor_pos * unit_width,)
     )
-    qkv_part, out_part, up_part, down_part = (
-        lax.psum_scatter(
-            grad_qkv.astype(jnp.bfloat16), "dp", scatter_dimension=1, tiled=True
-        ).astype(jnp.float32),
-        lax.psum_scatter(
-            grad_out.astype(jnp.bfloat16), "dp", scatter_dimension=1, tiled=True
-        ).astype(jnp.float32),
-        lax.psum_scatter(
-            grad_up.astype(jnp.bfloat16), "dp", scatter_dimension=1, tiled=True
-        ).astype(jnp.float32),
-        lax.psum_scatter(
-            grad_down.astype(jnp.bfloat16), "dp", scatter_dimension=1, tiled=True
-        ).astype(jnp.float32),
-    )
+    if fast:
+        low = lambda v: v.astype(jnp.bfloat16)
+        grads = jnp.concatenate(
+            [low(grad_qkv[0]), low(grad_qkv[1]), low(grad_qkv[2]), low(grad_out).T, low(grad_up[0]), low(grad_down).T],
+            axis=1,
+        )
+        part = scatter_all(grads)
+        qkv_part = jnp.stack([part[:, 0:512], part[:, 512:1024], part[:, 1024:1536]])
+        out_part = part[:, 1536:2048].T
+        up_part = part[None, :, 2048:4096]
+        down_part = part[:, 4096:6144].T
+    else:
+        qkv_part, out_part, up_part, down_part = (
+            lax.psum_scatter(
+                grad_qkv.astype(jnp.bfloat16), "dp", scatter_dimension=1, tiled=True
+            ).astype(jnp.float32),
+            lax.psum_scatter(
+                grad_out.astype(jnp.bfloat16), "dp", scatter_dimension=1, tiled=True
+            ).astype(jnp.float32),
+            lax.psum_scatter(
+                grad_up.astype(jnp.bfloat16), "dp", scatter_dimension=1, tiled=True
+            ).astype(jnp.float32),
+            lax.psum_scatter(
+                grad_down.astype(jnp.bfloat16), "dp", scatter_dimension=1, tiled=True
+            ).astype(jnp.float32),
+        )
     small_parts = (
         lax.psum_scatter(bias_qv_full, ("dp", "tensor"), scatter_dimension=1, tiled=True),
         lax.psum_scatter(grad_bias_out, ("dp", "tensor"), scatter_dimension=0, tiled=True),

time: 1050 us -> 538 us (0.51)
  waiting for transfers between devices: 782 us -> 31.4 us
  Pallas kernels: 0 us -> 242 us
    reduce_scatter x3 -> x0, waiting for transfers between devices: 264 us -> none  [the longest x1 95.2 us: local(): lax.psum_scatter(grad_up.astype(jnp.bfloat16), 'dp', scatter_dimension=1,...]
    pallas_call x0 -> x2, Pallas kernels: none -> 242 us  [the longest x1 123 us: scatter_all(): pl.pallas_call(scatter_kernel, out_shape=jax.ShapeDtypeStruct((shard, col...]
    all_gather x4 -> x0, waiting for transfers between devices: 241 us -> none  [the longest x1 80.4 us: local(): lax.all_gather(w_fc2, 'dp', axis=1, tiled=True)]
    unnamed x19 -> x10, waiting for transfers between devices: 215 us -> 0.15 us
    reduce_scatter x1, waiting for transfers between devices: 12.1 us -> 0.02 us  [local(): lax.psum_scatter(jnp.einsum('ru,du->rd', taken, up_full, preferred_elemen...]
    reduce_scatter x1, starting transfers between devices: 0.44 us -> 11.6 us  [local(): lax.psum_scatter(jnp.dot(taken, down_full, preferred_element_type=jnp.flo...]
    unnamed x117 -> x147, local copies, waits for them, and re-layouts: 18 us -> 21.9 us
  transfers between devices with their start and end apart: 17 -> 9, of which waited for: 17 -> 4; matrix products, arithmetic and copies ran while one was open for 11% -> 12% of each run, Pallas kernels for 0% -> 46%
where the time goes in v1:
time: 538 us; the launch traced here: 529 us
  Pallas kernels  242 us (45%)
  matrix products  92.4 us (17%)
  local copies, waits for them, and re-layouts  63.2 us (12%)
  blocking collectives  39.2 us (7%)
  other arithmetic  33.8 us (6%)
  waiting for transfers between devices  31.4 us (6%)
  between operations  15.8 us (3%)
  starting transfers between devices  11.9 us (2%)
    pallas_call x1, Pallas kernels, scatter_all(): pl.pallas_call(scatter_kernel, out_shape=jax.ShapeDtypeStruct((shard, col...  123 us
    pallas_call x1, Pallas kernels, gather_all(): pl.pallas_call(gather_kernel, out_shape=jax.ShapeDtypeStruct((16 * shard,...  118 us
    unnamed x1, blocking collectives  39.2 us
    unnamed x147, local copies, waits for them, and re-layouts  21.9 us
    dot_general x1, matrix products, local(): jnp.dot(second_rows, up_full, preferred_element_type=jnp.float32) + bias_up  17.4 us
    reduce_scatter x1, starting transfers between devices, local(): lax.psum_scatter(jnp.dot(taken, down_full, preferred_element_type=jnp.flo...  11.6 us
    dot_general x1, matrix products, local(): jnp.einsum('rd,ud->ru', d_feed_rows, down_full, preferred_element_type=jn...  10.8 us
  transfers between devices with their start and end apart: 9, of which 4 were waited for; matrix products, arithmetic and copies ran while one was open for 12% of the time, Pallas kernels for 46%

profile of v1, /device:TPU:0, one launch (start us, length us, event | category | flops | bytes accessed | tf_op | source)
XLA Modules:
  0.0 529.3 jit_solution(16774599719238342045)
XLA Ops:
  11.2 2.2 fusion.43
  13.7 118.3 %shard_map.262 = bf16[1024,6144]{1,0:T(8,128)(2,1)} custom-call(bf16[64,6144]{1,0:T(8,128)(2,1)S(1)} %bitcast_dynamic-update-slice_fusion.own_ref), custom_call_target="tpu_custom_call" | custom-call | tf_op jit(solution)/shard_map/pallas_call | solution.py:367
  132.9 2.1 slice_bitcast_fusion.5
  136.4 3.5 fusion.55
  141.3 2.0 reshape.162
  143.3 2.3 copy.98
  145.6 1.7 reshape.168
  147.3 1.9 copy.100
  149.2 3.2 reshape.161
  152.4 3.2 copy.96
  155.5 2.3 fusion.20
  157.9 2.1 fusion
  161.0 2.3 fusion.59
  165.6 3.4 convolution_convert_fusion
  169.1 8.8 %reduce-scatter.8.cloned.1.call-done = bf16[320,1024]{1,0:T(8,128)(2,1)} async-done(((bf16[640,1024]{1,0:T(8,128)(2,1)}), bf16[320,1024]{1,0:T(8,128)(2,1)}) %reduce-scatter.8.cloned.1.call-update) | async-done | bytes 655376 | tf_op jit(solution)/shard_map/reduce_scatter | solution.py:531
  182.1 1.9 add_convert_fusion.3
  185.3 1.6 convert_reduce_fusion.5
  188.4 6.4 %all-gather.7.cloned.1.call-done = bf16[640,1024]{1,0:T(8,128)(2,1)} async-done(((bf16[320,1024]{1,0:T(8,128)(2,1)}), bf16[640,1024]{1,0:T(8,128)(2,1)}) %all-gather.7.cloned.1.call-update) | async-done | bytes 1310736 | tf_op jit(solution)/shard_map/all_gather | solution.py:540
  194.8 17.4 %multiply_convert_fusion.1 = (bf16[640,2048]{1,0:T(8,128)(2,1)}, f32[640,2048]{1,0:T(8,128)}, f32[640,2048]{1,0:T(8,128)}) fusion(f32[2048]{0:T(1024)} %dynamic_slice.37, bf16[640,1024]{1,0:T(8,128)(2,1)} %all-gather.7.cloned.1.call-done, bf16[1024,6144]{1,0:T(8,128)(2,1)} %shard_map.262), kind=kOutput, calls=%fused_computation.12 | convolution fusion | flops 2770862080 | bytes 18620416 | tf_op jit(solution)/shard_map/dot_general | solution.py:541
  212.2 10.8 %convert_reduce_fusion = (f32[2048]{0:T(1024)}, bf16[640,2048]{1,0:T(8,128)(2,1)S(1)}) fusion(f32[640,2048]{1,0:T(8,128)} %get-tuple-element.98, bf16[640,1024]{1,0:T(8,128)(2,1)} %all-gather.9.cloned.1.call-done, bf16[1024,6144]{1,0:T(8,128)(2,1)} %shard_map.262, f32[640,2048]{1,0:T(8,128)} %get-tuple-element.119, f32[2048]{0:T(1024)} %dynamic_slice.37), kind=kOutput, calls=%fused_computation.10 | convolution fusion | flops 2706634752 | bytes 18628608 | tf_op jit(solution)/shard_map/rd,ud->ru/dot_general | solution.py:564
  224.5 6.3 %fusion.27 = bf16[640,1024]{1,0:T(8,128)(2,1)} fusion(bf16[640,2048]{1,0:T(8,128)(2,1)S(1)} %get-tuple-element.123, bf16[1024,6144]{1,0:T(8,128)(2,1)} %shard_map.262), kind=kOutput, calls=%fused_computation.66 | convolution fusion | flops 2685009920 | bytes 8126464 | tf_op jit(solution)/shard_map/ru,du->rd/dot_general | solution.py:573
  230.8 11.6 %reduce-scatter.10.cloned.1.call-start = ((), (), s32[]{:S(2)}) async-start(), calls=%async_computation.8 | async-start | bytes 1966080 | tf_op jit(solution)/shard_map/reduce_scatter | solution.py:544
  242.3 6.9 %fusion.30 = bf16[640,1024]{1,0:T(8,128)(2,1)} fusion(bf16[640,2048]{1,0:T(8,128)(2,1)} %get-tuple-element.97, bf16[1024,6144]{1,0:T(8,128)(2,1)} %shard_map.262), kind=kOutput, calls=%fused_computation.67 | convolution fusion | flops 2685009920 | bytes 8126464 | tf_op jit(solution)/shard_map/dot_general | solution.py:545
  249.4 10.0 %reduce-scatter.10.cloned.1.call-done = bf16[320,1024]{1,0:T(8,128)(2,1)} async-done(((bf16[640,1024]{1,0:T(8,128)(2,1)}), bf16[320,1024]{1,0:T(8,128)(2,1)}) %reduce-scatter.10.cloned.1.call-update) | async-done | bytes 655376 | tf_op jit(solution)/shard_map/reduce_scatter | solution.py:544
  259.4 4.5 fusion.45
  267.0 1.7 convert_reduce_fusion.6
  269.7 3.8 stack.63
  273.5 6.0 %all-gather.11.cloned.1.call-done = bf16[640,1024]{1,0:T(8,128)(2,1)} async-done(((bf16[320,1024]{1,0:T(8,128)(2,1)}), bf16[640,1024]{1,0:T(8,128)(2,1)}) %all-gather.11.cloned.1.call-update) | async-done | bytes 1310736 | tf_op jit(solution)/shard_map/all_gather | solution.py:585
  279.5 2.5 convolution_convert_fusion.2
  282.0 1.7 reshape.169
  283.7 2.5 copy.104
  286.3 6.4 %fusion.60 = bf16[2,320,8,64]{1,3,2,0:T(8,128)(2,1)} fusion(bf16[2,320,8,64]{1,3,2,0:T(8,128)(2,1)} %copy.104, f32[2,8,320]{2,1,0:T(8,128)} %log_add_fusion, f32[2,8,320,320]{2,3,1,0:T(8,128)} %copy-done, pred[2,320]{1,0:T(4,128)(4,1)S(1)} %get-tuple-element.116), kind=kOutput, calls=%fused_computation.110 | convolution fusion | flops 216596480 | bytes 7885440 | tf_op jit(solution)/shard_map/while/body/eval_jaxpr/bhqk,bqhd->bkhd/dot_general | solution.py:448
  292.8 6.2 %multiply_reduce_fusion = (f32[2,8,320]{2,1,0:T(8,128)S(1)}, f32[2,8,320,320]{2,3,1,0:T(8,128)S(1)}) fusion(f32[2,8,320]{2,1,0:T(8,128)S(1)} %copy-done.26, f32[2,8,320,320]{2,3,1,0:T(8,128)} %copy-done, pred[2,320]{1,0:T(4,128)(4,1)S(1)} %get-tuple-element.116, bf16[2,320,8,64]{1,3,2,0:T(8,128)(2,1)S(1)} %copy-done.12, f32[2,320,8,64]{1,3,2,0:T(8,128)S(1)} %copy-done.8, ...), kind=kOutput, calls=%fused_computation.1 | convolution fusion | flops 218557440 | bytes 15116928 | tf_op jit(solution)/shard_map/while/body/eval_jaxpr/bqhd,bkhd->bhqk/dot_general | solution.py:451
  299.0 2.4 multiply_convert_fusion
  301.5 2.2 fusion.64
  304.5 1.9 copy.132
  308.0 1.9 copy.131
  316.9 3.3 bitcast_convert_fusion
  321.6 4.4 convert_bitcast_fusion
  329.2 2.5 fusion.65
  331.7 3.4 fusion.36
  335.0 5.1 convert_dynamic-update-slice_fusion.1
  340.1 5.1 convert_dynamic-update-slice_fusion.g_ref
  345.2 123.3 %shard_map.263 = f32[64,6144]{1,0:T(8,128)S(1)} custom-call(bf16[1024,6144]{1,0:T(8,128)(2,1)} %convert_dynamic-update-slice_fusion.g_ref), custom_call_target="tpu_custom_call" | custom-call | tf_op jit(solution)/shard_map/pallas_call | solution.py:387
  472.5 1.6 convert_reduce_fusion.3
  474.2 1.9 fusion.47
  476.1 39.2 %all-reduce.7 = (f32[1024]{0:T(1024)S(1)}, f32[4096]{0:T(1024)S(1)}, f32[1024]{0:T(1024)S(1)}, f32[1024]{0:T(1024)S(1)}, f32[1024]{0:T(1024)S(1)}, /*index=5*/f3...) all-reduce(f32[1024]{0:T(1024)S(1)} %copy-done.52, ...), channel_id=7, replica_groups=mesh['dp'=16,'tensor'=2] {'dp','tensor'}, use_global_device_ids=true, to_apply=%region_18.19.clone | all-reduce | flops 10246 | bytes 81968
  520.6 1.7 add_add_fusion.2
  (212 shorter events, 46.0 us)
Async XLA Ops:
  7.2 6.4 %copy-start.27 = (bf16[3,64,512]{2,1,0:T(8,128)(2,1)S(1)}, bf16[3,64,512]{2,1,0:T(8,128)(2,1)}, u32[]{:S(2)}) copy-start(bf16[3,64,512]{2,1,0:T(8,128)(2,1)} %param.18) | copy-start | bytes 589828
  7.2 6.4 %copy-start.33 = (bf16[512,64]{0,1:T(8,128)(2,1)S(1)}, bf16[512,64]{0,1:T(8,128)(2,1)}, u32[]{:S(2)}) copy-start(bf16[512,64]{0,1:T(8,128)(2,1)} %param.20) | copy-start | bytes 196612
  7.2 6.4 %copy-start.22 = (bf16[64,2048]{1,0:T(8,128)(2,1)S(1)}, bf16[64,2048]{1,0:T(8,128)(2,1)}, u32[]{:S(2)}) copy-start(bf16[64,2048]{1,0:T(8,128)(2,1)} %param.22) | copy-start | bytes 786436
  7.2 6.5 %copy-start.23 = (bf16[2048,64]{0,1:T(8,128)(2,1)S(1)}, bf16[2048,64]{0,1:T(8,128)(2,1)}, u32[]{:S(2)}) copy-start(bf16[2048,64]{0,1:T(8,128)(2,1)} %param.24) | copy-start | bytes 786436
  7.2 127.8 %all-gather.5.cloned.1.call-start = ((), (), s32[]{:S(2)}) async-start(), calls=%async_computation.5 | async-start | bytes 1966080 | tf_op jit(solution)/shard_map/all_gather | solution.py:522
  13.5 164.4 %reduce-scatter.8.cloned.1.call-start = ((), (), s32[]{:S(2)}) async-start(), calls=%async_computation.6 | async-start | bytes 1966080 | tf_op jit(solution)/shard_map/reduce_scatter | solution.py:531
  13.7 118.3 %copy-start.53 = (f32[2,1024]{1,0:T(2,128)S(1)}, f32[2,1024]{1,0:T(2,128)}, u32[]{:S(2)}) copy-start(f32[2,1024]{1,0:T(2,128)} %param.19) | copy-start | bytes 24580
  13.7 118.5 %copy-start.58 = (s32[2]{0:T(128)S(1)}, s32[2]{0:T(128)}, u32[]{:S(2)}) copy-start(s32[2]{0:T(128)} %param.16) | copy-start | bytes 28
  132.2 27.8 %copy-start.39 = (f32[8,64]{1,0:T(8,128)}, f32[8,64]{1,0:T(8,128)S(1)}, u32[]{:S(2)}) copy-start(f32[8,64]{1,0:T(8,128)S(1)} %add.157) | copy-start | bytes 6148
  135.0 4.9 copy-start.19
  149.2 6.3 %copy-start.5 = (bf16[2,320,8,64]{1,3,2,0:T(8,128)(2,1)}, bf16[2,320,8,64]{1,3,2,0:T(8,128)(2,1)S(1)}, u32[]{:S(2)}) copy-start(bf16[2,320,8,64]{1,3,2,0:T(8,128)(2,1)S(1)} %copy.100) | copy-start | bytes 1966084
  165.6 12.3 %copy-start.1 = (bf16[320,1024]{1,0:T(8,128)(2,1)S(1)}, bf16[320,1024]{1,0:T(8,128)(2,1)}, u32[]{:S(2)}) copy-start(bf16[320,1024]{1,0:T(8,128)(2,1)} %param.15) | copy-start | bytes 1966084
  165.6 12.3 %copy-start.28 = (f32[1024]{0:T(1024)S(1)}, f32[1024]{0:T(1024)}, u32[]{:S(2)}) copy-start(f32[1024]{0:T(1024)} %param.21) | copy-start | bytes 12292
  169.0 13.0 %copy-start.38 = (f32[1024]{0:T(1024)S(1)}, f32[1024]{0:T(1024)}, u32[]{:S(2)}) copy-start(f32[1024]{0:T(1024)} %param.28) | copy-start | bytes 12292
  169.1 16.3 %copy-start.9 = (bf16[320,1024]{1,0:T(8,128)(2,1)S(1)}, bf16[320,1024]{1,0:T(8,128)(2,1)}, u32[]{:S(2)}) copy-start(bf16[320,1024]{1,0:T(8,128)(2,1)} %param.17) | copy-start | bytes 1966084
  169.1 25.7 %all-gather.7.cloned.1.call-start = ((), (), s32[]{:S(2)}) async-start(), calls=%async_computation.7 | async-start | bytes 1966080 | tf_op jit(solution)/shard_map/all_gather | solution.py:540
  177.9 4.1 copy-start.2
  184.0 28.2 %all-gather.9.cloned.1.call-start = ((), (), s32[]{:S(2)}) async-start(), calls=%async_computation.9 | async-start | bytes 1966080 | tf_op jit(solution)/shard_map/all_gather | solution.py:563
  187.0 62.4 %reduce-scatter.12.cloned.1.call-start = ((), (), s32[]{:S(2)}) async-start(), calls=%async_computation.10 | async-start | bytes 1966080 | tf_op jit(solution)/shard_map/reduce_scatter | solution.py:572
  230.8 28.6 %reduce-scatter.10.cloned.1.call-start = ((), (), s32[]{:S(2)}) async-start(), calls=%async_computation.8 | async-start | bytes 1966080 | tf_op jit(solution)/shard_map/reduce_scatter | solution.py:544
  249.3 30.2 %all-gather.11.cloned.1.call-start = ((), (), s32[]{:S(2)}) async-start(), calls=%async_computation.11 | async-start | bytes 1966080 | tf_op jit(solution)/shard_map/all_gather | solution.py:585
  259.4 5.1 copy-start.14
  265.9 16.0 %copy-start.44 = (f32[320]{0:T(512)}, f32[320]{0:T(512)S(1)}, u32[]{:S(2)}) copy-start(f32[320]{0:T(512)S(1)} %negate_multiply_fusion.2) | copy-start | bytes 3844
  268.7 202.4 %reduce-scatter.16.cloned.1.call-start = ((), (), s32[]{:S(2)}) async-start(), calls=%async_computation.13 | async-start | bytes 540672
  286.3 6.5 %copy-start.8 = (f32[2,320,8,64]{1,3,2,0:T(8,128)S(1)}, f32[2,320,8,64]{1,3,2,0:T(8,128)}, u32[]{:S(2)}) copy-start(f32[2,320,8,64]{1,3,2,0:T(8,128)} %copy.96) | copy-start | bytes 3932164
  286.3 6.5 %copy-start.12 = (bf16[2,320,8,64]{1,3,2,0:T(8,128)(2,1)S(1)}, bf16[2,320,8,64]{1,3,2,0:T(8,128)(2,1)}, u32[]{:S(2)}) copy-start(bf16[2,320,8,64]{1,3,2,0:T(8,128)(2,1)} %copy.104) | copy-start | bytes 1966084
  286.3 6.5 %copy-start.26 = (f32[2,8,320]{2,1,0:T(8,128)S(1)}, f32[2,8,320]{2,1,0:T(8,128)}, u32[]{:S(2)}) copy-start(f32[2,8,320]{2,1,0:T(8,128)} %log_add_fusion) | copy-start | bytes 61444
  286.3 6.5 %copy-start.40 = (f32[8,64]{1,0:T(8,128)S(1)}, f32[8,64]{1,0:T(8,128)}, u32[]{:S(2)}) copy-start(f32[8,64]{1,0:T(8,128)} %copy-done.39) | copy-start | bytes 6148
  286.3 12.7 %slice-start = ((s8[7864320]{0:T(1024)(128)(4,1)}), s8[4194304]{0:T(1024)(128)(4,1)S(1)}, s32[]{:S(2)}) async-start(s8[7864320]{0:T(1024)(128)(4,1)} %bitcast.96), calls=%async_computation.14 | async-start | bytes 8388608
  292.7 6.3 %slice-start.1 = ((s8[7864320]{0:T(1024)(128)(4,1)}), s8[3670016]{0:T(1024)(128)(4,1)S(1)}, s32[]{:S(2)}) async-start(s8[7864320]{0:T(1024)(128)(4,1)} %bitcast.96), calls=%async_computation.15 | async-start | bytes 7340032
  321.6 150.9 %reduce-scatter.14.cloned.1.call-start = ((), (), s32[]{:S(2)}) async-start(), calls=%async_computation.12 | async-start | bytes 1966080 | tf_op jit(solution)/shard_map/reduce_scatter | solution.py:609
  329.2 5.9 %copy-start.56 = (bf16[640,1024]{1,0:T(8,128)(2,1)S(1)}, bf16[640,1024]{1,0:T(8,128)(2,1)}, u32[]{:S(2)}) copy-start(bf16[640,1024]{1,0:T(8,128)(2,1)} %all-gather.7.cloned.1.call-done) | copy-start | bytes 3932164
  329.2 5.9 %copy-start.61 = (bf16[640,2048]{1,0:T(8,128)(2,1)S(1)}, bf16[640,2048]{1,0:T(8,128)(2,1)}, u32[]{:S(2)}) copy-start(bf16[640,2048]{1,0:T(8,128)(2,1)} %copy-done.60) | copy-start | bytes 7864324
  335.0 5.1 copy-start.57
  335.0 5.1 copy-start.59
  468.5 4.0 copy-start.32
  468.5 4.0 copy-start.36
  468.5 5.6 %copy-start.47 = (f32[320]{0:T(512)S(1)}, f32[320]{0:T(512)}, u32[]{:S(2)}) copy-start(f32[320]{0:T(512)} %copy-done.46) | copy-start | bytes 3844
  468.6 5.6 %copy-start.42 = (f32[320]{0:T(512)S(1)}, f32[320]{0:T(512)}, u32[]{:S(2)}) copy-start(f32[320]{0:T(512)} %copy-done.41) | copy-start | bytes 3844
  469.3 6.8 %copy-start.35 = (f32[4096]{0:T(1024)S(1)}, f32[4096]{0:T(1024)}, u32[]{:S(2)}) copy-start(f32[4096]{0:T(1024)} %copy-done.34) | copy-start | bytes 49156
  469.3 6.8 %copy-start.49 = (f32[1024]{0:T(1024)S(1)}, f32[1024]{0:T(1024)}, u32[]{:S(2)}) copy-start(f32[1024]{0:T(1024)} %get-tuple-element.91) | copy-start | bytes 12292
  469.3 6.8 %copy-start.50 = (f32[1024]{0:T(1024)S(1)}, f32[1024]{0:T(1024)}, u32[]{:S(2)}) copy-start(f32[1024]{0:T(1024)} %get-tuple-element.71) | copy-start | bytes 12292
  469.3 6.8 %copy-start.51 = (f32[1024]{0:T(1024)S(1)}, f32[1024]{0:T(1024)}, u32[]{:S(2)}) copy-start(f32[1024]{0:T(1024)} %get-tuple-element.77) | copy-start | bytes 12292
  469.3 6.8 %copy-start.52 = (f32[1024]{0:T(1024)S(1)}, f32[1024]{0:T(1024)}, u32[]{:S(2)}) copy-start(f32[1024]{0:T(1024)} %get-tuple-element.93) | copy-start | bytes 12292
  469.3 6.8 %copy-start.55 = (f32[5]{0:T(128)S(1)}, f32[5]{0:T(128)}, u32[]{:S(2)}) copy-start(f32[5]{0:T(128)} %stack.63) | copy-start | bytes 64
  470.1 50.5 %copy-start.4 = (f32[320,1024]{1,0:T(8,128)S(1)}, f32[320,1024]{1,0:T(8,128)}, u32[]{:S(2)}) copy-start(f32[320,1024]{1,0:T(8,128)} %copy-done.3) | copy-start | bytes 3932164
  470.1 50.5 %copy-start.45 = (f32[320]{0:T(512)S(1)}, f32[320]{0:T(512)}, u32[]{:S(2)}) copy-start(f32[320]{0:T(512)} %copy-done.44) | copy-start | bytes 3844
  472.5 48.1 %copy-start.10 = (bf16[320,1024]{1,0:T(8,128)(2,1)S(1)}, bf16[320,1024]{1,0:T(8,128)(2,1)}, u32[]{:S(2)}) copy-start(bf16[320,1024]{1,0:T(8,128)(2,1)} %reduce-scatter.14.cloned.1.call-done) | copy-start | bytes 1966084
  (25 other events, 54.3 us)
Sparse Core Ops, SparseCore 0:
  13.6 12.1 all-gather.4
  169.2 8.7 reduce-scatter.7
  184.1 10.6 all-gather.6
  196.8 10.5 all-gather.8
  230.9 9.9 reduce-scatter.11
  249.4 9.9 reduce-scatter.9
  268.8 10.6 all-gather.10
  321.7 137.4 reduce-scatter.15
  462.0 4.6 reduce-scatter.13

commit v2 on v1

--- a/solution.py
+++ b/solution.py
@@ -4,6 +4,14 @@
 from jax.experimental import pallas as pl
 from jax.experimental.pallas import tpu as pltpu
 from jax.sharding import PartitionSpec as P
+
+HD = 64
+BUFFER = 64
+SLOTS = 320
+
+
+eps_norm = 1e-06
+
 
 MESH = pl.DeviceIdType.MESH
 
@@ -37,20 +45,26 @@
     def across_y(self):
         return (self.chip(self.z, 1 - self.y, self.x), self.t)
 
+    def near(self):
+        return (self.chip(self.z + 1 - 2 * (self.z % 2), self.y, self.x), self.t)
+
+    def far(self):
+        return (self.chip((self.z + 2) % 4, self.y, self.x), self.t)
+
     def twin(self):
         return (self.dp, 1 - self.t)
 
 
 def enter(at):
     barrier = pltpu.get_barrier_semaphore()
-    for other in (at.across_x(), at.across_y(), at.inward(), at.twin()):
+    for other in (at.across_x(), at.across_y(), at.inward(), at.twin(), at.far()):
         pl.semaphore_signal(barrier, inc=1, device_id=other, device_id_type=MESH)
 
     @pl.when(at.w == 1)
     def _():
         pl.semaphore_signal(barrier, inc=1, device_id=at.outward(), device_id_type=MESH)
 
-    pl.semaphore_wait(barrier, 4 + at.w)
+    pl.semaphore_wait(barrier, 5 + at.w)
 
 
 class Gather:
@@ -283,12 +297,12 @@
 
             @pl.when(at.w == 0)
             def _():
-                out[...] = total
+                out(total)
 
             @pl.when(at.w == 1)
             def _():
                 self.wait_line(p, z, z)
-                out[...] = total + self.zl[z, :, self.cols(p)].astype(jnp.float32)
+                out(total + self.zl[z, :, self.cols(p)].astype(jnp.float32))
 
     def drain(self, p):
         at = self.at
@@ -299,7 +313,12 @@
             if k > 0:
                 self.z_in(p, z, z).wait_send()
 
+
 WIDTHS = (1536, 512, 1024, 1024, 1024, 1024)
+QKV, OUT, UP, DOWN = 0, 1536, 2048, 4096
+BF, F32 = jnp.bfloat16, jnp.float32
+SUMS = ("bq", "bv", "bout", "bdown", "g1", "s1", "g2", "s2", "x", "mid", "res", "branch", "feed")
+BLOCK = 32
 
 
 def pieces_of():
@@ -310,106 +329,519 @@
     return out
 
 
-def gather_kernel(own_ref, full_ref, held, sem, send, recv):
+def nn(a, b):
+    return lax.dot_general(a, b, (((1,), (0,)), ((), ())), preferred_element_type=F32)
+
+
+def nt(a, b):
+    return lax.dot_general(a, b, (((1,), (1,)), ((), ())), preferred_element_type=F32)
+
+
+def at_rows(start, size):
+    return pl.ds(pl.multiple_of(start, size), size)
+
+
+def fold(v):
+    return jnp.sum(v.reshape(v.shape[0] // 8, 8, v.shape[1]), axis=0)
+
+
+def normed(v):
+    centre = jnp.mean(v, axis=1, keepdims=True)
+    offset = v - centre
+    r = lax.rsqrt(jnp.mean(offset * offset, axis=1, keepdims=True) + eps_norm)
+    return offset * r, r
+
+
+def norm_back(dy, n, r, gain):
+    dn = dy * gain
+    first = jnp.mean(dn, axis=1, keepdims=True)
+    second = jnp.mean(dn * n, axis=1, keepdims=True)
+    return r * (dn - first - n * second)
+
+
+def block_kernel(
+    counts, x_ref, cot_ref, wqkv, wout, wup, wdown, bqv, bout, bup, bdown, g1, s1, g2, s2,
+    act_out, gin_out, o_qkv, o_out, o_up, o_down, o_sums,
+    W, G2, xh, yh, xf, yf, zl, rows1, dfeed, qkv, probs, heads, mid, rows2, act, gp, datt, dproj,
+    tall, own_a, own_b, send_a, send_b, got, acc, acc_up, sums, sums_got,
+    sem_in, ag_send, ag_recv, rs_send, rs_recv, pair_send, pair_recv, sums_send, sums_recv,
+):
     at = Place()
-    shard = own_ref.shape[0]
+    t = at.t
+    shard = wup.shape[0]
+    pieces = pieces_of()
+    n_pieces = len(pieces)
+    own = x_ref.shape[0]
+    group = 2 * own
+    width = x_ref.shape[1]
+    mine = at_rows(t * own, own)
+    dbr = dfeed
+    theirs = at_rows((1 - t) * own, own)
+
+    here = at_rows(at.dp * shard, shard)
+    loads = [
+        pltpu.make_async_copy(src, W.at[here, pl.ds(c0, n)], sem_in.at[i])
+        for i, (src, c0, n) in enumerate(
+            [(wqkv.at[j], QKV + 512 * j, 512) for j in range(3)]
+            + [(wout, OUT, 512), (wup, UP, 2048), (wdown, DOWN, 2048)]
+        )
+    ]
+    for c in loads:
+        c.start()
     enter(at)
-    pieces = pieces_of()
-    g = Gather(at, held, shard, pieces, send, recv)
-    cp = pltpu.make_async_copy(own_ref, held.at[pl.ds(pl.multiple_of(at.dp * shard, shard), shard), :], sem)
-    cp.start()
-    cp.wait()
-    n = len(pieces)
+    g = Gather(at, W, shard, pieces, ag_send, ag_recv)
+    for c in loads:
+        c.wait()
     g.line(0, 0)
-    for p in range(n):
-        for k in range(1, 4):
-            g.line(p, k)
-            g.plane(p, k - 1)
-            if k == 2 and p + 1 < n:
-                g.line(p + 1, 0)
-        g.plane(p, 3)
-    for p in range(n):
+
+    steps = []
+    for p in range(n_pieces):
+        for k in range(4):
+            def step(p=p, k=k):
+                if k < 3:
+                    g.line(p, k + 1)
+                g.plane(p, k)
+                if k == 1 and p + 1 < n_pieces:
+                    g.line(p + 1, 0)
+            steps.append(step)
+    done = [0]
+
+    def gather(n):
+        while n > 0 and done[0] < len(steps):
+            steps[done[0]]()
+            done[0] += 1
+            n -= 1
+
+    def need(p):
+        gather(4 * p + 5 - done[0])
         g.finish(p)
+
+    home = {0: (W, UP, UP + 1536), 1: (W, UP + 1536, DOWN), 2: (W, DOWN, DOWN + 1024), 3: (W, DOWN + 1024, DOWN + 2048),
+            4: (G2, 0, 1024), 5: (G2, 1024, 2048)}
+    sc = Scatter(at, lambda p: home[p], shard, pieces, xh, yh, xf, yf, zl, rs_send, rs_recv)
+
+    def write(p):
+        def store(total):
+            if p == 0:
+                for j in range(3):
+                    o_qkv[j] = total[:, 512 * j : 512 * (j + 1)]
+            elif p == 1:
+                o_out[...] = total
+            elif p < 4:
+                o_up[:, (p - 2) * 1024 : (p - 1) * 1024] = total
+            else:
+                o_down[:, (p - 4) * 1024 : (p - 3) * 1024] = total
+        return store
+
+    queue = []
+
+    def reduce_begin(p):
+        sc.begin(p)
+        for k in (3, 2, 1, 0):
+            queue.append(lambda p=p, k=k: sc.plane(p, k))
+        for k in (3, 2, 1, 0):
+            queue.append(lambda p=p, k=k: sc.line(p, k, write(p)))
+
+    def scatter(n):
+        while n > 0 and queue:
+            queue.pop(0)()
+            n -= 1
+
+    def pair(i, src, dst):
+        return pltpu.make_async_remote_copy(
+            src_ref=src, dst_ref=dst, send_sem=pair_send.at[i], recv_sem=pair_recv.at[i],
+            device_id=at.twin(), device_id_type=MESH,
+        )
+
+    def share(i, ref):
+        c = pair(i, ref.at[mine, :], ref.at[mine, :])
+        c.start()
+        return c
+
+    def take(i, ref):
+        pair(i, ref.at[theirs, :], ref.at[theirs, :]).wait_recv()
+
+    for ref in (acc, acc_up):
+        ref[...] = jnp.zeros_like(ref)
+    total_of = {name: acc.at[i] for i, name in enumerate(SUMS)}
+
+    def add(name, v):
+        ref = total_of[name]
+        ref[...] += fold(v)
+
+    def valid_of(image, start, size):
+        slot = lax.broadcasted_iota(jnp.int32, (size, 1), 0) + start
+        return slot < counts[image] + BUFFER
+
+    def each_block(body):
+        def go(b, _):
+            body(b * BLOCK, pl.ds(pl.multiple_of(b * BLOCK, BLOCK), BLOCK))
+            return 0
+        lax.fori_loop(0, own // BLOCK, go, 0)
+
+    def tiles(first, last, body, size=256):
+        def go(i, _):
+            body(pl.multiple_of(i * size, size))
+            return 0
+        lax.fori_loop(first // size, last // size, go, 0)
+
+    def flip(src):
+        def body(c):
+            tall[pl.ds(c, 128), :] = src[:, pl.ds(c, 128)].T
+        tiles(0, src.shape[1], body, 128)
+
+    def first_norm(b, r):
+        xv = x_ref[r, :].astype(F32)
+        keep = valid_of(t, b, BLOCK).astype(F32)
+        n, _ = normed(xv)
+        mine_b = pl.ds(pl.multiple_of(t * own + b, BLOCK), BLOCK)
+        rows1[mine_b, :] = (n * g1[...] + s1[...]).astype(BF)
+        add("x", keep * xv * xv)
+        low = (cot_ref[r, :].astype(F32) * keep).astype(BF)
+        dfeed[mine_b, :] = low
+        add("bdown", low.astype(F32))
+
+    each_block(first_norm)
+    shares = [share(0, rows1), share(1, dfeed)]
+    gather(1)
+    take(1, dfeed)
+    flip(dfeed)
+    gather(1)
+    take(0, rows1)
+    need(0)
+
+    def project(c):
+        v = nn(rows1[...], W[:, pl.ds(c, 256)])
+        part = c // 512
+        inside = pl.ds(pl.multiple_of(c % 512 + t * 512, 256), 256)
+        bias = jnp.where(part == 0, bqv[0:1, inside], jnp.where(part == 2, bqv[1:2, inside], 0.0))
+        scale = jnp.where(part == 0, HD**-0.5, 1.0)
+        qkv[:, pl.ds(c, 256)] = ((v + bias) * scale).astype(BF)
+
+    tiles(0, 1536, project)
+    gather(2)
+
+    first_lanes = lax.broadcasted_iota(jnp.int32, (own, 128), 1) < HD
+
+    def attend(it):
+        image, j = it // 4, it % 4
+        r = pl.ds(pl.multiple_of(image * own, own), own)
+        c = j * 128
+        q2 = qkv[r, pl.ds(pl.multiple_of(c, 128), 128)]
+        k2 = qkv[r, pl.ds(pl.multiple_of(c + 512, 128), 128)]
+        v_t = qkv[r, pl.ds(pl.multiple_of(c + 1024, 128), 128)].T
+        hide = jnp.where(valid_of(image, 0, own), 0.0, -1e30)
+        outs = []
+        for a in range(2):
+            qm = jnp.where(first_lanes if a == 0 else ~first_lanes, q2, jnp.zeros_like(q2))
+            s = nt(k2, qm) + hide
+            e = jnp.exp(s - jnp.max(s, axis=0, keepdims=True))
+            low = (e * (1.0 / jnp.sum(e, axis=0, keepdims=True))).astype(BF)
+            probs[it * 2 + a] = low
+            outs.append(nn(v_t[a * HD : (a + 1) * HD], low))
+        heads[r, pl.ds(pl.multiple_of(c, 128), 128)] = jnp.concatenate(outs, axis=0).T.astype(BF)
+
+    def attend_some(first, last, body):
+        def go(i, _):
+            body(i)
+            return 0
+        lax.fori_loop(first, last, go, 0)
+
+    for i in range(4):
+        attend_some(2 * i, 2 * i + 2, attend)
+        gather(1)
+    need(1)
+
+    def reduced(i, src, cols, k, keep, send):
+        def other(c):
+            send[:, pl.ds(c, 256)] = nt(src[theirs, :], W[pl.ds(c, 256), cols]).astype(BF)
+        tiles(0, width, other)
+        copy = pair(i, send, got.at[k])
+        copy.start()
+        def self(c):
+            keep[:, pl.ds(c, 256)] = nt(src[mine, :], W[pl.ds(c, 256), cols])
+        tiles(0, width, self)
+        return copy
+
+    branch_copy = reduced(2, heads, pl.ds(OUT, 512), 0, own_a, send_a)
+    gather(1)
+    branch_copy.wait()
+
+    def second_norm(b, r):
+        keep = valid_of(t, b, BLOCK).astype(F32)
+        branch = own_a[r, :] + got[0, r, :].astype(F32) + bout[...]
+        m = x_ref[r, :].astype(F32) + branch
+        mid[r, :] = m
+        add("branch", keep * branch * branch)
+        add("mid", keep * m * m)
+        n, _ = normed(m)
+        rows2[pl.ds(pl.multiple_of(t * own + b, BLOCK), BLOCK), :] = (n * g2[...] + s2[...]).astype(BF)
+
+    each_block(second_norm)
+    shares.append(share(3, rows2))
+    gather(1)
+    take(3, rows2)
+
+    def hidden(c):
+        u = nn(rows2[...], W[:, pl.ds(UP + c, 256)]) + bup[:, pl.ds(pl.multiple_of(t * 2048 + c, 256), 256)]
+        below = 0.5 * (1.0 + lax.erf(u * (0.5**0.5)))
+        dense = jnp.exp(-0.5 * u * u) * 0.3989422804014327
+        act[:, pl.ds(c, 256)] = (u * below).astype(BF)
+        gp[:, pl.ds(c, 256)] = (below + u * dense).astype(BF)
+
+    def grad_down(c):
+        G2[:, pl.ds(c, 256)] = nn(tall[...], act[:, pl.ds(c, 256)]).astype(BF)
+
+    need(2)
+    tiles(0, 1024, hidden)
+    gather(1)
+    tiles(0, 1024, grad_down)
+    need(3)
+    tiles(1024, 2048, hidden)
+    gather(1)
+    tiles(1024, 2048, grad_down)
+    flip(rows2)
+    reduce_begin(4)
+
+    def back_act(c):
+        d = nn(dfeed[...], W[:, pl.ds(DOWN + c, 256)])
+        low = (d * gp[:, pl.ds(c, 256)].astype(F32)).astype(BF)
+        gp[:, pl.ds(c, 256)] = low
+        acc_up[t, :, pl.ds(c, 256)] += fold(low.astype(F32))
+
+    need(4)
+    tiles(0, 1024, back_act)
+    gather(9)
+    reduce_begin(5)
+    need(5)
+    tiles(1024, 2048, back_act)
+    two_copy = reduced(4, gp, pl.ds(UP, 2048), 1, own_a, send_a)
+    feed_copy = reduced(5, act, pl.ds(DOWN, 2048), 2, own_b, send_b)
+    for p in range(n_pieces):
         g.drain(p)
-    cp = pltpu.make_async_copy(held, full_ref, sem)
-    cp.start()
-    cp.wait()
-
-
-def scatter_kernel(g_ref, out_ref, held, xh, yh, xf, yf, zl, sem, send, recv):
-    at = Place()
-    shard = out_ref.shape[0]
-    enter(at)
-    pieces = pieces_of()
-    cp = pltpu.make_async_copy(g_ref, held, sem)
-    cp.start()
-    cp.wait()
-    s = Scatter(at, lambda p: (held,) + pieces[p], shard, pieces, xh, yh, xf, yf, zl, send, recv)
-    n = len(pieces)
-    s.begin(0)
-    for p in range(n):
-        if p + 1 < n:
-            s.begin(p + 1)
-        for k in (3, 2, 1, 0):
-            s.plane(p, k)
-        if p > 0:
-            for k in (3, 2, 1, 0):
-                s.line(p - 1, k, out_ref.at[:, s.cols(p - 1)])
-    for k in (3, 2, 1, 0):
-        s.line(n - 1, k, out_ref.at[:, s.cols(n - 1)])
-    for p in range(n):
-        s.drain(p)
-
-
-def gather_all(own):
-    shard, cols = own.shape
+    scatter(2)
+
+    def grad_up(c):
+        W[:, pl.ds(DOWN + c, 256)] = nn(tall[...], gp[:, pl.ds(c, 256)]).astype(BF)
+
+    two_copy.wait()
+    shares[1].wait_send()
+
+    def second_back(b, r):
+        dy = own_a[r, :] + got[1, r, :].astype(F32)
+        n, scale = normed(mid[r, :])
+        keep = valid_of(t, b, BLOCK).astype(F32)
+        add("g2", dy * n)
+        add("s2", dy)
+        d = cot_ref[r, :].astype(F32) * keep + norm_back(dy, n, scale, g2[...])
+        gin_out[r, :] = d
+        low = d.astype(BF)
+        dbr[pl.ds(pl.multiple_of(t * own + b, BLOCK), BLOCK), :] = low
+        add("bout", low.astype(F32))
+
+    each_block(second_back)
+    shares.append(share(6, dbr))
+    tiles(0, 1024, grad_up)
+    reduce_begin(2)
+    scatter(2)
+    tiles(1024, 2048, grad_up)
+    reduce_begin(3)
+    scatter(2)
+    take(6, dbr)
+
+    def back_heads(c):
+        datt[:, pl.ds(c, 256)] = nn(dbr[...], W[:, pl.ds(OUT + c, 256)]).astype(BF)
+
+    tiles(0, 512, back_heads)
+    flip(dbr)
+
+    def grad_out(c):
+        W[:, pl.ds(UP + 1536 + c, 256)] = nn(tall[...], heads[:, pl.ds(c, 256)]).astype(BF)
+
+    tiles(0, 512, grad_out)
+    reduce_begin(1)
+    scatter(4)
+
+    def attend_back(it):
+        image, j = it // 4, it % 4
+        r = pl.ds(pl.multiple_of(image * own, own), own)
+        c = j * 128
+        q2 = qkv[r, pl.ds(pl.multiple_of(c, 128), 128)]
+        k_t = qkv[r, pl.ds(pl.multiple_of(c + 512, 128), 128)].T
+        v2 = qkv[r, pl.ds(pl.multiple_of(c + 1024, 128), 128)]
+        da = datt[r, pl.ds(pl.multiple_of(c, 128), 128)]
+        dq, dk, dv = [], [], []
+        for a in range(2):
+            dam = jnp.where(first_lanes if a == 0 else ~first_lanes, da, jnp.zeros_like(da))
+            low = probs[it * 2 + a]
+            p = low.astype(F32)
+            dp = nt(v2, dam)
+            ds = (p * (dp - jnp.sum(p * dp, axis=0, keepdims=True))).astype(BF)
+            dq.append(nn(k_t[a * HD : (a + 1) * HD], ds))
+            dk.append(nn(ds, q2))
+            dv.append(nn(low, da))
+        for base, v in (
+            (0, jnp.concatenate(dq, axis=0).T * HD**-0.5),
+            (512, jnp.where(first_lanes, dk[0], dk[1])),
+            (1024, jnp.where(first_lanes, dv[0], dv[1])),
+        ):
+            v = v.astype(BF)
+            dproj[r, pl.ds(pl.multiple_of(base + c, 128), 128)] = v
+            if base != 512:
+                lanes = pl.ds(pl.multiple_of(t * 512 + c, 128), 128)
+                ref = total_of["bq" if base == 0 else "bv"]
+                ref[:, lanes] += fold(v.astype(F32))
+
+    for i in range(4):
+        attend_some(2 * i, 2 * i + 2, attend_back)
+        scatter(4)
+
+    one_copy = reduced(7, dproj, pl.ds(QKV, 1536), 3, own_a, send_a)
+    flip(rows1)
+
+    def grad_qkv(c):
+        W[:, pl.ds(UP + c, 256)] = nn(tall[...], dproj[:, pl.ds(c, 256)]).astype(BF)
+
+    tiles(0, 1536, grad_qkv)
+    reduce_begin(0)
+    one_copy.wait()
+
+    def first_back(b, r):
+        dy = own_a[r, :] + got[3, r, :].astype(F32)
+        n, scale = normed(x_ref[r, :].astype(F32))
+        add("g1", dy * n)
+        add("s1", dy)
+        gin_out[r, :] += norm_back(dy, n, scale, g1[...])
+
+    each_block(first_back)
+    scatter(4)
+    feed_copy.wait()
+
+    def finish_feed(b, r):
+        keep = valid_of(t, b, BLOCK).astype(F32)
+        feed = own_b[r, :] + got[2, r, :].astype(F32) + bdown[...]
+        res = mid[r, :] + feed
+        add("feed", keep * feed * feed)
+        add("res", keep * res * res)
+        act_out[r, :] = (keep * res).astype(BF)
+
+    each_block(finish_feed)
+
+    for i in range(8):
+        sums[i : i + 1, :] = jnp.sum(acc[i], axis=0, keepdims=True)
+    for i in range(4):
+        sums[8 + i : 9 + i, :] = jnp.sum(acc_up[i // 2, :, (i % 2) * 1024 : (i % 2 + 1) * 1024], axis=0, keepdims=True)
+    lane = lax.broadcasted_iota(jnp.int32, (1, width), 1)
+    row = jnp.where(lane == 5, (counts[t] + BUFFER).astype(F32), 0.0)
+    for i, name in enumerate(("x", "mid", "res", "branch", "feed")):
+        row = jnp.where(lane == i, jnp.sum(jnp.sum(total_of[name][...], axis=0, keepdims=True), axis=1, keepdims=True), row)
+    sums[12:13, :] = row
+    sums[13:16, :] = jnp.zeros((3, width), F32)
+    for i, other in enumerate((at.twin(), at.across_x(), at.across_y(), at.near(), at.far())):
+        c = pltpu.make_async_remote_copy(
+            src_ref=sums, dst_ref=sums_got.at[i], send_sem=sums_send.at[i], recv_sem=sums_recv.at[i],
+            device_id=other, device_id_type=MESH,
+        )
+        c.start()
+        scatter(2)
+        c.wait()
+        sums[...] += sums_got[i]
+    o_sums[...] = sums[...]
+    scatter(1000)
+    for p in range(n_pieces):
+        sc.drain(p)
+    for i in (0, 2, 3):
+        shares[i].wait_send()
+
+
+def block(counts, stream, cotangent, w_qkv, w_out_t, w_up, w_down_t, b_qv, b_out, b_up, b_down, g1, s1, g2, s2):
+    own, width = stream.shape
+    shard = w_up.shape[0]
     n = len(WIDTHS)
+    cols = sum(WIDTHS)
+    rows = 16 * shard
+    group = 2 * own
+    vmem = pl.BlockSpec(memory_space=pltpu.VMEM)
+    hbm = pl.BlockSpec(memory_space=pl.ANY)
+    dma = pltpu.SemaphoreType.DMA
+    row = lambda v: v.reshape(1, -1)
     return pl.pallas_call(
-        gather_kernel,
-        out_shape=jax.ShapeDtypeStruct((16 * shard, cols), jnp.bfloat16),
-        in_specs=[pl.BlockSpec(memory_space=pl.ANY)],
-        out_specs=pl.BlockSpec(memory_space=pl.ANY),
+        block_kernel,
+        out_shape=(
+            jax.ShapeDtypeStruct((own, width), BF),
+            jax.ShapeDtypeStruct((own, width), F32),
+            jax.ShapeDtypeStruct((3, shard, 512), F32),
+            jax.ShapeDtypeStruct((shard, 512), F32),
+            jax.ShapeDtypeStruct((shard, 2048), F32),
+            jax.ShapeDtypeStruct((shard, 2048), F32),
+            jax.ShapeDtypeStruct((16, width), F32),
+        ),
+        in_specs=[pl.BlockSpec(memory_space=pltpu.SMEM), vmem, vmem, hbm, hbm, hbm, hbm] + [vmem] * 8,
+        out_specs=(vmem,) * 7,
         scratch_shapes=[
-            pltpu.VMEM((16 * shard, cols), jnp.bfloat16),
-            pltpu.SemaphoreType.DMA,
-            pltpu.SemaphoreType.DMA((n, 6, 4)),
-            pltpu.SemaphoreType.DMA((n, 5, 4)),
+            pltpu.VMEM((rows, cols), BF),
+            pltpu.VMEM((rows, 2048), BF),
+            pltpu.VMEM((4, shard // 2, cols), BF),
+            pltpu.VMEM((4, shard // 2, cols), BF),
+            pltpu.VMEM((4, shard, cols), BF),
+            pltpu.VMEM((4, shard, cols), BF),
+            pltpu.VMEM((5, shard, cols), BF),
+            pltpu.VMEM((group, width), BF),
+            pltpu.VMEM((group, width), BF),
+            pltpu.VMEM((group, 1536), BF),
+            pltpu.VMEM((16, own, own), BF),
+            pltpu.VMEM((group, 512), BF),
+            pltpu.VMEM((own, width), F32),
+            pltpu.VMEM((group, width), BF),
+            pltpu.VMEM((group, 2048), BF),
+            pltpu.VMEM((group, 2048), BF),
+            pltpu.VMEM((group, 512), BF),
+            pltpu.VMEM((group, 1536), BF),
+            pltpu.VMEM((width, group), BF),
+            pltpu.VMEM((own, width), F32),
+            pltpu.VMEM((own, width), F32),
+            pltpu.VMEM((own, width), BF),
+            pltpu.VMEM((own, width), BF),
+            pltpu.VMEM((4, own, width), BF),
+            pltpu.VMEM((len(SUMS), 8, width), F32),
+            pltpu.VMEM((2, 8, 2048), F32),
+            pltpu.VMEM((16, width), F32),
+            pltpu.VMEM((5, 16, width), F32),
+            dma((6,)),
+            dma((n, 6, 4)),
+            dma((n, 5, 4)),
+            dma((n, 5, 4)),
+            dma((n, 5, 5)),
+            dma((8,)),
+            dma((8,)),
+            dma((5,)),
+            dma((5,)),
         ],
-        compiler_params=pltpu.CompilerParams(collective_id=1, has_side_effects=True, vmem_limit_bytes=48 << 20),
-    )(own)
-
-
-def scatter_all(grads):
-    rows, cols = grads.shape
-    shard = rows // 16
-    n = len(WIDTHS)
-    bf = jnp.bfloat16
-    return pl.pallas_call(
-        scatter_kernel,
-        out_shape=jax.ShapeDtypeStruct((shard, cols), jnp.float32),
-        in_specs=[pl.BlockSpec(memory_space=pl.ANY)],
-        out_specs=pl.BlockSpec(memory_space=pltpu.VMEM),
-        scratch_shapes=[
-            pltpu.VMEM((rows, cols), bf),
-            pltpu.VMEM((4, shard // 2, cols), bf),
-            pltpu.VMEM((4, shard // 2, cols), bf),
-            pltpu.VMEM((4, shard, cols), bf),
-            pltpu.VMEM((4, shard, cols), bf),
-            pltpu.VMEM((5, shard, cols), bf),
-            pltpu.SemaphoreType.DMA,
-            pltpu.SemaphoreType.DMA((n, 5, 4)),
-            pltpu.SemaphoreType.DMA((n, 5, 5)),
-        ],
-        compiler_params=pltpu.CompilerParams(collective_id=2, has_side_effects=True, vmem_limit_bytes=48 << 20),
-    )(grads)
-
-
-HD = 64
-BUFFER = 64
-SLOTS = 320
-
-
-eps_norm = 1e-06
+        compiler_params=pltpu.CompilerParams(
+            collective_id=1, has_side_effects=True, vmem_limit_bytes=63 << 20
+        ),
+    )(
+        counts, stream, cotangent, w_qkv, w_out_t, w_up, w_down_t,
+        b_qv, row(b_out), row(b_up), row(b_down), row(g1), row(s1), row(g2), row(s2),
+    )
+
+
+def local_fast(
+    stream, counts, cotangent, w_qkv, b_qv, w_out, b_out, w_fc1, b_fc1, w_fc2, b_fc2,
+    gain_one, shift_one, gain_two, shift_two,
+):
+    acts, grad_in, p_qkv, p_out, p_up, p_down, sums = block(
+        counts, stream, cotangent, w_qkv, w_out.T, w_fc1, w_fc2.T, b_qv, b_out, b_fc1, b_fc2,
+        gain_one, shift_one, gain_two, shift_two,
+    )
+    place = lax.axis_index("dp") * 2 + lax.axis_index("tensor")
+    vectors = lax.dynamic_slice(sums[:8], (0, place * 32), (8, 32))
+    up = lax.dynamic_slice(sums[8:12].reshape(-1), (place * 128,), (128,))
+    rms = jnp.sqrt(sums[12, :5] / (sums[12, 5] * stream.shape[1]))
+    return (
+        acts, grad_in, p_qkv, vectors[0:2], p_out.T, vectors[2], p_up, up, p_down.T, vectors[3],
+        vectors[4], vectors[5], vectors[6], vectors[7], rms,
+    )
 
 
 def layer_norm(values, gain, shift):
@@ -490,21 +922,12 @@
     validity_all = (slot_index[None, :] < (BUFFER + counts)[:, None]).astype(jnp.float32)
     own_validity = lax.dynamic_slice_in_dim(validity_all, tensor_pos * own_images, own_images, 0)
     own_valid = own_validity.reshape(own_rows, 1)
-    fast = lax.axis_size("dp") == 16 and lax.axis_size("tensor") == 2
-    if fast:
-        own = jnp.concatenate([w_qkv[0], w_qkv[1], w_qkv[2], w_out.T, w_fc1, w_fc2.T], axis=1)
-        full = gather_all(own)
-        qkv_full = jnp.stack([full[:, 0:512], full[:, 512:1024], full[:, 1024:1536]])
-        out_full = full[:, 1536:2048].T
-        up_full = full[None, :, 2048:4096]
-        down_full = full[:, 4096:6144].T
-    else:
-        qkv_full, out_full, up_full, down_full = (
-            lax.all_gather(w_qkv, "dp", axis=1, tiled=True),
-            lax.all_gather(w_out, "dp", axis=1, tiled=True),
-            lax.all_gather(w_fc1[None], "dp", axis=1, tiled=True),
-            lax.all_gather(w_fc2, "dp", axis=1, tiled=True),
-        )
+    qkv_full, out_full, up_full, down_full = (
+        lax.all_gather(w_qkv, "dp", axis=1, tiled=True),
+        lax.all_gather(w_out, "dp", axis=1, tiled=True),
+        lax.all_gather(w_fc1[None], "dp", axis=1, tiled=True),
+        lax.all_gather(w_fc2, "dp", axis=1, tiled=True),
+    )
     head_width = w_qkv.shape[2]
     unit_width = w_fc1.shape[1]
     bias_query = lax.dynamic_slice_in_dim(b_qv[0], tensor_pos * head_width, head_width, 0)
@@ -626,32 +1049,20 @@
     bias_up_full = lax.dynamic_update_slice(
         jnp.zeros((b_fc1.shape[0],), jnp.float32), grad_bias_up, (tensor_pos * unit_width,)
     )
-    if fast:
-        low = lambda v: v.astype(jnp.bfloat16)
-        grads = jnp.concatenate(
-            [low(grad_qkv[0]), low(grad_qkv[1]), low(grad_qkv[2]), low(grad_out).T, low(grad_up[0]), low(grad_down).T],
-            axis=1,
-        )
-        part = scatter_all(grads)
-        qkv_part = jnp.stack([part[:, 0:512], part[:, 512:1024], part[:, 1024:1536]])
-        out_part = part[:, 1536:2048].T
-        up_part = part[None, :, 2048:4096]
-        down_part = part[:, 4096:6144].T
-    else:
-        qkv_part, out_part, up_part, down_part = (
-            lax.psum_scatter(
-                grad_qkv.astype(jnp.bfloat16), "dp", scatter_dimension=1, tiled=True
-            ).astype(jnp.float32),
-            lax.psum_scatter(
-                grad_out.astype(jnp.bfloat16), "dp", scatter_dimension=1, tiled=True
-            ).astype(jnp.float32),
-            lax.psum_scatter(
-                grad_up.astype(jnp.bfloat16), "dp", scatter_dimension=1, tiled=True
-            ).astype(jnp.float32),
-            lax.psum_scatter(
-                grad_down.astype(jnp.bfloat16), "dp", scatter_dimension=1, tiled=True
-            ).astype(jnp.float32),
-        )
+    qkv_part, out_part, up_part, down_part = (
+        lax.psum_scatter(
+            grad_qkv.astype(jnp.bfloat16), "dp", scatter_dimension=1, tiled=True
+        ).astype(jnp.float32),
+        lax.psum_scatter(
+            grad_out.astype(jnp.bfloat16), "dp", scatter_dimension=1, tiled=True
+        ).astype(jnp.float32),
+        lax.psum_scatter(
+            grad_up.astype(jnp.bfloat16), "dp", scatter_dimension=1, tiled=True
+        ).astype(jnp.float32),
+        lax.psum_scatter(
+            grad_down.astype(jnp.bfloat16), "dp", scatter_dimension=1, tiled=True
+        ).astype(jnp.float32),
+    )
     small_parts = (
         lax.psum_scatter(bias_qv_full, ("dp", "tensor"), scatter_dimension=1, tiled=True),
         lax.psum_scatter(grad_bias_out, ("dp", "tensor"), scatter_dimension=0, tiled=True),
@@ -682,8 +1093,9 @@
 
 
 def solution(mesh):
+    fast = mesh.shape["dp"] == 16 and mesh.shape["tensor"] == 2
     return jax.shard_map(
-        local,
+        local_fast if fast else local,
         mesh=mesh,
         in_specs=(
             P(("dp", "tensor"), None),

time: 538 us -> 280 us (0.52); the launches traced: 529 us -> 280 us
  matrix products: 92.4 us -> 0 us
  local copies, waits for them, and re-layouts: 63.2 us -> 10.8 us
  blocking collectives: 39.2 us -> 0 us
  other arithmetic: 33.8 us -> 1.21 us
  waiting for transfers between devices: 31.4 us -> 0 us
  Pallas kernels: 242 us -> 266 us
  between operations: 15.8 us -> 1.34 us
  starting transfers between devices: 11.9 us -> 0 us
    dot_general x18 -> x0, matrix products: 92.4 us -> none  [the longest x1 17.4 us: local(): jnp.dot(second_rows, up_full, preferred_element_type=jnp.float32) + bias_up]
    unnamed x1 -> x0, blocking collectives: 39.2 us -> none
    pallas_call x2 -> x1, Pallas kernels: 242 us -> 266 us  [block(): pl.pallas_call(block_kernel, out_shape=(jax.ShapeDtypeStruct((own, width)...]
    reduce_sum x13 -> x0, other arithmetic: 22.2 us -> none  [the longest x1 4.46 us: local(): jnp.sum(own_valid * member * member)]
    reduce_scatter x4 -> x0, waiting for transfers between devices: 18.8 us -> none  [the longest x1 10 us: local(): lax.psum_scatter(jnp.dot(taken, down_full, preferred_element_type=jnp.flo...]
    another operation x9 -> x0, local copies, waits for them, and re-layouts: 15.7 us -> none  [the longest x7 9.77 us: local(): jnp.stack([d_queries.reshape(group_rows, head_width), d_keys.reshape(grou...]
    unnamed x147 -> x18, local copies, waits for them, and re-layouts: 21.9 us -> 6.93 us
    squeeze x6 -> x1, local copies, waits for them, and re-layouts: 14.9 us -> 0.53 us  [local_fast(): vectors[7]]
  transfers between devices with their start and end apart: 9 -> 0, of which waited for: 4 -> 0; matrix products, arithmetic and copies ran while one was open for 12% -> 0% of each run, Pallas kernels for 46% -> 0%
where the time goes in v2:
time: 280 us
  Pallas kernels  266 us (95%)
  local copies, waits for them, and re-layouts  10.8 us (4%)
    pallas_call x1, Pallas kernels, block(): pl.pallas_call(block_kernel, out_shape=(jax.ShapeDtypeStruct((own, width)...  266 us
    unnamed x18, local copies, waits for them, and re-layouts  6.93 us

profile of v2, /device:TPU:0, one launch (start us, length us, event | category | flops | bytes accessed | tf_op | source)
XLA Modules:
  0.0 279.8 jit_solution(8611402785475366028)
XLA Ops:
  0.7 266.5 %shard_map.262 = (bf16[320,1024]{1,0:T(8,128)(2,1)}, f32[320,1024]{1,0:T(8,128)}, f32[3,64,512]{2,1,0:T(8,128)}, f32[64,512]{1,0:T(8,128)}, f32[64,2048]{1,0:T(8...) custom-call(s32[2]{0:T(128)} %counts.1, bf16[320,1024]{1,0:T(8,128)(2,1)} %x_ref.1, bf16[320,1024]{1,0:T(8,128)(2,1)} %cot_ref.1, ...), custom_call_target="tpu_custom_call" | custom-call | tf_op jit(solution)/shard_map/pallas_call | solution.py:768
  267.1 0.0 copy-start
  267.1 1.4 slice.43
  269.2 1.2 sqrt_bitcast_fusion
  270.4 0.8 slice_bitcast_fusion
  271.1 0.8 slice.33
  271.9 0.1 constant_dynamic-slice_fusion
  272.0 0.6 dynamic_slice.7
  272.6 0.6 slice.34
  273.1 0.5 slice_bitcast_fusion.1
  273.6 2.0 copy.39
  275.6 0.0 copy-done
  275.6 0.0 copy-start.3
  275.6 0.0 copy-start.4
  275.6 0.0 copy-start.2
  275.6 1.1 copy.40
  276.7 0.1 copy-done.3
  276.8 0.0 copy-start.1
  276.8 0.7 copy.41
  277.6 0.0 copy-done.4
  277.6 0.7 copy.42
  278.2 0.0 copy-done.2
  278.2 0.8 copy.43
  279.0 0.0 copy-done.1
  279.0 0.8 copy.44
  (1 shorter events, 0.0 us)
Async XLA Ops:
  267.1 8.5 %copy-start = (f32[320,1024]{1,0:T(8,128)S(1)}, f32[320,1024]{1,0:T(8,128)}, u32[]{:S(2)}) copy-start(f32[320,1024]{1,0:T(8,128)} %get-tuple-element.51) | copy-start | bytes 3932164
  275.6 1.2 copy-start.3
  275.6 2.0 copy-start.4
  275.6 2.6 copy-start.2
  276.8 2.2 copy-start.1

commit v3 on v2

--- a/solution.py
+++ b/solution.py
@@ -314,19 +314,217 @@
                 self.z_in(p, z, z).wait_send()
 
 
-WIDTHS = (1536, 512, 1024, 1024, 1024, 1024)
-QKV, OUT, UP, DOWN = 0, 1536, 2048, 4096
+class PairGather:
+    def __init__(self, at, full, shard, columns, sources, send, recv):
+        self.at, self.full, self.shard, self.columns, self.sources = at, full, shard, columns, sources
+        self.send, self.recv = send, recv
+
+    def far_x(self, h):
+        return self.at.x if h == 0 else 1 - self.at.x
+
+    def rows(self, m, z, y, x):
+        c0, n = self.columns[m]
+        start = self.at.chip(z, y, x) * self.shard
+        return self.full.at[pl.ds(pl.multiple_of(start, self.shard), self.shard), pl.ds(c0, n)]
+
+    def copy(self, m, h, src, dst, s, r, z, other):
+        i = 2 * m + h
+        return pltpu.make_async_remote_copy(
+            src_ref=src,
+            dst_ref=dst,
+            send_sem=self.send.at[i, s, z],
+            recv_sem=self.recv.at[i, r, z],
+            device_id=other,
+            device_id_type=MESH,
+        )
+
+    def x_copy(self, m):
+        at = self.at
+        c0, n = self.columns[m]
+        src = self.sources[m].at[:, pl.ds(pl.multiple_of((1 - at.x) * n, n), n)]
+        return self.copy(m, 1, src, self.rows(m, at.z, at.y, at.x), 3, 2, at.z, at.across_x())
+
+    def z_in(self, m, h, z):
+        ref = self.rows(m, z, self.at.y, self.far_x(h))
+        return self.copy(m, h, ref, ref, 0, 0, z, self.at.inward())
+
+    def z_out(self, m, h, z):
+        ref = self.rows(m, z, self.at.y, self.far_x(h))
+        return self.copy(m, h, ref, ref, 1, 0, z, self.at.outward())
+
+    def y_copy(self, m, h, z):
+        ref = self.rows(m, z, self.at.y, self.far_x(h))
+        return self.copy(m, h, ref, ref, 2, 1, z, self.at.across_y())
+
+    def line(self, m, h, k):
+        at = self.at
+        z = at.order(k)
+        if k > 0:
+            ref = self.rows(m, z, at.y, self.far_x(h))
+            self.copy(m, h, ref, ref, 0, 0, z, at.inward()).wait_recv()
+        elif h == 1:
+            ref = self.rows(m, z, at.y, self.far_x(h))
+            self.copy(m, h, ref, ref, 0, 2, z, at.across_x()).wait_recv()
+        if k == 0:
+            self.z_in(m, h, z).start()
+        if k == 1:
+
+            @pl.when(at.w == 1)
+            def _():
+                self.z_in(m, h, z).start()
+
+        else:
+
+            @pl.when(at.w == 1)
+            def _():
+                self.z_out(m, h, z).start()
+
+    def cross(self, m, h, k):
+        self.y_copy(m, h, self.at.order(k)).start()
+
+    def finish(self, m):
+        at = self.at
+        for h in range(2):
+            for k in range(4):
+                z = at.order(k)
+                ref = self.rows(m, z, 1 - at.y, self.far_x(h))
+                self.copy(m, h, ref, ref, 2, 1, z, at.across_y()).wait_recv()
+
+    def drain(self, m):
+        at = self.at
+        self.x_copy(m).wait_send()
+        for h in range(2):
+            for k in range(4):
+                z = at.order(k)
+                if k == 0:
+                    self.z_in(m, h, z).wait_send()
+                if k == 1:
+
+                    @pl.when(at.w == 1)
+                    def _(z=z):
+                        self.z_in(m, h, z).wait_send()
+
+                else:
+
+                    @pl.when(at.w == 1)
+                    def _(z=z):
+                        self.z_out(m, h, z).wait_send()
+
+                self.y_copy(m, h, z).wait_send()
+
+
+class PairScatter:
+    def __init__(self, at, full, shard, yf, zl, xs, xr, send, recv):
+        self.at, self.full, self.shard = at, full, shard
+        self.yf, self.zl, self.xs, self.xr, self.send, self.recv = yf, zl, xs, xr, send, recv
+
+    def unit(self, m, z, y):
+        ref, c0, n = self.full(m)
+        size = 2 * self.shard
+        return ref.at[pl.ds(pl.multiple_of((z * 2 + y) * size, size), size), pl.ds(c0, n)]
+
+    def copy(self, m, src, dst, s, r, other):
+        return pltpu.make_async_remote_copy(
+            src_ref=src,
+            dst_ref=dst,
+            send_sem=self.send.at[m, s[0], s[1]],
+            recv_sem=self.recv.at[m, r[0], r[1]],
+            device_id=other,
+            device_id_type=MESH,
+        )
+
+    def y_copy(self, m, z):
+        at = self.at
+        return self.copy(m, self.unit(m, z, 1 - at.y), self.yf.at[m, z], (1, z), (1, z), at.across_y())
+
+    def z_copy(self, m, z, slot, other):
+        return self.copy(m, self.unit(m, z, self.at.y), self.zl.at[m, slot], (0, z), (0, slot), other)
+
+    def x_copy(self, m):
+        return self.copy(m, self.xs.at[m], self.xr.at[m], (2, 0), (2, 0), self.at.across_x())
+
+    def begin(self, m):
+        for k in (3, 2, 1, 0):
+            self.y_copy(m, self.at.order(k)).start()
+
+    def line(self, m, k, out):
+        at = self.at
+        z = at.order(k)
+        self.y_copy(m, z).wait_recv()
+        ref = self.unit(m, z, at.y)
+        if k > 0:
+
+            @pl.when(at.w == 0)
+            def _():
+                ref[...] = ref[...] + self.yf[m, z]
+                self.z_copy(m, z, z, at.inward()).start()
+
+            @pl.when(at.w == 1)
+            def _():
+                self.z_copy(m, z, z, at.inward()).wait_recv()
+                ref[...] = (
+                    ref[...].astype(jnp.float32)
+                    + self.yf[m, z].astype(jnp.float32)
+                    + self.zl[m, z].astype(jnp.float32)
+                ).astype(jnp.bfloat16)
+                if k == 3:
+                    self.z_copy(m, z, z, at.inward()).start()
+                elif k == 2:
+                    self.z_copy(m, z, 4, at.inward()).start()
+                else:
+                    self.z_copy(m, z, 4, at.outward()).start()
+
+        else:
+            self.z_copy(m, z, 4, at.inward()).wait_recv()
+
+            def total(x, second):
+                full, c0, n = self.full(m)
+                size = self.shard
+                own = full[pl.ds(pl.multiple_of(at.chip(z, at.y, x) * size, size), size), pl.ds(c0, n)]
+                part = pl.ds(pl.multiple_of(x * size, size), size)
+                v = (
+                    own.astype(jnp.float32)
+                    + self.yf[m, z, part, :].astype(jnp.float32)
+                    + self.zl[m, 4, part, :].astype(jnp.float32)
+                )
+                if second:
+                    v = v + self.zl[m, z, part, :].astype(jnp.float32)
+                return v
+
+            def put(second):
+                self.xs[m] = total(1 - at.x, second).astype(jnp.bfloat16)
+                self.x_copy(m).start()
+                out(at.x, total(at.x, second))
+
+            @pl.when(at.w == 0)
+            def _():
+                put(False)
+
+            @pl.when(at.w == 1)
+            def _():
+                self.z_copy(m, z, z, at.inward()).wait_recv()
+                put(True)
+
+    def last(self, m, out):
+        self.x_copy(m).wait_recv()
+        out(1 - self.at.x, self.xr[m].astype(jnp.float32))
+
+    def drain(self, m):
+        at = self.at
+        for k in range(4):
+            z = at.order(k)
+            self.y_copy(m, z).wait_send()
+            if k > 0:
+                self.z_copy(m, z, z, at.inward()).wait_send()
+        self.x_copy(m).wait_send()
+
+
+QKV, OUT, UP, DOWN, COLS = 0, 1536, 2048, 3072, 4096
+GATHERED = ((0, 1536), (1536, 2048))
+SCATTERED = ((512, 1536), (0, 512), (1536, 2048))
 BF, F32 = jnp.bfloat16, jnp.float32
 SUMS = ("bq", "bv", "bout", "bdown", "g1", "s1", "g2", "s2", "x", "mid", "res", "branch", "feed")
 BLOCK = 32
-
-
-def pieces_of():
-    out, c = [], 0
-    for n in WIDTHS:
-        out.append((c, c + n))
-        c += n
-    return out
 
 
 def nn(a, b):
@@ -362,48 +560,87 @@
 def block_kernel(
     counts, x_ref, cot_ref, wqkv, wout, wup, wdown, bqv, bout, bup, bdown, g1, s1, g2, s2,
     act_out, gin_out, o_qkv, o_out, o_up, o_down, o_sums,
-    W, G2, xh, yh, xf, yf, zl, rows1, dfeed, qkv, probs, heads, mid, rows2, act, gp, datt, dproj,
-    tall, own_a, own_b, send_a, send_b, got, acc, acc_up, sums, sums_got,
-    sem_in, ag_send, ag_recv, rs_send, rs_recv, pair_send, pair_recv, sums_send, sums_recv,
+    W, G2, G3, xh, yh, xf, yf, zl, yf2, zl2, xs2, xr2,
+    rows1, dfeed, qkv, probs, heads, mid, rows2, act, gp, datt,
+    tall, own_a, own_b, own_c, send_t, send_x, got, got_t, acc, acc_up, sums, sums_got,
+    sem_in, ag_send, ag_recv, pg_send, pg_recv, rs_send, rs_recv, ps_send, ps_recv,
+    pair_send, pair_recv, sums_send, sums_recv,
 ):
     at = Place()
-    t = at.t
+    t, x = at.t, at.x
     shard = wup.shape[0]
-    pieces = pieces_of()
-    n_pieces = len(pieces)
     own = x_ref.shape[0]
-    group = 2 * own
     width = x_ref.shape[1]
-    mine = at_rows(t * own, own)
-    dbr = dfeed
-    theirs = at_rows((1 - t) * own, own)
+    dbr = dfeed.at[0 : 2 * own, :]
+    dproj = qkv
+
+    def spot(far_x, far_t):
+        return at_rows((far_x * 2 + far_t) * own, own)
+
+    mine, theirs = at_rows(t * own, own), at_rows((1 - t) * own, own)
 
     here = at_rows(at.dp * shard, shard)
+    quarter = pl.ds(pl.multiple_of(x * 1024, 1024), 1024)
     loads = [
         pltpu.make_async_copy(src, W.at[here, pl.ds(c0, n)], sem_in.at[i])
         for i, (src, c0, n) in enumerate(
             [(wqkv.at[j], QKV + 512 * j, 512) for j in range(3)]
-            + [(wout, OUT, 512), (wup, UP, 2048), (wdown, DOWN, 2048)]
+            + [(wout, OUT, 512), (wup.at[:, quarter], UP, 1024), (wdown.at[:, quarter], DOWN, 1024)]
         )
     ]
     for c in loads:
         c.start()
     enter(at)
-    g = Gather(at, W, shard, pieces, ag_send, ag_recv)
+    g = Gather(at, W, shard, GATHERED, ag_send, ag_recv)
+    pg = PairGather(at, W, shard, ((UP, 1024), (DOWN, 1024)), (wup, wdown), pg_send, pg_recv)
     for c in loads:
         c.wait()
     g.line(0, 0)
 
     steps = []
-    for p in range(n_pieces):
+    ends = {}
+
+    def plan(f, *a):
+        steps.append(lambda: f(*a))
+
+    def attention_step(p, k):
+        if k < 3:
+            plan(g.line, p, k + 1)
+        plan(g.plane, p, k)
+
+    attention_step(0, 0)
+    plan(pg.x_copy(0).start)
+    plan(pg.line, 0, 0, 0)
+    attention_step(0, 1)
+    plan(g.line, 1, 0)
+    attention_step(0, 2)
+    plan(pg.line, 0, 0, 1)
+    attention_step(0, 3)
+    plan(pg.line, 0, 1, 0)
+    plan(pg.x_copy(1).start)
+    ends["qkv"] = len(steps)
+    for k in range(4):
+        attention_step(1, k)
+        if k < 2:
+            plan(pg.line, 0, 0, k + 2)
+        else:
+            plan(pg.line, 0, 1, k - 1)
+    ends["out"] = len(steps)
+    for k in range(4):
+        plan(pg.cross, 0, 0, k)
+    plan(pg.line, 0, 1, 3)
+    plan(pg.line, 1, 0, 0)
+    plan(pg.line, 1, 1, 0)
+    for k in range(4):
+        plan(pg.cross, 0, 1, k)
+    for h in range(2):
+        for k in range(1, 4):
+            plan(pg.line, 1, h, k)
         for k in range(4):
-            def step(p=p, k=k):
-                if k < 3:
-                    g.line(p, k + 1)
-                g.plane(p, k)
-                if k == 1 and p + 1 < n_pieces:
-                    g.line(p + 1, 0)
-            steps.append(step)
+            plan(pg.cross, 1, h, k)
+        if h == 0:
+            ends["up"] = len(steps)
+    ends["down"] = len(steps)
     done = [0]
 
     def gather(n):
@@ -412,25 +649,36 @@
             done[0] += 1
             n -= 1
 
-    def need(p):
-        gather(4 * p + 5 - done[0])
-        g.finish(p)
-
-    home = {0: (W, UP, UP + 1536), 1: (W, UP + 1536, DOWN), 2: (W, DOWN, DOWN + 1024), 3: (W, DOWN + 1024, DOWN + 2048),
-            4: (G2, 0, 1024), 5: (G2, 1024, 2048)}
-    sc = Scatter(at, lambda p: home[p], shard, pieces, xh, yh, xf, yf, zl, rs_send, rs_recv)
+    def need(name):
+        gather(ends[name] - done[0])
+        if name == "qkv":
+            g.finish(0)
+        elif name == "out":
+            g.finish(1)
+        else:
+            pg.finish(0 if name == "up" else 1)
+
+    home = {0: (W, DOWN, DOWN + 1024), 1: (G3, 0, 512), 2: (G3, 512, 1024)}
+    sc = Scatter(at, lambda p: home[p], shard, SCATTERED, xh, yh, xf, yf, zl, rs_send, rs_recv)
+    home_pair = {0: (W, UP, 1024), 1: (G2, 0, 1024)}
+    ps = PairScatter(at, lambda m: home_pair[m], shard, yf2, zl2, xs2, xr2, ps_send, ps_recv)
 
     def write(p):
         def store(total):
             if p == 0:
-                for j in range(3):
-                    o_qkv[j] = total[:, 512 * j : 512 * (j + 1)]
+                o_qkv[1] = total[:, :512]
+                o_qkv[2] = total[:, 512:]
             elif p == 1:
+                o_qkv[0] = total
+            else:
                 o_out[...] = total
-            elif p < 4:
-                o_up[:, (p - 2) * 1024 : (p - 1) * 1024] = total
-            else:
-                o_down[:, (p - 4) * 1024 : (p - 3) * 1024] = total
+        return store
+
+    def write_pair(m):
+        ref = o_up if m == 0 else o_down
+
+        def store(far_x, total):
+            ref[:, pl.ds(pl.multiple_of(far_x * 1024, 1024), 1024)] = total
         return store
 
     queue = []
@@ -442,24 +690,29 @@
         for k in (3, 2, 1, 0):
             queue.append(lambda p=p, k=k: sc.line(p, k, write(p)))
 
+    def reduce_pair(m):
+        ps.begin(m)
+        for k in (3, 2, 1, 0):
+            queue.append(lambda m=m, k=k: ps.line(m, k, write_pair(m)))
+
     def scatter(n):
         while n > 0 and queue:
             queue.pop(0)()
             n -= 1
 
-    def pair(i, src, dst):
+    def send(i, src, dst, other):
         return pltpu.make_async_remote_copy(
             src_ref=src, dst_ref=dst, send_sem=pair_send.at[i], recv_sem=pair_recv.at[i],
-            device_id=at.twin(), device_id_type=MESH,
+            device_id=other, device_id_type=MESH,
         )
 
-    def share(i, ref):
-        c = pair(i, ref.at[mine, :], ref.at[mine, :])
+    def share(i, ref, r, other):
+        c = send(i, ref.at[r, :], ref.at[r, :], other)
         c.start()
         return c
 
-    def take(i, ref):
-        pair(i, ref.at[theirs, :], ref.at[theirs, :]).wait_recv()
+    def take(i, ref, r):
+        send(i, ref.at[r, :], ref.at[r, :], at.twin()).wait_recv()
 
     for ref in (acc, acc_up):
         ref[...] = jnp.zeros_like(ref)
@@ -487,7 +740,7 @@
 
     def flip(src):
         def body(c):
-            tall[pl.ds(c, 128), :] = src[:, pl.ds(c, 128)].T
+            tall[pl.ds(c, 128), 0 : src.shape[0]] = src[:, pl.ds(c, 128)].T
         tiles(0, src.shape[1], body, 128)
 
     def first_norm(b, r):
@@ -498,17 +751,15 @@
         rows1[mine_b, :] = (n * g1[...] + s1[...]).astype(BF)
         add("x", keep * xv * xv)
         low = (cot_ref[r, :].astype(F32) * keep).astype(BF)
-        dfeed[mine_b, :] = low
+        dfeed[pl.ds(pl.multiple_of((x * 2 + t) * own + b, BLOCK), BLOCK), :] = low
         add("bdown", low.astype(F32))
 
     each_block(first_norm)
-    shares = [share(0, rows1), share(1, dfeed)]
-    gather(1)
-    take(1, dfeed)
-    flip(dfeed)
-    gather(1)
-    take(0, rows1)
-    need(0)
+    shares = [share(0, rows1, mine, at.twin()), share(1, dfeed, spot(x, t), at.twin())]
+    gather(3)
+    take(0, rows1, theirs)
+    need("qkv")
+    shares.append(share(2, dfeed, spot(x, t), at.across_x()))
 
     def project(c):
         v = nn(rows1[...], W[:, pl.ds(c, 256)])
@@ -549,22 +800,22 @@
 
     for i in range(4):
         attend_some(2 * i, 2 * i + 2, attend)
-        gather(1)
-    need(1)
-
-    def reduced(i, src, cols, k, keep, send):
+        gather(3)
+    need("out")
+
+    def reduced(i, src, cols, keep):
         def other(c):
-            send[:, pl.ds(c, 256)] = nt(src[theirs, :], W[pl.ds(c, 256), cols]).astype(BF)
+            send_t[0, :, pl.ds(c, 256)] = nt(src[theirs, :], W[pl.ds(c, 256), cols]).astype(BF)
         tiles(0, width, other)
-        copy = pair(i, send, got.at[k])
+        copy = send(i, send_t.at[0], got.at[0 if i == 3 else 1], at.twin())
         copy.start()
         def self(c):
             keep[:, pl.ds(c, 256)] = nt(src[mine, :], W[pl.ds(c, 256), cols])
         tiles(0, width, self)
         return copy
 
-    branch_copy = reduced(2, heads, pl.ds(OUT, 512), 0, own_a, send_a)
-    gather(1)
+    branch_copy = reduced(3, heads, pl.ds(OUT, 512), own_a)
+    gather(2)
     branch_copy.wait()
 
     def second_norm(b, r):
@@ -575,60 +826,130 @@
         add("branch", keep * branch * branch)
         add("mid", keep * m * m)
         n, _ = normed(m)
-        rows2[pl.ds(pl.multiple_of(t * own + b, BLOCK), BLOCK), :] = (n * g2[...] + s2[...]).astype(BF)
+        rows2[pl.ds(pl.multiple_of((x * 2 + t) * own + b, BLOCK), BLOCK), :] = (n * g2[...] + s2[...]).astype(BF)
 
     each_block(second_norm)
-    shares.append(share(3, rows2))
+    shares.append(share(4, rows2, spot(x, t), at.across_x()))
+    shares.append(share(5, rows2, spot(x, t), at.twin()))
     gather(1)
-    take(3, rows2)
-
-    def hidden(c):
-        u = nn(rows2[...], W[:, pl.ds(UP + c, 256)]) + bup[:, pl.ds(pl.multiple_of(t * 2048 + c, 256), 256)]
-        below = 0.5 * (1.0 + lax.erf(u * (0.5**0.5)))
-        dense = jnp.exp(-0.5 * u * u) * 0.3989422804014327
-        act[:, pl.ds(c, 256)] = (u * below).astype(BF)
-        gp[:, pl.ds(c, 256)] = (below + u * dense).astype(BF)
+
+    take(2, dfeed, spot(1 - x, t))
+    shares.append(share(6, dfeed, spot(1 - x, t), at.twin()))
+    take(1, dfeed, spot(x, 1 - t))
+    take(6, dfeed, spot(1 - x, 1 - t))
+    flip(dfeed)
+    take(5, rows2, spot(x, 1 - t))
+
+    chip_rows = lambda far_x: at_rows(far_x * 2 * own, 2 * own)
+
+    def hidden(far_x):
+        r = chip_rows(far_x)
+
+        def body(c):
+            lanes = pl.ds(pl.multiple_of(t * 2048 + x * 1024 + c, 256), 256)
+            u = nn(rows2[r, :], W[:, pl.ds(UP + c, 256)]) + bup[:, lanes]
+            below = 0.5 * (1.0 + lax.erf(u * (0.5**0.5)))
+            dense = jnp.exp(-0.5 * u * u) * 0.3989422804014327
+            act[r, pl.ds(c, 256)] = (u * below).astype(BF)
+            gp[r, pl.ds(c, 256)] = (below + u * dense).astype(BF)
+        tiles(0, 1024, body)
 
     def grad_down(c):
         G2[:, pl.ds(c, 256)] = nn(tall[...], act[:, pl.ds(c, 256)]).astype(BF)
 
-    need(2)
-    tiles(0, 1024, hidden)
-    gather(1)
+    need("up")
+    hidden(x)
+    gather(2)
+    take(4, rows2, spot(1 - x, t))
+    shares.append(share(7, rows2, spot(1 - x, t), at.twin()))
+    take(7, rows2, spot(1 - x, 1 - t))
+    hidden(1 - x)
+    gather(2)
     tiles(0, 1024, grad_down)
-    need(3)
-    tiles(1024, 2048, hidden)
-    gather(1)
-    tiles(1024, 2048, grad_down)
     flip(rows2)
-    reduce_begin(4)
-
-    def back_act(c):
-        d = nn(dfeed[...], W[:, pl.ds(DOWN + c, 256)])
-        low = (d * gp[:, pl.ds(c, 256)].astype(F32)).astype(BF)
-        gp[:, pl.ds(c, 256)] = low
-        acc_up[t, :, pl.ds(c, 256)] += fold(low.astype(F32))
-
-    need(4)
-    tiles(0, 1024, back_act)
-    gather(9)
-    reduce_begin(5)
-    need(5)
-    tiles(1024, 2048, back_act)
-    two_copy = reduced(4, gp, pl.ds(UP, 2048), 1, own_a, send_a)
-    feed_copy = reduced(5, act, pl.ds(DOWN, 2048), 2, own_b, send_b)
-    for p in range(n_pieces):
+    gather(100)
+    reduce_pair(1)
+
+    def back_act(far_x):
+        r = chip_rows(far_x)
+
+        def body(c):
+            d = nn(dfeed[r, :], W[:, pl.ds(DOWN + c, 256)])
+            low = (d * gp[r, pl.ds(c, 256)].astype(F32)).astype(BF)
+            gp[r, pl.ds(c, 256)] = low
+            acc_up[t * 2 + x, :, pl.ds(c, 256)] += fold(low.astype(F32))
+        tiles(0, 1024, body)
+
+    def product(src, r, cols, put):
+        def body(c):
+            put(pl.ds(c, 256), nt(src[r, :], W[pl.ds(c, 256), cols]))
+        tiles(0, width, body)
+
+    class Sum4:
+        def __init__(self, i, n, src, cols, keep):
+            self.i, self.n, self.src, self.cols, self.keep = i, n, src, cols, keep
+
+        def away(self, far_x, slot):
+            def put(c, v):
+                send_t[slot, :, c] = v.astype(BF)
+            product(self.src, spot(far_x, 1 - t), self.cols, put)
+            copy = send(self.i + slot, send_t.at[slot], got_t.at[self.n, slot], at.twin())
+            copy.start()
+            return copy
+
+        def far(self):
+            first = self.away(1 - x, 0)
+
+            def put(c, v):
+                own_b[:, c] = v
+            product(self.src, spot(1 - x, t), self.cols, put)
+            first.wait()
+
+            def body(b, r):
+                send_x[self.n, r, :] = (own_b[r, :] + got_t[self.n, 0, r, :].astype(F32)).astype(BF)
+            each_block(body)
+            self.cross = send(self.i + 2, send_x.at[self.n], got.at[2 + self.n], at.across_x())
+            self.cross.start()
+
+        def near(self):
+            second = self.away(x, 1)
+
+            def put(c, v):
+                self.keep[:, c] = v
+            product(self.src, spot(x, t), self.cols, put)
+            second.wait()
+
+        def value(self, r):
+            return self.keep[r, :] + got_t[self.n, 1, r, :].astype(F32) + got[2 + self.n, r, :].astype(F32)
+
+    need("down")
+    back_act(1 - x)
+    two = Sum4(8, 0, gp, pl.ds(UP, 1024), own_a)
+    two.far()
+    scatter(1)
+    back_act(x)
+    two.near()
+    for p in range(2):
         g.drain(p)
-    scatter(2)
+        pg.drain(p)
+    scatter(1)
 
     def grad_up(c):
-        W[:, pl.ds(DOWN + c, 256)] = nn(tall[...], gp[:, pl.ds(c, 256)]).astype(BF)
-
-    two_copy.wait()
-    shares[1].wait_send()
+        W[:, pl.ds(UP + c, 256)] = nn(tall[...], gp[:, pl.ds(c, 256)]).astype(BF)
+
+    tiles(0, 1024, grad_up)
+    reduce_pair(0)
+    scatter(1)
+    four = Sum4(11, 1, act, pl.ds(DOWN, 1024), own_c)
+    four.far()
+    scatter(1)
+    four.near()
+    two.cross.wait()
+    for i in (1, 2, 5):
+        shares[i].wait_send()
 
     def second_back(b, r):
-        dy = own_a[r, :] + got[1, r, :].astype(F32)
+        dy = two.value(r)
         n, scale = normed(mid[r, :])
         keep = valid_of(t, b, BLOCK).astype(F32)
         add("g2", dy * n)
@@ -640,27 +961,23 @@
         add("bout", low.astype(F32))
 
     each_block(second_back)
-    shares.append(share(6, dbr))
-    tiles(0, 1024, grad_up)
+    shares.append(share(14, dbr, mine, at.twin()))
+    scatter(1)
+    take(14, dbr, theirs)
+
+    def back_heads(c):
+        datt[:, pl.ds(c, 256)] = nn(dbr[...], W[:, pl.ds(OUT + c, 256)]).astype(BF)
+
+    tiles(0, 512, back_heads)
+    flip(dbr)
+    short = pl.ds(0, 2 * own)
+
+    def grad_out(c):
+        G3[:, pl.ds(512 + c, 256)] = nn(tall[:, short], heads[:, pl.ds(c, 256)]).astype(BF)
+
+    tiles(0, 512, grad_out)
     reduce_begin(2)
     scatter(2)
-    tiles(1024, 2048, grad_up)
-    reduce_begin(3)
-    scatter(2)
-    take(6, dbr)
-
-    def back_heads(c):
-        datt[:, pl.ds(c, 256)] = nn(dbr[...], W[:, pl.ds(OUT + c, 256)]).astype(BF)
-
-    tiles(0, 512, back_heads)
-    flip(dbr)
-
-    def grad_out(c):
-        W[:, pl.ds(UP + 1536 + c, 256)] = nn(tall[...], heads[:, pl.ds(c, 256)]).astype(BF)
-
-    tiles(0, 512, grad_out)
-    reduce_begin(1)
-    scatter(4)
 
     def attend_back(it):
         image, j = it // 4, it % 4
@@ -694,20 +1011,25 @@
 
     for i in range(4):
         attend_some(2 * i, 2 * i + 2, attend_back)
-        scatter(4)
-
-    one_copy = reduced(7, dproj, pl.ds(QKV, 1536), 3, own_a, send_a)
+        scatter(3)
+
+    one_copy = reduced(15, dproj, pl.ds(QKV, 1536), own_a)
     flip(rows1)
 
-    def grad_qkv(c):
-        W[:, pl.ds(UP + c, 256)] = nn(tall[...], dproj[:, pl.ds(c, 256)]).astype(BF)
-
-    tiles(0, 1536, grad_qkv)
+    def grad_kv(c):
+        W[:, pl.ds(DOWN + c, 256)] = nn(tall[:, short], dproj[:, pl.ds(512 + c, 256)]).astype(BF)
+
+    def grad_q(c):
+        G3[:, pl.ds(c, 256)] = nn(tall[:, short], dproj[:, pl.ds(c, 256)]).astype(BF)
+
+    tiles(0, 1024, grad_kv)
     reduce_begin(0)
+    tiles(0, 512, grad_q)
+    reduce_begin(1)
     one_copy.wait()
 
     def first_back(b, r):
-        dy = own_a[r, :] + got[3, r, :].astype(F32)
+        dy = own_a[r, :] + got[1, r, :].astype(F32)
         n, scale = normed(x_ref[r, :].astype(F32))
         add("g1", dy * n)
         add("s1", dy)
@@ -715,11 +1037,11 @@
 
     each_block(first_back)
     scatter(4)
-    feed_copy.wait()
+    four.cross.wait()
 
     def finish_feed(b, r):
         keep = valid_of(t, b, BLOCK).astype(F32)
-        feed = own_b[r, :] + got[2, r, :].astype(F32) + bdown[...]
+        feed = four.value(r) + bdown[...]
         res = mid[r, :] + feed
         add("feed", keep * feed * feed)
         add("res", keep * res * res)
@@ -730,7 +1052,7 @@
     for i in range(8):
         sums[i : i + 1, :] = jnp.sum(acc[i], axis=0, keepdims=True)
     for i in range(4):
-        sums[8 + i : 9 + i, :] = jnp.sum(acc_up[i // 2, :, (i % 2) * 1024 : (i % 2 + 1) * 1024], axis=0, keepdims=True)
+        sums[8 + i : 9 + i, :] = jnp.sum(acc_up[i], axis=0, keepdims=True)
     lane = lax.broadcasted_iota(jnp.int32, (1, width), 1)
     row = jnp.where(lane == 5, (counts[t] + BUFFER).astype(F32), 0.0)
     for i, name in enumerate(("x", "mid", "res", "branch", "feed")):
@@ -748,17 +1070,18 @@
         sums[...] += sums_got[i]
     o_sums[...] = sums[...]
     scatter(1000)
-    for p in range(n_pieces):
+    for m in (1, 0):
+        ps.last(m, write_pair(m))
+        ps.drain(m)
+    for p in range(3):
         sc.drain(p)
-    for i in (0, 2, 3):
+    for i in (0, 3, 4, 6, 7):
         shares[i].wait_send()
 
 
 def block(counts, stream, cotangent, w_qkv, w_out_t, w_up, w_down_t, b_qv, b_out, b_up, b_down, g1, s1, g2, s2):
     own, width = stream.shape
     shard = w_up.shape[0]
-    n = len(WIDTHS)
-    cols = sum(WIDTHS)
     rows = 16 * shard
     group = 2 * own
     vmem = pl.BlockSpec(memory_space=pltpu.VMEM)
@@ -779,41 +1102,51 @@
         in_specs=[pl.BlockSpec(memory_space=pltpu.SMEM), vmem, vmem, hbm, hbm, hbm, hbm] + [vmem] * 8,
         out_specs=(vmem,) * 7,
         scratch_shapes=[
-            pltpu.VMEM((rows, cols), BF),
-            pltpu.VMEM((rows, 2048), BF),
-            pltpu.VMEM((4, shard // 2, cols), BF),
-            pltpu.VMEM((4, shard // 2, cols), BF),
-            pltpu.VMEM((4, shard, cols), BF),
-            pltpu.VMEM((4, shard, cols), BF),
-            pltpu.VMEM((5, shard, cols), BF),
+            pltpu.VMEM((rows, COLS), BF),
+            pltpu.VMEM((rows, 1024), BF),
+            pltpu.VMEM((rows, 1024), BF),
+            pltpu.VMEM((4, shard // 2, 2048), BF),
+            pltpu.VMEM((4, shard // 2, 2048), BF),
+            pltpu.VMEM((4, shard, 2048), BF),
+            pltpu.VMEM((4, shard, 2048), BF),
+            pltpu.VMEM((5, shard, 2048), BF),
+            pltpu.VMEM((2, 4, 2 * shard, 1024), BF),
+            pltpu.VMEM((2, 5, 2 * shard, 1024), BF),
+            pltpu.VMEM((2, shard, 1024), BF),
+            pltpu.VMEM((2, shard, 1024), BF),
             pltpu.VMEM((group, width), BF),
-            pltpu.VMEM((group, width), BF),
+            pltpu.VMEM((2 * group, width), BF),
             pltpu.VMEM((group, 1536), BF),
             pltpu.VMEM((16, own, own), BF),
             pltpu.VMEM((group, 512), BF),
             pltpu.VMEM((own, width), F32),
-            pltpu.VMEM((group, width), BF),
-            pltpu.VMEM((group, 2048), BF),
-            pltpu.VMEM((group, 2048), BF),
+            pltpu.VMEM((2 * group, width), BF),
+            pltpu.VMEM((2 * group, 1024), BF),
+            pltpu.VMEM((2 * group, 1024), BF),
             pltpu.VMEM((group, 512), BF),
-            pltpu.VMEM((group, 1536), BF),
-            pltpu.VMEM((width, group), BF),
+            pltpu.VMEM((width, 2 * group), BF),
             pltpu.VMEM((own, width), F32),
             pltpu.VMEM((own, width), F32),
-            pltpu.VMEM((own, width), BF),
-            pltpu.VMEM((own, width), BF),
+            pltpu.VMEM((own, width), F32),
+            pltpu.VMEM((2, own, width), BF),
+            pltpu.VMEM((2, own, width), BF),
             pltpu.VMEM((4, own, width), BF),
+            pltpu.VMEM((2, 2, own, width), BF),
             pltpu.VMEM((len(SUMS), 8, width), F32),
-            pltpu.VMEM((2, 8, 2048), F32),
+            pltpu.VMEM((4, 8, 1024), F32),
             pltpu.VMEM((16, width), F32),
             pltpu.VMEM((5, 16, width), F32),
             dma((6,)),
-            dma((n, 6, 4)),
-            dma((n, 5, 4)),
-            dma((n, 5, 4)),
-            dma((n, 5, 5)),
-            dma((8,)),
-            dma((8,)),
+            dma((2, 6, 4)),
+            dma((2, 5, 4)),
+            dma((4, 4, 4)),
+            dma((4, 3, 4)),
+            dma((3, 5, 4)),
+            dma((3, 5, 5)),
+            dma((2, 3, 4)),
+            dma((2, 3, 5)),
+            dma((16,)),
+            dma((16,)),
             dma((5,)),
             dma((5,)),
         ],

time: 280 us -> 262 us (0.936)
  Pallas kernels: 266 us -> 248 us
    pallas_call x1, Pallas kernels: 266 us -> 248 us  [block(): pl.pallas_call(block_kernel, out_shape=(jax.ShapeDtypeStruct((own, width)...]
where the time goes in v3:
time: 262 us; the launch traced here: 261 us
  Pallas kernels  248 us (95%)
  local copies, waits for them, and re-layouts  10.8 us (4%)
    pallas_call x1, Pallas kernels, block(): pl.pallas_call(block_kernel, out_shape=(jax.ShapeDtypeStruct((own, width)...  248 us
    unnamed x18, local copies, waits for them, and re-layouts  6.93 us

profile of v3, /device:TPU:0, one launch (start us, length us, event | category | flops | bytes accessed | tf_op | source)
XLA Modules:
  0.0 261.2 jit_solution(2701866154889611840)
XLA Ops:
  0.7 247.8 %shard_map.262 = (bf16[320,1024]{1,0:T(8,128)(2,1)}, f32[320,1024]{1,0:T(8,128)}, f32[3,64,512]{2,1,0:T(8,128)}, f32[64,512]{1,0:T(8,128)}, f32[64,2048]{1,0:T(8...) custom-call(s32[2]{0:T(128)} %counts.1, bf16[320,1024]{1,0:T(8,128)(2,1)} %x_ref.1, bf16[320,1024]{1,0:T(8,128)(2,1)} %cot_ref.1, ...), custom_call_target="tpu_custom_call" | custom-call | tf_op jit(solution)/shard_map/pallas_call | solution.py:1091
  248.5 0.0 copy-start
  248.5 1.4 slice.43
  250.5 1.2 sqrt_bitcast_fusion
  251.8 0.8 slice_bitcast_fusion
  252.5 0.8 slice.33
  253.3 0.1 constant_dynamic-slice_fusion
  253.3 0.6 dynamic_slice.7
  253.9 0.6 slice.34
  254.5 0.5 slice_bitcast_fusion.1
  255.0 2.0 copy.39
  257.0 0.0 copy-done
  257.0 0.0 copy-start.3
  257.0 0.0 copy-start.4
  257.0 0.0 copy-start.2
  257.0 1.1 copy.40
  258.1 0.1 copy-done.3
  258.2 0.0 copy-start.1
  258.2 0.7 copy.41
  259.0 0.0 copy-done.4
  259.0 0.7 copy.42
  259.6 0.0 copy-done.2
  259.6 0.8 copy.43
  260.4 0.0 copy-done.1
  260.4 0.8 copy.44
  (1 shorter events, 0.0 us)
Async XLA Ops:
  248.5 8.5 %copy-start = (f32[320,1024]{1,0:T(8,128)S(1)}, f32[320,1024]{1,0:T(8,128)}, u32[]{:S(2)}) copy-start(f32[320,1024]{1,0:T(8,128)} %get-tuple-element.51) | copy-start | bytes 3932164
  257.0 1.2 copy-start.3
  257.0 2.0 copy-start.4
  257.0 2.6 %copy-start.2 = (f32[64,2048]{1,0:T(8,128)S(1)}, f32[64,2048]{1,0:T(8,128)}, u32[]{:S(2)}) copy-start(f32[64,2048]{1,0:T(8,128)} %get-tuple-element.56) | copy-start | bytes 1572868
  258.2 2.2 copy-start.1

commit v4 on v3

--- a/solution.py
+++ b/solution.py
@@ -241,11 +241,10 @@
             p, self.rows(p, z, at.y, at.x), self.zl.at[slot, :, self.cols(p)], (0, z), (0, slot), at.outward()
         )
 
-    def begin(self, p):
-        for k in (3, 2, 1, 0):
-            z = self.at.order(k)
-            self.x_half(p, z).start()
-            self.y_half(p, z).start()
+    def begin(self, p, k):
+        z = self.at.order(k)
+        self.x_half(p, z).start()
+        self.y_half(p, z).start()
 
     def plane(self, p, k):
         at = self.at
@@ -443,9 +442,8 @@
     def x_copy(self, m):
         return self.copy(m, self.xs.at[m], self.xr.at[m], (2, 0), (2, 0), self.at.across_x())
 
-    def begin(self, m):
-        for k in (3, 2, 1, 0):
-            self.y_copy(m, self.at.order(k)).start()
+    def begin(self, m, k):
+        self.y_copy(m, self.at.order(k)).start()
 
     def line(self, m, k, out):
         at = self.at
@@ -520,8 +518,101 @@
 
 
 QKV, OUT, UP, DOWN, COLS = 0, 1536, 2048, 3072, 4096
-GATHERED = ((0, 1536), (1536, 2048))
-SCATTERED = ((512, 1536), (0, 512), (1536, 2048))
+GATHERED = ((0, 512), (512, 1024), (1024, 1536), (1536, 2048))
+SCATTERED = ((0, 512), (512, 1024), (1024, 1536), (1536, 2048))
+GATHER_PLAN = (
+    ((0, 2, 0), (0, 1, 0), (0, 0, 0), (0, 3, 0), (0, 0, 1), (1, 0, 0), (0, 1, 1), (0, 1, 2), (1, 1, 0), (3, 0, 0, 0), (0, 2, 1), (0, 2, 2), (1, 1, 1), (0, 0, 2), (0, 1, 3), (3, 0, 0, 1), (0, 3, 1), (0, 2, 3), (1, 1, 2), (1, 0, 1), (3, 0, 0, 2), (0, 0, 3), (1, 2, 0), (3, 1, 0, 0), (1, 2, 1), (1, 2, 2),),
+    ((1, 0, 2), (1, 1, 3), (3, 0, 0, 3), (1, 0, 3), (1, 2, 3), (0, 3, 2), (0, 3, 3), (1, 3, 0), (2, 0), (2, 1), (4, 1, 0, 0), (3, 1, 0, 1),),
+    (),
+    ((4, 0, 0, 0),),
+    (),
+    (),
+    (),
+    ((1, 3, 1), (1, 3, 2), (1, 3, 3), (4, 0, 0, 1), (5,),),
+    ((3, 0, 1, 0),),
+    (),
+    (),
+    (),
+    ((3, 1, 0, 2), (3, 1, 1, 0), (4, 0, 1, 0),),
+    (),
+    ((4, 1, 1, 0), (3, 0, 1, 1), (4, 0, 0, 2), (4, 0, 1, 1),),
+    (),
+    (),
+    (),
+    ((4, 0, 0, 3),),
+    ((3, 0, 1, 2),),
+    (),
+    (),
+    ((4, 0, 1, 2), (3, 0, 1, 3), (4, 0, 1, 3), (3, 1, 1, 1), (3, 1, 1, 2), (4, 1, 1, 1), (4, 1, 1, 2), (4, 1, 0, 1), (3, 1, 1, 3),),
+    (),
+    ((3, 1, 0, 3), (4, 1, 0, 2),),
+    (),
+    (),
+    ((4, 1, 1, 3),),
+    (),
+    (),
+    (),
+    (),
+    (),
+    ((4, 1, 0, 3),),
+)
+SCATTER_PLAN = (
+    (),
+    (),
+    (),
+    ((3, 1, 3),),
+    (),
+    (),
+    (),
+    ((3, 1, 2), (3, 1, 1),),
+    ((4, 1, 3),),
+    (),
+    (),
+    ((3, 1, 0), (4, 1, 2),),
+    (),
+    ((4, 1, 1),),
+    ((3, 0, 3),),
+    (),
+    (),
+    ((3, 0, 2),),
+    (),
+    (),
+    (),
+    (),
+    (),
+    ((3, 0, 1), (0, 3, 3),),
+    (),
+    (),
+    ((4, 1, 0),),
+    ((0, 3, 2),),
+    ((3, 0, 0), (0, 3, 1), (0, 3, 0),),
+    (),
+    ((1, 3, 3),),
+    (),
+    ((1, 3, 2),),
+    (),
+    (),
+    (),
+    (),
+    ((0, 2, 3), (0, 1, 3), (4, 0, 3), (0, 2, 2), (1, 3, 1),),
+    (),
+    ((0, 0, 3), (0, 2, 1), (1, 1, 3),),
+    ((0, 2, 0), (1, 0, 3), (1, 3, 0), (2, 3, 3), (0, 1, 2), (0, 0, 2), (1, 2, 3), (4, 0, 2), (0, 0, 1), (1, 2, 2), (4, 0, 1),),
+    ((0, 1, 1),),
+    ((1, 0, 2),),
+    (),
+    (),
+    ((1, 0, 1), (2, 2, 3), (1, 1, 2), (1, 1, 1), (0, 0, 0), (2, 3, 2), (0, 1, 0),),
+    ((2, 0, 3),),
+    ((1, 2, 1), (2, 1, 3),),
+    (),
+    ((4, 0, 0), (2, 3, 1), (1, 1, 0), (2, 1, 2),),
+    (),
+    ((1, 2, 0), (2, 2, 2), (2, 1, 1), (2, 2, 1), (5, 1), (1, 0, 0),),
+    (),
+    ((5, 0), (2, 0, 2), (2, 0, 1), (2, 3, 0), (2, 2, 0), (2, 1, 0),),
+    ((2, 0, 0),),
+)
 BF, F32 = jnp.bfloat16, jnp.float32
 SUMS = ("bq", "bv", "bout", "bdown", "g1", "s1", "g2", "s2", "x", "mid", "res", "branch", "feed")
 BLOCK = 32
@@ -562,7 +653,7 @@
     act_out, gin_out, o_qkv, o_out, o_up, o_down, o_sums,
     W, G2, G3, xh, yh, xf, yf, zl, yf2, zl2, xs2, xr2,
     rows1, dfeed, qkv, probs, heads, mid, rows2, act, gp, datt,
-    tall, own_a, own_b, own_c, send_t, send_x, got, got_t, acc, acc_up, sums, sums_got,
+    tall, own_a, own_c, send_t, send_x, got, got_t, acc, acc_up, sums, sums_got,
     sem_in, ag_send, ag_recv, pg_send, pg_recv, rs_send, rs_recv, ps_send, ps_recv,
     pair_send, pair_recv, sums_send, sums_recv,
 ):
@@ -595,81 +686,37 @@
     pg = PairGather(at, W, shard, ((UP, 1024), (DOWN, 1024)), (wup, wdown), pg_send, pg_recv)
     for c in loads:
         c.wait()
-    g.line(0, 0)
-
-    steps = []
-    ends = {}
-
-    def plan(f, *a):
-        steps.append(lambda: f(*a))
-
-    def attention_step(p, k):
-        if k < 3:
-            plan(g.line, p, k + 1)
-        plan(g.plane, p, k)
-
-    attention_step(0, 0)
-    plan(pg.x_copy(0).start)
-    plan(pg.line, 0, 0, 0)
-    attention_step(0, 1)
-    plan(g.line, 1, 0)
-    attention_step(0, 2)
-    plan(pg.line, 0, 0, 1)
-    attention_step(0, 3)
-    plan(pg.line, 0, 1, 0)
-    plan(pg.x_copy(1).start)
-    ends["qkv"] = len(steps)
-    for k in range(4):
-        attention_step(1, k)
-        if k < 2:
-            plan(pg.line, 0, 0, k + 2)
+
+    def gather_step(kind, *a):
+        if kind == 0:
+            g.line(*a)
+        elif kind == 1:
+            g.plane(*a)
+        elif kind == 2:
+            pg.x_copy(*a).start()
+        elif kind == 3:
+            pg.line(*a)
+        elif kind == 4:
+            pg.cross(*a)
         else:
-            plan(pg.line, 0, 1, k - 1)
-    ends["out"] = len(steps)
-    for k in range(4):
-        plan(pg.cross, 0, 0, k)
-    plan(pg.line, 0, 1, 3)
-    plan(pg.line, 1, 0, 0)
-    plan(pg.line, 1, 1, 0)
-    for k in range(4):
-        plan(pg.cross, 0, 1, k)
-    for h in range(2):
-        for k in range(1, 4):
-            plan(pg.line, 1, h, k)
-        for k in range(4):
-            plan(pg.cross, 1, h, k)
-        if h == 0:
-            ends["up"] = len(steps)
-    ends["down"] = len(steps)
-    done = [0]
-
-    def gather(n):
-        while n > 0 and done[0] < len(steps):
-            steps[done[0]]()
-            done[0] += 1
-            n -= 1
-
-    def need(name):
-        gather(ends[name] - done[0])
-        if name == "qkv":
-            g.finish(0)
-        elif name == "out":
-            g.finish(1)
-        else:
-            pg.finish(0 if name == "up" else 1)
-
-    home = {0: (W, DOWN, DOWN + 1024), 1: (G3, 0, 512), 2: (G3, 512, 1024)}
+            shares.append(share(2, dfeed, spot(x, t), at.across_x()))
+
+    plan = list(GATHER_PLAN)
+
+    def gather(last):
+        while plan and len(GATHER_PLAN) - len(plan) <= last:
+            for step in plan.pop(0):
+                gather_step(*step)
+
+    home = {0: (G3, 0, 512), 1: (W, DOWN, DOWN + 512), 2: (W, DOWN + 512, COLS), 3: (G3, 512, 1024)}
     sc = Scatter(at, lambda p: home[p], shard, SCATTERED, xh, yh, xf, yf, zl, rs_send, rs_recv)
     home_pair = {0: (W, UP, 1024), 1: (G2, 0, 1024)}
     ps = PairScatter(at, lambda m: home_pair[m], shard, yf2, zl2, xs2, xr2, ps_send, ps_recv)
 
     def write(p):
         def store(total):
-            if p == 0:
-                o_qkv[1] = total[:, :512]
-                o_qkv[2] = total[:, 512:]
-            elif p == 1:
-                o_qkv[0] = total
+            if p < 3:
+                o_qkv[p] = total
             else:
                 o_out[...] = total
         return store
@@ -681,24 +728,26 @@
             ref[:, pl.ds(pl.multiple_of(far_x * 1024, 1024), 1024)] = total
         return store
 
-    queue = []
-
-    def reduce_begin(p):
-        sc.begin(p)
-        for k in (3, 2, 1, 0):
-            queue.append(lambda p=p, k=k: sc.plane(p, k))
-        for k in (3, 2, 1, 0):
-            queue.append(lambda p=p, k=k: sc.line(p, k, write(p)))
-
-    def reduce_pair(m):
-        ps.begin(m)
-        for k in (3, 2, 1, 0):
-            queue.append(lambda m=m, k=k: ps.line(m, k, write_pair(m)))
-
-    def scatter(n):
-        while n > 0 and queue:
-            queue.pop(0)()
-            n -= 1
+    def scatter_step(kind, p, k=None):
+        if kind == 0:
+            sc.begin(p, k)
+        elif kind == 1:
+            sc.plane(p, k)
+        elif kind == 2:
+            sc.line(p, k, write(p))
+        elif kind == 3:
+            ps.begin(p, k)
+        elif kind == 4:
+            ps.line(p, k, write_pair(p))
+        else:
+            ps.last(p, write_pair(p))
+
+    back_plan = list(SCATTER_PLAN)
+
+    def scatter(last):
+        while back_plan and len(SCATTER_PLAN) - len(back_plan) <= last:
+            for step in back_plan.pop(0):
+                scatter_step(*step)
 
     def send(i, src, dst, other):
         return pltpu.make_async_remote_copy(
@@ -754,12 +803,14 @@
         dfeed[pl.ds(pl.multiple_of((x * 2 + t) * own + b, BLOCK), BLOCK), :] = low
         add("bdown", low.astype(F32))
 
+    gather(0)
     each_block(first_norm)
     shares = [share(0, rows1, mine, at.twin()), share(1, dfeed, spot(x, t), at.twin())]
-    gather(3)
+    for p in range(3):
+        gather(1 + p)
+        g.finish(p)
     take(0, rows1, theirs)
-    need("qkv")
-    shares.append(share(2, dfeed, spot(x, t), at.across_x()))
+    gather(5)
 
     def project(c):
         v = nn(rows1[...], W[:, pl.ds(c, 256)])
@@ -770,7 +821,6 @@
         qkv[:, pl.ds(c, 256)] = ((v + bias) * scale).astype(BF)
 
     tiles(0, 1536, project)
-    gather(2)
 
     first_lanes = lax.broadcasted_iota(jnp.int32, (own, 128), 1) < HD
 
@@ -798,10 +848,15 @@
             return 0
         lax.fori_loop(first, last, go, 0)
 
-    for i in range(4):
-        attend_some(2 * i, 2 * i + 2, attend)
-        gather(3)
-    need("out")
+    first = 0
+    for i in range(1, 9):
+        if i == 8 or GATHER_PLAN[6 + i]:
+            gather(6 + first)
+            attend_some(first, i, attend)
+            first = i
+    gather(14)
+    g.finish(3)
+    gather(17)
 
     def reduced(i, src, cols, keep):
         def other(c):
@@ -815,7 +870,7 @@
         return copy
 
     branch_copy = reduced(3, heads, pl.ds(OUT, 512), own_a)
-    gather(2)
+    gather(18)
     branch_copy.wait()
 
     def second_norm(b, r):
@@ -828,15 +883,17 @@
         n, _ = normed(m)
         rows2[pl.ds(pl.multiple_of((x * 2 + t) * own + b, BLOCK), BLOCK), :] = (n * g2[...] + s2[...]).astype(BF)
 
+    gather(19)
     each_block(second_norm)
     shares.append(share(4, rows2, spot(x, t), at.across_x()))
     shares.append(share(5, rows2, spot(x, t), at.twin()))
-    gather(1)
+    gather(22)
 
     take(2, dfeed, spot(1 - x, t))
     shares.append(share(6, dfeed, spot(1 - x, t), at.twin()))
     take(1, dfeed, spot(x, 1 - t))
     take(6, dfeed, spot(1 - x, 1 - t))
+    gather(23)
     flip(dfeed)
     take(5, rows2, spot(x, 1 - t))
 
@@ -857,18 +914,21 @@
     def grad_down(c):
         G2[:, pl.ds(c, 256)] = nn(tall[...], act[:, pl.ds(c, 256)]).astype(BF)
 
-    need("up")
+    gather(24)
+    pg.finish(0)
+    gather(26)
     hidden(x)
-    gather(2)
+    gather(28)
     take(4, rows2, spot(1 - x, t))
     shares.append(share(7, rows2, spot(1 - x, t), at.twin()))
     take(7, rows2, spot(1 - x, 1 - t))
+    gather(31)
     hidden(1 - x)
-    gather(2)
+    gather(33)
     tiles(0, 1024, grad_down)
+    gather(100)
+    scatter(1)
     flip(rows2)
-    gather(100)
-    reduce_pair(1)
 
     def back_act(far_x):
         r = chip_rows(far_x)
@@ -886,8 +946,8 @@
         tiles(0, width, body)
 
     class Sum4:
-        def __init__(self, i, n, src, cols, keep):
-            self.i, self.n, self.src, self.cols, self.keep = i, n, src, cols, keep
+        def __init__(self, i, n, src, cols, keep, parts):
+            self.i, self.n, self.src, self.cols, self.keep, self.parts = i, n, src, cols, keep, parts
 
         def away(self, far_x, slot):
             def put(c, v):
@@ -901,14 +961,16 @@
             first = self.away(1 - x, 0)
 
             def put(c, v):
-                own_b[:, c] = v
+                send_x[self.n, :, c] = v.astype(BF)
             product(self.src, spot(1 - x, t), self.cols, put)
+            scatter(self.parts[0])
             first.wait()
 
             def body(b, r):
-                send_x[self.n, r, :] = (own_b[r, :] + got_t[self.n, 0, r, :].astype(F32)).astype(BF)
+                send_x[self.n, r, :] = send_x[self.n, r, :] + got_t[self.n, 0, r, :]
             each_block(body)
             self.cross = send(self.i + 2, send_x.at[self.n], got.at[2 + self.n], at.across_x())
+            scatter(self.parts[1])
             self.cross.start()
 
         def near(self):
@@ -922,28 +984,34 @@
         def value(self, r):
             return self.keep[r, :] + got_t[self.n, 1, r, :].astype(F32) + got[2 + self.n, r, :].astype(F32)
 
-    need("down")
+    pg.finish(1)
+    scatter(2)
     back_act(1 - x)
-    two = Sum4(8, 0, gp, pl.ds(UP, 1024), own_a)
+    scatter(3)
+    two = Sum4(8, 0, gp, pl.ds(UP, 1024), own_a, (4, 5))
     two.far()
-    scatter(1)
+    scatter(6)
     back_act(x)
+    scatter(7)
     two.near()
-    for p in range(2):
+    for p in range(4):
         g.drain(p)
-        pg.drain(p)
-    scatter(1)
+    for m in range(2):
+        pg.drain(m)
+    scatter(8)
 
     def grad_up(c):
         W[:, pl.ds(UP + c, 256)] = nn(tall[...], gp[:, pl.ds(c, 256)]).astype(BF)
 
-    tiles(0, 1024, grad_up)
-    reduce_pair(0)
-    scatter(1)
-    four = Sum4(11, 1, act, pl.ds(DOWN, 1024), own_c)
+    tiles(0, 512, grad_up)
+    scatter(9)
+    tiles(512, 1024, grad_up)
+    scatter(11)
+    four = Sum4(11, 1, act, pl.ds(DOWN, 1024), own_c, (11, 12))
     four.far()
-    scatter(1)
+    scatter(13)
     four.near()
+    scatter(14)
     two.cross.wait()
     for i in (1, 2, 5):
         shares[i].wait_send()
@@ -960,24 +1028,26 @@
         dbr[pl.ds(pl.multiple_of(t * own + b, BLOCK), BLOCK), :] = low
         add("bout", low.astype(F32))
 
+    scatter(16)
     each_block(second_back)
     shares.append(share(14, dbr, mine, at.twin()))
-    scatter(1)
+    scatter(17)
     take(14, dbr, theirs)
+    scatter(18)
 
     def back_heads(c):
         datt[:, pl.ds(c, 256)] = nn(dbr[...], W[:, pl.ds(OUT + c, 256)]).astype(BF)
 
     tiles(0, 512, back_heads)
+    scatter(19)
     flip(dbr)
+    scatter(20)
     short = pl.ds(0, 2 * own)
 
     def grad_out(c):
         G3[:, pl.ds(512 + c, 256)] = nn(tall[:, short], heads[:, pl.ds(c, 256)]).astype(BF)
 
     tiles(0, 512, grad_out)
-    reduce_begin(2)
-    scatter(2)
 
     def attend_back(it):
         image, j = it // 4, it % 4
@@ -1009,11 +1079,16 @@
                 ref = total_of["bq" if base == 0 else "bv"]
                 ref[:, lanes] += fold(v.astype(F32))
 
-    for i in range(4):
-        attend_some(2 * i, 2 * i + 2, attend_back)
-        scatter(3)
-
+    first = 0
+    for i in range(1, 9):
+        if i == 8 or SCATTER_PLAN[22 + i]:
+            scatter(22 + first)
+            attend_some(first, i, attend_back)
+            first = i
+
+    scatter(30)
     one_copy = reduced(15, dproj, pl.ds(QKV, 1536), own_a)
+    scatter(32)
     flip(rows1)
 
     def grad_kv(c):
@@ -1022,10 +1097,13 @@
     def grad_q(c):
         G3[:, pl.ds(c, 256)] = nn(tall[:, short], dproj[:, pl.ds(c, 256)]).astype(BF)
 
-    tiles(0, 1024, grad_kv)
-    reduce_begin(0)
+    scatter(33)
+    tiles(0, 512, grad_kv)
+    scatter(35)
+    tiles(512, 1024, grad_kv)
+    scatter(37)
     tiles(0, 512, grad_q)
-    reduce_begin(1)
+    scatter(39)
     one_copy.wait()
 
     def first_back(b, r):
@@ -1035,8 +1113,9 @@
         add("s1", dy)
         gin_out[r, :] += norm_back(dy, n, scale, g1[...])
 
+    scatter(40)
     each_block(first_back)
-    scatter(4)
+    scatter(41)
     four.cross.wait()
 
     def finish_feed(b, r):
@@ -1047,7 +1126,9 @@
         add("res", keep * res * res)
         act_out[r, :] = (keep * res).astype(BF)
 
+    scatter(42)
     each_block(finish_feed)
+    scatter(43)
 
     for i in range(8):
         sums[i : i + 1, :] = jnp.sum(acc[i], axis=0, keepdims=True)
@@ -1065,15 +1146,14 @@
             device_id=other, device_id_type=MESH,
         )
         c.start()
-        scatter(2)
+        scatter(45 + 2 * i)
         c.wait()
         sums[...] += sums_got[i]
     o_sums[...] = sums[...]
     scatter(1000)
     for m in (1, 0):
-        ps.last(m, write_pair(m))
         ps.drain(m)
-    for p in range(3):
+    for p in range(4):
         sc.drain(p)
     for i in (0, 3, 4, 6, 7):
         shares[i].wait_send()
@@ -1127,7 +1207,6 @@
             pltpu.VMEM((width, 2 * group), BF),
             pltpu.VMEM((own, width), F32),
             pltpu.VMEM((own, width), F32),
-            pltpu.VMEM((own, width), F32),
             pltpu.VMEM((2, own, width), BF),
             pltpu.VMEM((2, own, width), BF),
             pltpu.VMEM((4, own, width), BF),
@@ -1137,12 +1216,12 @@
             pltpu.VMEM((16, width), F32),
             pltpu.VMEM((5, 16, width), F32),
             dma((6,)),
-            dma((2, 6, 4)),
-            dma((2, 5, 4)),
+            dma((4, 6, 4)),
+            dma((4, 5, 4)),
             dma((4, 4, 4)),
             dma((4, 3, 4)),
-            dma((3, 5, 4)),
-            dma((3, 5, 5)),
+            dma((4, 5, 4)),
+            dma((4, 5, 5)),
             dma((2, 3, 4)),
             dma((2, 3, 5)),
             dma((16,)),

time: 262 us -> 208 us (0.79)
  Pallas kernels: 248 us -> 195 us
    pallas_call x1, Pallas kernels: 248 us -> 195 us  [block(): pl.pallas_call(block_kernel, out_shape=(jax.ShapeDtypeStruct((own, width)...]
where the time goes in v4:
time: 208 us
  Pallas kernels  195 us (94%)
  local copies, waits for them, and re-layouts  10.8 us (5%)
    pallas_call x1, Pallas kernels, block(): pl.pallas_call(block_kernel, out_shape=(jax.ShapeDtypeStruct((own, width)...  195 us
    unnamed x18, local copies, waits for them, and re-layouts  6.93 us

profile of v4, /device:TPU:0, one launch (start us, length us, event | category | flops | bytes accessed | tf_op | source)
XLA Modules:
  0.0 208.0 jit_solution(304730023996108674)
XLA Ops:
  0.7 194.7 %shard_map.262 = (bf16[320,1024]{1,0:T(8,128)(2,1)}, f32[320,1024]{1,0:T(8,128)}, f32[3,64,512]{2,1,0:T(8,128)}, f32[64,512]{1,0:T(8,128)}, f32[64,2048]{1,0:T(8...) custom-call(s32[2]{0:T(128)} %counts.1, bf16[320,1024]{1,0:T(8,128)(2,1)} %x_ref.1, bf16[320,1024]{1,0:T(8,128)(2,1)} %cot_ref.1, ...), custom_call_target="tpu_custom_call" | custom-call | tf_op jit(solution)/shard_map/pallas_call | solution.py:1171
  195.3 0.0 copy-start
  195.3 1.4 slice.43
  197.4 1.2 sqrt_bitcast_fusion
  198.6 0.8 slice_bitcast_fusion
  199.3 0.8 slice.33
  200.1 0.1 constant_dynamic-slice_fusion
  200.2 0.6 dynamic_slice.7
  200.7 0.6 slice.34
  201.3 0.5 slice_bitcast_fusion.1
  201.8 2.0 copy.39
  203.8 0.0 copy-done
  203.8 0.0 copy-start.3
  203.8 0.0 copy-start.4
  203.8 0.0 copy-start.2
  203.8 1.1 copy.40
  204.9 0.1 copy-done.3
  205.0 0.0 copy-start.1
  205.0 0.7 copy.41
  205.8 0.0 copy-done.4
  205.8 0.7 copy.42
  206.4 0.0 copy-done.2
  206.4 0.8 copy.43
  207.2 0.0 copy-done.1
  207.2 0.8 copy.44
  (1 shorter events, 0.0 us)
Async XLA Ops:
  195.3 8.5 %copy-start = (f32[320,1024]{1,0:T(8,128)S(1)}, f32[320,1024]{1,0:T(8,128)}, u32[]{:S(2)}) copy-start(f32[320,1024]{1,0:T(8,128)} %get-tuple-element.51) | copy-start | bytes 3932164
  203.8 1.2 copy-start.3
  203.8 2.0 copy-start.4
  203.8 2.6 %copy-start.2 = (f32[64,2048]{1,0:T(8,128)S(1)}, f32[64,2048]{1,0:T(8,128)}, u32[]{:S(2)}) copy-start(f32[64,2048]{1,0:T(8,128)} %get-tuple-element.56) | copy-start | bytes 1572868
  205.0 2.2 %copy-start.1 = (f32[64,2048]{1,0:T(8,128)S(1)}, f32[64,2048]{1,0:T(8,128)}, u32[]{:S(2)}) copy-start(f32[64,2048]{1,0:T(8,128)} %get-tuple-element.28) | copy-start | bytes 1572868

commit v5 on v4

--- a/solution.py
+++ b/solution.py
@@ -118,27 +118,20 @@
         )[kind]()
         self.copy(p, ref, (kind, z), (kind, z), at.across_x()).wait_recv()
 
-    def line(self, p, k):
-        at = self.at
-        z = at.order(k)
-        if k > 0:
-            self.arrived(p, 0, z)
-        if k == 0:
-            self.z_in(p, z).start()
-        if k == 1:
-
-            @pl.when(at.w == 1)
-            def _():
+    def line(self, p, k, w):
+        at = self.at
+
+        @pl.when(at.w == w)
+        def _():
+            z = at.order(k)
+            if k > 0:
+                self.arrived(p, 0, z)
+            if k == 0 or (k == 1 and w == 1):
                 self.z_in(p, z).start()
-
-        else:
-
-            @pl.when(at.w == 1)
-            def _():
+            if w == 1 and k != 1:
                 self.z_out(p, z).start()
-
-        self.x_full(p, z).start()
-        self.y_full(p, z).start()
+            self.x_full(p, z).start()
+            self.y_full(p, z).start()
 
     def plane(self, p, k):
         z = self.at.order(k)
@@ -261,47 +254,35 @@
     def wait_line(self, p, z, slot):
         self.z_in(p, z, slot).wait_recv()
 
-    def line(self, p, k, out=None):
-        at = self.at
-        z = at.order(k)
-        self.x_full(p, z).wait_recv()
-        self.y_full(p, z).wait_recv()
-        ref = self.rows(p, z, at.y, at.x)
-        total = (
-            ref[...].astype(jnp.float32)
-            + self.xf[z, :, self.cols(p)].astype(jnp.float32)
-            + self.yf[z, :, self.cols(p)].astype(jnp.float32)
-        )
-        if k > 0:
-
-            @pl.when(at.w == 0)
-            def _():
+    def line(self, p, k, w, out):
+        at = self.at
+
+        @pl.when(at.w == w)
+        def _():
+            z = at.order(k)
+            self.x_full(p, z).wait_recv()
+            self.y_full(p, z).wait_recv()
+            ref = self.rows(p, z, at.y, at.x)
+            parts = [self.xf.at[z, :, self.cols(p)], self.yf.at[z, :, self.cols(p)]]
+            if w == 1:
+                self.wait_line(p, z, z)
+                parts.append(self.zl.at[z, :, self.cols(p)])
+            if k == 0:
+                self.wait_line(p, z, 4)
+                parts.append(self.zl.at[4, :, self.cols(p)])
+            total = ref[...].astype(jnp.float32)
+            for part in parts:
+                total = total + part[...].astype(jnp.float32)
+            if k == 0:
+                out(total)
+            else:
                 ref[...] = total.astype(jnp.bfloat16)
-                self.z_in(p, z, z).start()
-
-            @pl.when(at.w == 1)
-            def _():
-                self.wait_line(p, z, z)
-                ref[...] = (total + self.zl[z, :, self.cols(p)].astype(jnp.float32)).astype(jnp.bfloat16)
-                if k == 3:
+                if w == 0 or k == 3:
                     self.z_in(p, z, z).start()
                 elif k == 2:
                     self.z_in(p, z, 4).start()
                 else:
                     self.z_out(p, z, 4).start()
-
-        else:
-            self.wait_line(p, z, 4)
-            total = total + self.zl[4, :, self.cols(p)].astype(jnp.float32)
-
-            @pl.when(at.w == 0)
-            def _():
-                out(total)
-
-            @pl.when(at.w == 1)
-            def _():
-                self.wait_line(p, z, z)
-                out(total + self.zl[z, :, self.cols(p)].astype(jnp.float32))
 
     def drain(self, p):
         at = self.at
@@ -355,31 +336,26 @@
         ref = self.rows(m, z, self.at.y, self.far_x(h))
         return self.copy(m, h, ref, ref, 2, 1, z, self.at.across_y())
 
-    def line(self, m, h, k):
-        at = self.at
-        z = at.order(k)
-        if k > 0:
+    def line(self, m, h, k, w):
+        at = self.at
+
+        @pl.when(at.w == w)
+        def _():
+            z = at.order(k)
             ref = self.rows(m, z, at.y, self.far_x(h))
-            self.copy(m, h, ref, ref, 0, 0, z, at.inward()).wait_recv()
-        elif h == 1:
-            ref = self.rows(m, z, at.y, self.far_x(h))
-            self.copy(m, h, ref, ref, 0, 2, z, at.across_x()).wait_recv()
-        if k == 0:
-            self.z_in(m, h, z).start()
-        if k == 1:
-
-            @pl.when(at.w == 1)
-            def _():
+            if k > 0:
+                self.copy(m, h, ref, ref, 0, 0, z, at.inward()).wait_recv()
+            elif h == 1:
+                self.copy(m, h, ref, ref, 0, 2, z, at.across_x()).wait_recv()
+            if k == 0 or (k == 1 and w == 1):
                 self.z_in(m, h, z).start()
-
-        else:
-
-            @pl.when(at.w == 1)
-            def _():
+            if w == 1 and k != 1:
                 self.z_out(m, h, z).start()
 
-    def cross(self, m, h, k):
-        self.y_copy(m, h, self.at.order(k)).start()
+    def cross(self, m, h, k, w):
+        @pl.when(self.at.w == w)
+        def _():
+            self.y_copy(m, h, self.at.order(k)).start()
 
     def finish(self, m):
         at = self.at
@@ -413,9 +389,10 @@
 
 
 class PairScatter:
-    def __init__(self, at, full, shard, yf, zl, xs, xr, send, recv):
-        self.at, self.full, self.shard = at, full, shard
-        self.yf, self.zl, self.xs, self.xr, self.send, self.recv = yf, zl, xs, xr, send, recv
+    def __init__(self, at, full, shard, first, units, xs, xr, send, recv):
+        self.at, self.full, self.shard, self.first = at, full, shard, first
+        self.units, self.xs, self.xr, self.send, self.recv = units, xs, xr, send, recv
+        self.base = {1: 0, 0: 11 if 1 in first else 9}
 
     def unit(self, m, z, y):
         ref, c0, n = self.full(m)
@@ -432,12 +409,22 @@
             device_id_type=MESH,
         )
 
+    def from_y(self, m, z):
+        return self.units.at[self.base[m] + (10 if m in self.first else z)]
+
+    def from_z(self, m, col, slot):
+        return self.units.at[self.base[m] + (5 * col if m in self.first else 4) + slot]
+
+    def column(self, col):
+        return self.at.y if col == 0 else 1 - self.at.y
+
     def y_copy(self, m, z):
-        at = self.at
-        return self.copy(m, self.unit(m, z, 1 - at.y), self.yf.at[m, z], (1, z), (1, z), at.across_y())
-
-    def z_copy(self, m, z, slot, other):
-        return self.copy(m, self.unit(m, z, self.at.y), self.zl.at[m, slot], (0, z), (0, slot), other)
+        return self.copy(m, self.unit(m, z, 1 - self.at.y), self.from_y(m, z), (1, z), (1, z), self.at.across_y())
+
+    def z_copy(self, m, col, z, slot, other):
+        return self.copy(
+            m, self.unit(m, z, self.column(col)), self.from_z(m, col, slot), (3 + col, z), (3 + col, slot), other
+        )
 
     def x_copy(self, m):
         return self.copy(m, self.xs.at[m], self.xr.at[m], (2, 0), (2, 0), self.at.across_x())
@@ -445,63 +432,74 @@
     def begin(self, m, k):
         self.y_copy(m, self.at.order(k)).start()
 
-    def line(self, m, k, out):
+    def pass_on(self, m, col, k, w):
         at = self.at
         z = at.order(k)
-        self.y_copy(m, z).wait_recv()
-        ref = self.unit(m, z, at.y)
-        if k > 0:
-
-            @pl.when(at.w == 0)
-            def _():
-                ref[...] = ref[...] + self.yf[m, z]
-                self.z_copy(m, z, z, at.inward()).start()
-
-            @pl.when(at.w == 1)
-            def _():
-                self.z_copy(m, z, z, at.inward()).wait_recv()
-                ref[...] = (
-                    ref[...].astype(jnp.float32)
-                    + self.yf[m, z].astype(jnp.float32)
-                    + self.zl[m, z].astype(jnp.float32)
-                ).astype(jnp.bfloat16)
-                if k == 3:
-                    self.z_copy(m, z, z, at.inward()).start()
-                elif k == 2:
-                    self.z_copy(m, z, 4, at.inward()).start()
-                else:
-                    self.z_copy(m, z, 4, at.outward()).start()
-
+        if w == 0:
+            self.z_copy(m, col, z, z, at.inward()).start()
+        elif k == 1:
+            self.z_copy(m, col, z, 4, at.outward()).start()
         else:
-            self.z_copy(m, z, 4, at.inward()).wait_recv()
-
-            def total(x, second):
-                full, c0, n = self.full(m)
-                size = self.shard
-                own = full[pl.ds(pl.multiple_of(at.chip(z, at.y, x) * size, size), size), pl.ds(c0, n)]
-                part = pl.ds(pl.multiple_of(x * size, size), size)
-                v = (
-                    own.astype(jnp.float32)
-                    + self.yf[m, z, part, :].astype(jnp.float32)
-                    + self.zl[m, 4, part, :].astype(jnp.float32)
-                )
-                if second:
-                    v = v + self.zl[m, z, part, :].astype(jnp.float32)
-                return v
-
-            def put(second):
-                self.xs[m] = total(1 - at.x, second).astype(jnp.bfloat16)
-                self.x_copy(m).start()
-                out(at.x, total(at.x, second))
-
-            @pl.when(at.w == 0)
-            def _():
-                put(False)
-
-            @pl.when(at.w == 1)
-            def _():
-                self.z_copy(m, z, z, at.inward()).wait_recv()
-                put(True)
+            self.z_copy(m, col, z, z if k == 3 else 4, at.inward()).start()
+
+    def add_line(self, m, col, k, w, extra):
+        at = self.at
+        z = at.order(k)
+        ref = self.unit(m, z, self.column(col))
+        parts = list(extra)
+        if k == 0:
+            self.z_copy(m, col, z, 4, at.inward()).wait_recv()
+            parts.append(self.from_z(m, col, 4))
+        if w == 1:
+            self.z_copy(m, col, z, z, at.inward()).wait_recv()
+            parts.append(self.from_z(m, col, z))
+        if parts:
+            v = ref[...].astype(jnp.float32)
+            for part in parts:
+                v = v + part[...].astype(jnp.float32)
+            ref[...] = v.astype(jnp.bfloat16)
+
+    def finish(self, m, out, second):
+        at = self.at
+        size = self.shard
+        full, c0, n = self.full(m)
+
+        def total(x):
+            rows = pl.ds(pl.multiple_of(at.chip(at.z, at.y, x) * size, size), size)
+            v = full[rows, pl.ds(c0, n)].astype(jnp.float32)
+            if second:
+                v = v + self.from_y(m, at.z)[pl.ds(pl.multiple_of(x * size, size), size), :].astype(jnp.float32)
+            return v
+
+        self.xs[m] = total(1 - at.x).astype(jnp.bfloat16)
+        self.x_copy(m).start()
+        out(at.x, total(at.x))
+
+    def line(self, m, k, w, out):
+        at = self.at
+
+        @pl.when(at.w == w)
+        def _():
+            z = at.order(k)
+            self.y_copy(m, z).wait_recv()
+            self.add_line(m, 0, k, w, [self.from_y(m, z)])
+            if k > 0:
+                self.pass_on(m, 0, k, w)
+            else:
+                self.finish(m, out, False)
+
+    def line_first(self, m, col, k, w):
+        @pl.when(self.at.w == w)
+        def _():
+            self.add_line(m, col, k, w, [])
+            if k > 0:
+                self.pass_on(m, col, k, w)
+            elif col == 1:
+                self.y_copy(m, self.at.z).start()
+
+    def meet(self, m, out):
+        self.y_copy(m, self.at.z).wait_recv()
+        self.finish(m, out, True)
 
     def last(self, m, out):
         self.x_copy(m).wait_recv()
@@ -511,107 +509,114 @@
         at = self.at
         for k in range(4):
             z = at.order(k)
-            self.y_copy(m, z).wait_send()
+            if m not in self.first or k == 0:
+                self.y_copy(m, z).wait_send()
             if k > 0:
-                self.z_copy(m, z, z, at.inward()).wait_send()
+                for col in range(2 if m in self.first else 1):
+                    self.z_copy(m, col, z, z, at.inward()).wait_send()
         self.x_copy(m).wait_send()
 
 
 QKV, OUT, UP, DOWN, COLS = 0, 1536, 2048, 3072, 4096
-GATHERED = ((0, 512), (512, 1024), (1024, 1536), (1536, 2048))
-SCATTERED = ((0, 512), (512, 1024), (1024, 1536), (1536, 2048))
-GATHER_PLAN = (
-    ((0, 2, 0), (0, 1, 0), (0, 0, 0), (0, 3, 0), (0, 0, 1), (1, 0, 0), (0, 1, 1), (0, 1, 2), (1, 1, 0), (3, 0, 0, 0), (0, 2, 1), (0, 2, 2), (1, 1, 1), (0, 0, 2), (0, 1, 3), (3, 0, 0, 1), (0, 3, 1), (0, 2, 3), (1, 1, 2), (1, 0, 1), (3, 0, 0, 2), (0, 0, 3), (1, 2, 0), (3, 1, 0, 0), (1, 2, 1), (1, 2, 2),),
-    ((1, 0, 2), (1, 1, 3), (3, 0, 0, 3), (1, 0, 3), (1, 2, 3), (0, 3, 2), (0, 3, 3), (1, 3, 0), (2, 0), (2, 1), (4, 1, 0, 0), (3, 1, 0, 1),),
-    (),
-    ((4, 0, 0, 0),),
-    (),
-    (),
-    (),
-    ((1, 3, 1), (1, 3, 2), (1, 3, 3), (4, 0, 0, 1), (5,),),
-    ((3, 0, 1, 0),),
-    (),
-    (),
-    (),
-    ((3, 1, 0, 2), (3, 1, 1, 0), (4, 0, 1, 0),),
-    (),
-    ((4, 1, 1, 0), (3, 0, 1, 1), (4, 0, 0, 2), (4, 0, 1, 1),),
-    (),
-    (),
-    (),
-    ((4, 0, 0, 3),),
-    ((3, 0, 1, 2),),
-    (),
-    (),
-    ((4, 0, 1, 2), (3, 0, 1, 3), (4, 0, 1, 3), (3, 1, 1, 1), (3, 1, 1, 2), (4, 1, 1, 1), (4, 1, 1, 2), (4, 1, 0, 1), (3, 1, 1, 3),),
-    (),
-    ((3, 1, 0, 3), (4, 1, 0, 2),),
-    (),
-    (),
-    ((4, 1, 1, 3),),
-    (),
-    (),
-    (),
-    (),
-    (),
-    ((4, 1, 0, 3),),
-)
-SCATTER_PLAN = (
-    (),
-    (),
-    (),
-    ((3, 1, 3),),
-    (),
-    (),
-    (),
-    ((3, 1, 2), (3, 1, 1),),
-    ((4, 1, 3),),
-    (),
-    (),
-    ((3, 1, 0), (4, 1, 2),),
-    (),
-    ((4, 1, 1),),
-    ((3, 0, 3),),
-    (),
-    (),
-    ((3, 0, 2),),
-    (),
-    (),
-    (),
-    (),
-    (),
-    ((3, 0, 1), (0, 3, 3),),
-    (),
-    (),
-    ((4, 1, 0),),
-    ((0, 3, 2),),
-    ((3, 0, 0), (0, 3, 1), (0, 3, 0),),
-    (),
-    ((1, 3, 3),),
-    (),
-    ((1, 3, 2),),
-    (),
-    (),
-    (),
-    (),
-    ((0, 2, 3), (0, 1, 3), (4, 0, 3), (0, 2, 2), (1, 3, 1),),
-    (),
-    ((0, 0, 3), (0, 2, 1), (1, 1, 3),),
-    ((0, 2, 0), (1, 0, 3), (1, 3, 0), (2, 3, 3), (0, 1, 2), (0, 0, 2), (1, 2, 3), (4, 0, 2), (0, 0, 1), (1, 2, 2), (4, 0, 1),),
-    ((0, 1, 1),),
-    ((1, 0, 2),),
-    (),
-    (),
-    ((1, 0, 1), (2, 2, 3), (1, 1, 2), (1, 1, 1), (0, 0, 0), (2, 3, 2), (0, 1, 0),),
-    ((2, 0, 3),),
-    ((1, 2, 1), (2, 1, 3),),
-    (),
-    ((4, 0, 0), (2, 3, 1), (1, 1, 0), (2, 1, 2),),
-    (),
-    ((1, 2, 0), (2, 2, 2), (2, 1, 1), (2, 2, 1), (5, 1), (1, 0, 0),),
-    (),
-    ((5, 0), (2, 0, 2), (2, 0, 1), (2, 3, 0), (2, 2, 0), (2, 1, 0),),
-    ((2, 0, 0),),
+PIECES = ((0, 384), (384, 768), (768, 1152), (1152, 1536), (1536, 2048))
+LINE_FIRST = ()
+PLAN = (
+    ((2, 0), (0, 2, 0, 0), (0, 0, 0, 0), (0, 1, 0, 0), (3, 0, 0, 0, 0), (0, 3, 0, 0), (4, 0, 0, 0, 0), (0, 2, 0, 1), (0, 3, 0, 1), (0, 1, 0, 1), (0, 1, 1, 0), (0, 0, 0, 1), (0, 2, 1, 1), (0, 1, 1, 1), (0, 1, 2, 1), (0, 0, 1, 0), (0, 0, 1, 1), (0, 0, 2, 1), (0, 1, 3, 1), (3, 0, 1, 0, 0), (0, 3, 1, 1), (0, 3, 2, 1), (1, 0, 0), (0, 2, 1, 0), (0, 0, 3, 1), (3, 0, 0, 0, 1), (3, 1, 0, 0, 0), (1, 3, 0), (0, 2, 2, 1), (0, 3, 1, 0), (0, 1, 2, 0),),
+    ((0, 3, 3, 1), (0, 3, 2, 0), (0, 4, 0, 0), (3, 0, 1, 0, 1), (0, 0, 2, 0), (2, 1), (3, 0, 0, 1, 1), (1, 1, 0), (0, 2, 3, 1), (0, 1, 3, 0), (4, 0, 1, 0, 0), (3, 0, 1, 1, 0), (1, 1, 1), (1, 0, 1), (0, 0, 3, 0), (1, 2, 0), (3, 0, 0, 1, 0), (0, 2, 2, 0), (4, 0, 0, 0, 1), (0, 2, 3, 0), (3, 0, 0, 2, 1), (1, 0, 2), (1, 0, 3), (1, 1, 2), (0, 4, 0, 1), (3, 1, 1, 0, 0), (0, 3, 3, 0), (1, 1, 3), (0, 4, 1, 1), (0, 4, 2, 1), (0, 4, 3, 1), (3, 1, 1, 0, 1), (3, 0, 1, 1, 1), (3, 1, 0, 0, 1), (1, 2, 1), (1, 3, 1), (3, 0, 0, 3, 1), (3, 0, 0, 2, 0), (1, 2, 2), (3, 0, 1, 2, 1), (3, 1, 1, 1, 1),),
+    (),
+    ((1, 2, 3), (0, 4, 1, 0), (0, 4, 2, 0), (0, 4, 3, 0), (1, 3, 2), (1, 3, 3),),
+    (),
+    (),
+    (),
+    ((1, 4, 0), (3, 1, 0, 1, 0), (1, 4, 1), (4, 1, 0, 0, 1), (4, 1, 1, 0, 1),),
+    ((3, 1, 1, 1, 0), (3, 1, 0, 1, 1), (1, 4, 2), (1, 4, 3), (4, 0, 1, 1, 0), (3, 1, 1, 2, 1),),
+    ((5,), (4, 0, 0, 1, 0), (3, 0, 0, 3, 0),),
+    ((3, 0, 1, 3, 1), (3, 1, 0, 2, 1), (4, 1, 1, 0, 0), (3, 0, 1, 2, 0), (4, 0, 1, 2, 0),),
+    (),
+    (),
+    (),
+    (),
+    ((4, 0, 0, 2, 0), (4, 0, 1, 0, 1), (4, 0, 1, 1, 1),),
+    ((3, 1, 0, 3, 1),),
+    (),
+    ((4, 0, 0, 3, 0), (3, 1, 1, 3, 1), (4, 0, 1, 2, 1), (4, 0, 1, 3, 1),),
+    (),
+    (),
+    (),
+    (),
+    ((4, 0, 0, 1, 1), (4, 0, 0, 2, 1),),
+    ((4, 1, 0, 0, 0), (4, 0, 0, 3, 1), (4, 1, 0, 1, 1), (3, 0, 1, 3, 0), (4, 0, 1, 3, 0), (3, 1, 0, 2, 0), (4, 1, 1, 1, 0), (3, 1, 1, 2, 0), (3, 1, 1, 3, 0), (4, 1, 1, 1, 1), (4, 1, 1, 2, 1),),
+    ((4, 1, 0, 2, 1), (4, 1, 0, 1, 0), (4, 1, 1, 2, 0), (4, 1, 0, 3, 1), (4, 1, 0, 2, 0), (3, 1, 0, 3, 0), (4, 1, 1, 3, 0), (4, 1, 1, 3, 1),),
+    ((4, 1, 0, 3, 0),),
+    (),
+    (),
+    (),
+    (),
+    (),
+    (),
+    (),
+    (),
+    (),
+    (),
+    (),
+    (),
+    ((13, 1, 3),),
+    (),
+    (),
+    ((13, 1, 2),),
+    (),
+    (),
+    ((13, 1, 1),),
+    (),
+    (),
+    ((13, 0, 3),),
+    (),
+    (),
+    (),
+    (),
+    (),
+    ((13, 0, 2), (13, 1, 0),),
+    (),
+    (),
+    (),
+    (),
+    (),
+    (),
+    ((14, 1, 3, 0), (10, 4, 3), (10, 4, 2),),
+    (),
+    ((13, 0, 1),),
+    ((14, 1, 2, 0),),
+    (),
+    ((14, 0, 3, 0),),
+    ((10, 4, 1),),
+    ((14, 0, 2, 0),),
+    ((11, 4, 3),),
+    ((10, 0, 3), (14, 1, 3, 1), (10, 0, 2), (10, 1, 3), (10, 0, 1),),
+    ((11, 4, 2), (10, 1, 2), (10, 1, 1),),
+    ((11, 0, 3), (11, 0, 2), (11, 0, 1),),
+    ((14, 1, 1, 0), (10, 4, 0), (10, 0, 0), (14, 1, 2, 1), (13, 0, 0), (10, 1, 0), (14, 1, 1, 1),),
+    ((11, 4, 1),),
+    (),
+    ((14, 0, 3, 1), (11, 1, 3), (11, 1, 2), (14, 0, 1, 0), (10, 2, 3),),
+    (),
+    (),
+    ((11, 4, 0), (14, 0, 2, 1), (14, 1, 0, 0), (11, 1, 1),),
+    ((10, 3, 3), (12, 4, 3, 0),),
+    ((10, 2, 2), (14, 1, 0, 1),),
+    (),
+    ((11, 0, 0), (12, 4, 2, 0),),
+    (),
+    ((10, 3, 2), (11, 3, 3), (12, 0, 3, 0), (10, 3, 1), (14, 0, 1, 1), (12, 1, 3, 0), (12, 4, 3, 1), (11, 2, 3), (10, 3, 0), (12, 1, 2, 0),),
+    (),
+    ((14, 0, 0, 1), (11, 3, 2), (12, 0, 2, 0), (12, 3, 3, 0), (12, 4, 2, 1), (12, 4, 1, 1), (12, 0, 3, 1), (10, 2, 1), (11, 3, 1), (12, 4, 1, 0), (10, 2, 0),),
+    ((12, 1, 3, 1),),
+    ((12, 1, 2, 1), (12, 0, 2, 1), (12, 0, 1, 1), (11, 2, 2), (12, 3, 3, 1), (12, 2, 3, 0), (11, 2, 1), (12, 3, 2, 0), (14, 0, 0, 0), (12, 0, 1, 0),),
+    (),
+    ((12, 2, 2, 0), (12, 2, 1, 0), (11, 3, 0), (12, 1, 1, 1), (11, 1, 0), (12, 2, 3, 1), (12, 3, 1, 0), (12, 3, 2, 1), (12, 3, 1, 1), (12, 1, 1, 0),),
+    (),
+    ((11, 2, 0), (12, 0, 0, 0), (12, 2, 2, 1), (12, 2, 1, 1), (15, 1), (15, 0), (12, 4, 0, 1), (12, 3, 0, 0), (12, 0, 0, 1), (12, 4, 0, 0), (12, 1, 0, 0), (12, 3, 0, 1),),
+    (),
+    ((12, 2, 0, 1), (12, 1, 0, 1), (12, 2, 0, 0),),
 )
 BF, F32 = jnp.bfloat16, jnp.float32
 SUMS = ("bq", "bv", "bout", "bdown", "g1", "s1", "g2", "s2", "x", "mid", "res", "branch", "feed")
@@ -651,7 +656,7 @@
 def block_kernel(
     counts, x_ref, cot_ref, wqkv, wout, wup, wdown, bqv, bout, bup, bdown, g1, s1, g2, s2,
     act_out, gin_out, o_qkv, o_out, o_up, o_down, o_sums,
-    W, G2, G3, xh, yh, xf, yf, zl, yf2, zl2, xs2, xr2,
+    W, G2, G3, xh, yh, xf, yf, zl, units, xs2, xr2,
     rows1, dfeed, qkv, probs, heads, mid, rows2, act, gp, datt,
     tall, own_a, own_c, send_t, send_x, got, got_t, acc, acc_up, sums, sums_got,
     sem_in, ag_send, ag_recv, pg_send, pg_recv, rs_send, rs_recv, ps_send, ps_recv,
@@ -675,48 +680,28 @@
     loads = [
         pltpu.make_async_copy(src, W.at[here, pl.ds(c0, n)], sem_in.at[i])
         for i, (src, c0, n) in enumerate(
-            [(wqkv.at[j], QKV + 512 * j, 512) for j in range(3)]
+            [(wqkv.at[j, :, pl.ds(128 * h, 128)], QKV + 384 * h + 128 * j, 128) for h in range(4) for j in range(3)]
             + [(wout, OUT, 512), (wup.at[:, quarter], UP, 1024), (wdown.at[:, quarter], DOWN, 1024)]
         )
     ]
     for c in loads:
         c.start()
     enter(at)
-    g = Gather(at, W, shard, GATHERED, ag_send, ag_recv)
+    g = Gather(at, W, shard, PIECES, ag_send, ag_recv)
     pg = PairGather(at, W, shard, ((UP, 1024), (DOWN, 1024)), (wup, wdown), pg_send, pg_recv)
     for c in loads:
         c.wait()
 
-    def gather_step(kind, *a):
-        if kind == 0:
-            g.line(*a)
-        elif kind == 1:
-            g.plane(*a)
-        elif kind == 2:
-            pg.x_copy(*a).start()
-        elif kind == 3:
-            pg.line(*a)
-        elif kind == 4:
-            pg.cross(*a)
-        else:
-            shares.append(share(2, dfeed, spot(x, t), at.across_x()))
-
-    plan = list(GATHER_PLAN)
-
-    def gather(last):
-        while plan and len(GATHER_PLAN) - len(plan) <= last:
-            for step in plan.pop(0):
-                gather_step(*step)
-
-    home = {0: (G3, 0, 512), 1: (W, DOWN, DOWN + 512), 2: (W, DOWN + 512, COLS), 3: (G3, 512, 1024)}
-    sc = Scatter(at, lambda p: home[p], shard, SCATTERED, xh, yh, xf, yf, zl, rs_send, rs_recv)
+    home = {0: (W, DOWN, DOWN + 384), 1: (W, DOWN + 384, DOWN + 768), 2: (G3, 512, 896), 3: (W, OUT, OUT + 384), 4: (G3, 0, 512)}
+    sc = Scatter(at, lambda p: home[p], shard, PIECES, xh, yh, xf, yf, zl, rs_send, rs_recv)
     home_pair = {0: (W, UP, 1024), 1: (G2, 0, 1024)}
-    ps = PairScatter(at, lambda m: home_pair[m], shard, yf2, zl2, xs2, xr2, ps_send, ps_recv)
+    ps = PairScatter(at, lambda m: home_pair[m], shard, LINE_FIRST, units, xs2, xr2, ps_send, ps_recv)
 
     def write(p):
         def store(total):
-            if p < 3:
-                o_qkv[p] = total
+            if p < 4:
+                for j in range(3):
+                    o_qkv[j, :, 128 * p : 128 * (p + 1)] = total[:, 128 * j : 128 * (j + 1)]
             else:
                 o_out[...] = total
         return store
@@ -728,26 +713,25 @@
             ref[:, pl.ds(pl.multiple_of(far_x * 1024, 1024), 1024)] = total
         return store
 
-    def scatter_step(kind, p, k=None):
-        if kind == 0:
-            sc.begin(p, k)
-        elif kind == 1:
-            sc.plane(p, k)
-        elif kind == 2:
-            sc.line(p, k, write(p))
-        elif kind == 3:
-            ps.begin(p, k)
-        elif kind == 4:
-            ps.line(p, k, write_pair(p))
-        else:
-            ps.last(p, write_pair(p))
-
-    back_plan = list(SCATTER_PLAN)
-
-    def scatter(last):
-        while back_plan and len(SCATTER_PLAN) - len(back_plan) <= last:
-            for step in back_plan.pop(0):
-                scatter_step(*step)
+    def share_feed():
+        shares.append(share(2, dfeed, spot(x, t), at.across_x()))
+
+    actions = {
+        0: g.line, 1: g.plane, 2: lambda m: pg.x_copy(m).start(), 3: pg.line, 4: pg.cross, 5: share_feed,
+        10: sc.begin, 11: sc.plane, 12: lambda p, k, w: sc.line(p, k, w, write(p)),
+        13: ps.begin, 14: lambda m, k, w: ps.line(m, k, w, write_pair(m)), 15: lambda m: ps.last(m, write_pair(m)),
+        16: ps.line_first, 17: lambda m: ps.meet(m, write_pair(m)),
+    }
+    done = [0]
+
+    def run(part):
+        while done[0] <= min(part, len(PLAN) - 1):
+            for kind, *a in PLAN[done[0]]:
+                actions[kind](*a)
+            done[0] += 1
+
+    def quiet(part):
+        return part >= len(PLAN) or not PLAN[part]
 
     def send(i, src, dst, other):
         return pltpu.make_async_remote_copy(
@@ -787,9 +771,9 @@
             return 0
         lax.fori_loop(first // size, last // size, go, 0)
 
-    def flip(src):
+    def flip(src, first=0):
         def body(c):
-            tall[pl.ds(c, 128), 0 : src.shape[0]] = src[:, pl.ds(c, 128)].T
+            tall[pl.ds(c, 128), first : first + src.shape[0]] = src[:, pl.ds(c, 128)].T
         tiles(0, src.shape[1], body, 128)
 
     def first_norm(b, r):
@@ -803,34 +787,30 @@
         dfeed[pl.ds(pl.multiple_of((x * 2 + t) * own + b, BLOCK), BLOCK), :] = low
         add("bdown", low.astype(F32))
 
-    gather(0)
+    run(0)
     each_block(first_norm)
     shares = [share(0, rows1, mine, at.twin()), share(1, dfeed, spot(x, t), at.twin())]
-    for p in range(3):
-        gather(1 + p)
-        g.finish(p)
-    take(0, rows1, theirs)
-    gather(5)
-
-    def project(c):
-        v = nn(rows1[...], W[:, pl.ds(c, 256)])
-        part = c // 512
-        inside = pl.ds(pl.multiple_of(c % 512 + t * 512, 256), 256)
-        bias = jnp.where(part == 0, bqv[0:1, inside], jnp.where(part == 2, bqv[1:2, inside], 0.0))
-        scale = jnp.where(part == 0, HD**-0.5, 1.0)
-        qkv[:, pl.ds(c, 256)] = ((v + bias) * scale).astype(BF)
-
-    tiles(0, 1536, project)
+
+    def project(j):
+        heads_of = pl.ds(pl.multiple_of(t * 512 + 128 * j, 128), 128)
+        cols = pl.ds(QKV + 384 * j, 384)
+        bias = jnp.concatenate([bqv[0:1, heads_of], jnp.zeros((1, 128), F32), bqv[1:2, heads_of]], axis=1)
+        scale = jnp.where(lax.broadcasted_iota(jnp.int32, (1, 384), 1) < 128, HD**-0.5, 1.0)
+
+        def body(i, _):
+            r = at_rows(i * own, own)
+            qkv[r, pl.ds(384 * j, 384)] = ((nn(rows1[r, :], W[:, cols]) + bias) * scale).astype(BF)
+            return 0
+        lax.fori_loop(0, 2, body, 0)
 
     first_lanes = lax.broadcasted_iota(jnp.int32, (own, 128), 1) < HD
 
-    def attend(it):
-        image, j = it // 4, it % 4
+    def attend(image, j):
         r = pl.ds(pl.multiple_of(image * own, own), own)
-        c = j * 128
-        q2 = qkv[r, pl.ds(pl.multiple_of(c, 128), 128)]
-        k2 = qkv[r, pl.ds(pl.multiple_of(c + 512, 128), 128)]
-        v_t = qkv[r, pl.ds(pl.multiple_of(c + 1024, 128), 128)].T
+        c = 384 * j
+        q2 = qkv[r, c : c + 128]
+        k2 = qkv[r, c + 128 : c + 256]
+        v_t = qkv[r, c + 256 : c + 384].T
         hide = jnp.where(valid_of(image, 0, own), 0.0, -1e30)
         outs = []
         for a in range(2):
@@ -838,39 +818,51 @@
             s = nt(k2, qm) + hide
             e = jnp.exp(s - jnp.max(s, axis=0, keepdims=True))
             low = (e * (1.0 / jnp.sum(e, axis=0, keepdims=True))).astype(BF)
-            probs[it * 2 + a] = low
+            probs[(j * 2 + image) * 2 + a] = low
             outs.append(nn(v_t[a * HD : (a + 1) * HD], low))
-        heads[r, pl.ds(pl.multiple_of(c, 128), 128)] = jnp.concatenate(outs, axis=0).T.astype(BF)
-
-    def attend_some(first, last, body):
-        def go(i, _):
-            body(i)
-            return 0
-        lax.fori_loop(first, last, go, 0)
-
-    first = 0
-    for i in range(1, 9):
-        if i == 8 or GATHER_PLAN[6 + i]:
-            gather(6 + first)
-            attend_some(first, i, attend)
-            first = i
-    gather(14)
-    g.finish(3)
-    gather(17)
-
-    def reduced(i, src, cols, keep):
-        def other(c):
+        heads[r, 128 * j : 128 * (j + 1)] = jnp.concatenate(outs, axis=0).T.astype(BF)
+
+    def images(part, body, j):
+        run(part)
+        if quiet(part + 1):
+            def go(i, _):
+                body(i, j)
+                return 0
+            lax.fori_loop(0, 2, go, 0)
+        else:
+            body(0, j)
+            run(part + 1)
+            body(1, j)
+
+    for j in range(4):
+        run(1 + 4 * j)
+        g.finish(j)
+        if j == 0:
+            take(0, rows1, theirs)
+        run(2 + 4 * j)
+        project(j)
+        images(3 + 4 * j, attend, j)
+    run(17)
+    g.finish(4)
+    run(18)
+
+    def others(i, src, cols, k):
+        def body(c):
             send_t[0, :, pl.ds(c, 256)] = nt(src[theirs, :], W[pl.ds(c, 256), cols]).astype(BF)
-        tiles(0, width, other)
-        copy = send(i, send_t.at[0], got.at[0 if i == 3 else 1], at.twin())
+        tiles(0, width, body)
+        copy = send(i, send_t.at[0], got.at[k], at.twin())
         copy.start()
-        def self(c):
+        return copy
+
+    def owns(src, cols, keep):
+        def body(c):
             keep[:, pl.ds(c, 256)] = nt(src[mine, :], W[pl.ds(c, 256), cols])
-        tiles(0, width, self)
-        return copy
-
-    branch_copy = reduced(3, heads, pl.ds(OUT, 512), own_a)
-    gather(18)
+        tiles(0, width, body)
+
+    branch_copy = others(3, heads, pl.ds(OUT, 512), 0)
+    run(19)
+    owns(heads, pl.ds(OUT, 512), own_a)
+    run(20)
     branch_copy.wait()
 
     def second_norm(b, r):
@@ -883,23 +875,33 @@
         n, _ = normed(m)
         rows2[pl.ds(pl.multiple_of((x * 2 + t) * own + b, BLOCK), BLOCK), :] = (n * g2[...] + s2[...]).astype(BF)
 
-    gather(19)
+    run(21)
     each_block(second_norm)
+    run(22)
     shares.append(share(4, rows2, spot(x, t), at.across_x()))
     shares.append(share(5, rows2, spot(x, t), at.twin()))
-    gather(22)
+    run(23)
 
     take(2, dfeed, spot(1 - x, t))
     shares.append(share(6, dfeed, spot(1 - x, t), at.twin()))
     take(1, dfeed, spot(x, 1 - t))
     take(6, dfeed, spot(1 - x, 1 - t))
-    gather(23)
+    run(24)
     flip(dfeed)
     take(5, rows2, spot(x, 1 - t))
 
     chip_rows = lambda far_x: at_rows(far_x * 2 * own, 2 * own)
 
-    def hidden(far_x):
+    def halves(part, body):
+        run(part)
+        if quiet(part + 1):
+            tiles(0, 1024, body)
+        else:
+            tiles(0, 512, body)
+            run(part + 1)
+            tiles(512, 1024, body)
+
+    def hidden(far_x, part):
         r = chip_rows(far_x)
 
         def body(c):
@@ -909,26 +911,24 @@
             dense = jnp.exp(-0.5 * u * u) * 0.3989422804014327
             act[r, pl.ds(c, 256)] = (u * below).astype(BF)
             gp[r, pl.ds(c, 256)] = (below + u * dense).astype(BF)
-        tiles(0, 1024, body)
+        halves(part, body)
 
     def grad_down(c):
         G2[:, pl.ds(c, 256)] = nn(tall[...], act[:, pl.ds(c, 256)]).astype(BF)
 
-    gather(24)
+    run(25)
     pg.finish(0)
-    gather(26)
-    hidden(x)
-    gather(28)
+    hidden(x, 26)
+    run(28)
     take(4, rows2, spot(1 - x, t))
     shares.append(share(7, rows2, spot(1 - x, t), at.twin()))
+    run(29)
     take(7, rows2, spot(1 - x, 1 - t))
-    gather(31)
-    hidden(1 - x)
-    gather(33)
-    tiles(0, 1024, grad_down)
-    gather(100)
-    scatter(1)
+    hidden(1 - x, 30)
+    halves(33, grad_down)
+    run(36)
     flip(rows2)
+    run(37)
 
     def back_act(far_x):
         r = chip_rows(far_x)
@@ -963,14 +963,14 @@
             def put(c, v):
                 send_x[self.n, :, c] = v.astype(BF)
             product(self.src, spot(1 - x, t), self.cols, put)
-            scatter(self.parts[0])
+            run(self.parts[0])
             first.wait()
 
             def body(b, r):
                 send_x[self.n, r, :] = send_x[self.n, r, :] + got_t[self.n, 0, r, :]
             each_block(body)
             self.cross = send(self.i + 2, send_x.at[self.n], got.at[2 + self.n], at.across_x())
-            scatter(self.parts[1])
+            run(self.parts[1])
             self.cross.start()
 
         def near(self):
@@ -985,33 +985,30 @@
             return self.keep[r, :] + got_t[self.n, 1, r, :].astype(F32) + got[2 + self.n, r, :].astype(F32)
 
     pg.finish(1)
-    scatter(2)
+    run(39)
     back_act(1 - x)
-    scatter(3)
-    two = Sum4(8, 0, gp, pl.ds(UP, 1024), own_a, (4, 5))
+    run(40)
+    two = Sum4(8, 0, gp, pl.ds(UP, 1024), own_a, (41, 42))
     two.far()
-    scatter(6)
+    run(43)
     back_act(x)
-    scatter(7)
+    run(44)
     two.near()
-    for p in range(4):
+    for p in range(5):
         g.drain(p)
     for m in range(2):
         pg.drain(m)
-    scatter(8)
 
     def grad_up(c):
         W[:, pl.ds(UP + c, 256)] = nn(tall[...], gp[:, pl.ds(c, 256)]).astype(BF)
 
-    tiles(0, 512, grad_up)
-    scatter(9)
-    tiles(512, 1024, grad_up)
-    scatter(11)
-    four = Sum4(11, 1, act, pl.ds(DOWN, 1024), own_c, (11, 12))
+    halves(45, grad_up)
+    run(48)
+    four = Sum4(11, 1, act, pl.ds(DOWN, 1024), own_c, (49, 50))
     four.far()
-    scatter(13)
+    run(51)
     four.near()
-    scatter(14)
+    run(52)
     two.cross.wait()
     for i in (1, 2, 5):
         shares[i].wait_send()
@@ -1028,39 +1025,50 @@
         dbr[pl.ds(pl.multiple_of(t * own + b, BLOCK), BLOCK), :] = low
         add("bout", low.astype(F32))
 
-    scatter(16)
+    run(54)
     each_block(second_back)
     shares.append(share(14, dbr, mine, at.twin()))
-    scatter(17)
+    run(55)
     take(14, dbr, theirs)
-    scatter(18)
+    run(56)
 
     def back_heads(c):
         datt[:, pl.ds(c, 256)] = nn(dbr[...], W[:, pl.ds(OUT + c, 256)]).astype(BF)
 
     tiles(0, 512, back_heads)
-    scatter(19)
+    run(57)
     flip(dbr)
-    scatter(20)
-    short = pl.ds(0, 2 * own)
+    run(58)
+    flip(rows1, 2 * own)
+    run(59)
+    short, rest = pl.ds(0, 2 * own), pl.ds(2 * own, 2 * own)
 
     def grad_out(c):
-        G3[:, pl.ds(512 + c, 256)] = nn(tall[:, short], heads[:, pl.ds(c, 256)]).astype(BF)
+        G3[:, pl.ds(c, 256)] = nn(tall[:, short], heads[:, pl.ds(c, 256)]).astype(BF)
 
     tiles(0, 512, grad_out)
-
-    def attend_back(it):
-        image, j = it // 4, it % 4
+    run(60)
+
+    def grad_heads(p):
+        ref, c0, c1 = home[p]
+
+        def body(i, _):
+            r = at_rows(i * 256, 256)
+            ref[r, c0:c1] = nn(tall[r, rest], dproj[:, 384 * p : 384 * (p + 1)]).astype(BF)
+            return 0
+        lax.fori_loop(0, width // 256, body, 0)
+
+    def attend_back(image, j):
         r = pl.ds(pl.multiple_of(image * own, own), own)
-        c = j * 128
-        q2 = qkv[r, pl.ds(pl.multiple_of(c, 128), 128)]
-        k_t = qkv[r, pl.ds(pl.multiple_of(c + 512, 128), 128)].T
-        v2 = qkv[r, pl.ds(pl.multiple_of(c + 1024, 128), 128)]
-        da = datt[r, pl.ds(pl.multiple_of(c, 128), 128)]
+        c = 384 * j
+        q2 = qkv[r, c : c + 128]
+        k_t = qkv[r, c + 128 : c + 256].T
+        v2 = qkv[r, c + 256 : c + 384]
+        da = datt[r, 128 * j : 128 * (j + 1)]
         dq, dk, dv = [], [], []
         for a in range(2):
             dam = jnp.where(first_lanes if a == 0 else ~first_lanes, da, jnp.zeros_like(da))
-            low = probs[it * 2 + a]
+            low = probs[(j * 2 + image) * 2 + a]
             p = low.astype(F32)
             dp = nt(v2, dam)
             ds = (p * (dp - jnp.sum(p * dp, axis=0, keepdims=True))).astype(BF)
@@ -1069,54 +1077,15 @@
             dv.append(nn(low, da))
         for base, v in (
             (0, jnp.concatenate(dq, axis=0).T * HD**-0.5),
-            (512, jnp.where(first_lanes, dk[0], dk[1])),
-            (1024, jnp.where(first_lanes, dv[0], dv[1])),
+            (128, jnp.where(first_lanes, dk[0], dk[1])),
+            (256, jnp.where(first_lanes, dv[0], dv[1])),
         ):
             v = v.astype(BF)
-            dproj[r, pl.ds(pl.multiple_of(base + c, 128), 128)] = v
-            if base != 512:
-                lanes = pl.ds(pl.multiple_of(t * 512 + c, 128), 128)
+            dproj[r, c + base : c + base + 128] = v
+            if base != 128:
+                lanes = pl.ds(pl.multiple_of(t * 512 + 128 * j, 128), 128)
                 ref = total_of["bq" if base == 0 else "bv"]
                 ref[:, lanes] += fold(v.astype(F32))
-
-    first = 0
-    for i in range(1, 9):
-        if i == 8 or SCATTER_PLAN[22 + i]:
-            scatter(22 + first)
-            attend_some(first, i, attend_back)
-            first = i
-
-    scatter(30)
-    one_copy = reduced(15, dproj, pl.ds(QKV, 1536), own_a)
-    scatter(32)
-    flip(rows1)
-
-    def grad_kv(c):
-        W[:, pl.ds(DOWN + c, 256)] = nn(tall[:, short], dproj[:, pl.ds(512 + c, 256)]).astype(BF)
-
-    def grad_q(c):
-        G3[:, pl.ds(c, 256)] = nn(tall[:, short], dproj[:, pl.ds(c, 256)]).astype(BF)
-
-    scatter(33)
-    tiles(0, 512, grad_kv)
-    scatter(35)
-    tiles(512, 1024, grad_kv)
-    scatter(37)
-    tiles(0, 512, grad_q)
-    scatter(39)
-    one_copy.wait()
-
-    def first_back(b, r):
-        dy = own_a[r, :] + got[1, r, :].astype(F32)
-        n, scale = normed(x_ref[r, :].astype(F32))
-        add("g1", dy * n)
-        add("s1", dy)
-        gin_out[r, :] += norm_back(dy, n, scale, g1[...])
-
-    scatter(40)
-    each_block(first_back)
-    scatter(41)
-    four.cross.wait()
 
     def finish_feed(b, r):
         keep = valid_of(t, b, BLOCK).astype(F32)
@@ -1126,9 +1095,34 @@
         add("res", keep * res * res)
         act_out[r, :] = (keep * res).astype(BF)
 
-    scatter(42)
+    for j in range(3):
+        images(61 + 4 * j, attend_back, j)
+        run(63 + 4 * j)
+        grad_heads(j)
+    run(73)
+    four.cross.wait()
+    run(74)
     each_block(finish_feed)
-    scatter(43)
+    images(75, attend_back, 3)
+    run(77)
+    one_copy = others(15, dproj, pl.ds(QKV, 1536), 1)
+    run(78)
+    grad_heads(3)
+    run(80)
+    owns(dproj, pl.ds(QKV, 1536), own_a)
+    run(81)
+    one_copy.wait()
+    run(82)
+
+    def first_back(b, r):
+        dy = own_a[r, :] + got[1, r, :].astype(F32)
+        n, scale = normed(x_ref[r, :].astype(F32))
+        add("g1", dy * n)
+        add("s1", dy)
+        gin_out[r, :] += norm_back(dy, n, scale, g1[...])
+
+    each_block(first_back)
+    run(83)
 
     for i in range(8):
         sums[i : i + 1, :] = jnp.sum(acc[i], axis=0, keepdims=True)
@@ -1145,15 +1139,16 @@
             src_ref=sums, dst_ref=sums_got.at[i], send_sem=sums_send.at[i], recv_sem=sums_recv.at[i],
             device_id=other, device_id_type=MESH,
         )
+        run(84 + 2 * i)
         c.start()
-        scatter(45 + 2 * i)
+        run(85 + 2 * i)
         c.wait()
         sums[...] += sums_got[i]
     o_sums[...] = sums[...]
-    scatter(1000)
+    run(1000)
     for m in (1, 0):
         ps.drain(m)
-    for p in range(4):
+    for p in range(5):
         sc.drain(p)
     for i in (0, 3, 4, 6, 7):
         shares[i].wait_send()
@@ -1190,8 +1185,7 @@
             pltpu.VMEM((4, shard, 2048), BF),
             pltpu.VMEM((4, shard, 2048), BF),
             pltpu.VMEM((5, shard, 2048), BF),
-            pltpu.VMEM((2, 4, 2 * shard, 1024), BF),
-            pltpu.VMEM((2, 5, 2 * shard, 1024), BF),
+            pltpu.VMEM((18 + 2 * len(LINE_FIRST), 2 * shard, 1024), BF),
             pltpu.VMEM((2, shard, 1024), BF),
             pltpu.VMEM((2, shard, 1024), BF),
             pltpu.VMEM((group, width), BF),
@@ -1215,15 +1209,15 @@
             pltpu.VMEM((4, 8, 1024), F32),
             pltpu.VMEM((16, width), F32),
             pltpu.VMEM((5, 16, width), F32),
-            dma((6,)),
-            dma((4, 6, 4)),
-            dma((4, 5, 4)),
+            dma((15,)),
+            dma((5, 6, 4)),
+            dma((5, 5, 4)),
             dma((4, 4, 4)),
             dma((4, 3, 4)),
-            dma((4, 5, 4)),
-            dma((4, 5, 5)),
-            dma((2, 3, 4)),
-            dma((2, 3, 5)),
+            dma((5, 5, 4)),
+            dma((5, 5, 5)),
+            dma((2, 6, 4)),
+            dma((2, 6, 5)),
             dma((16,)),
             dma((16,)),
             dma((5,)),
@@ -1238,23 +1232,59 @@
     )
 
 
+def close_kernel(*refs):
+    big, sums, out, small, held, sem = refs[:6], refs[6], refs[7:13], refs[13:22], refs[22:28], refs[28]
+    loads = [pltpu.make_async_copy(a, h, sem.at[0, i]) for i, (a, h) in enumerate(zip(big, held))]
+    copies = [pltpu.make_async_copy(h, b, sem.at[1, i]) for i, (h, b) in enumerate(zip(held, out))]
+    for c in loads:
+        c.start()
+    place = lax.axis_index("dp") * 2 + lax.axis_index("tensor")
+    width = sums.shape[1]
+    turned = pltpu.roll(sums[0:8, :], width - place * 32, 1)
+    small[0][...] = turned[0:2, :32]
+    for i in range(1, 7):
+        small[i][...] = turned[i + 1 : i + 2, :32]
+    up = pl.ds(pl.multiple_of((place % 8) * 128, 128), 128)
+    which = lax.broadcasted_iota(jnp.int32, (8, 128), 0) == place // 8
+    small[7][...] = jnp.sum(jnp.where(which, sums[8:16, up], 0.0), axis=0, keepdims=True)
+    row = sums[12:13, :]
+    small[8][...] = jnp.sqrt(row[:, 0:5] / (row[:, 5:6] * width))
+    for load, c in zip(loads, copies):
+        load.wait()
+        c.start()
+    for c in copies:
+        c.wait()
+
+
+def close(*arrays):
+    vmem = pl.BlockSpec(memory_space=pltpu.VMEM)
+    hbm = pl.BlockSpec(memory_space=pl.ANY)
+    small = [(2, 32)] + [(1, 32)] * 6 + [(1, 128), (1, 5)]
+    return pl.pallas_call(
+        close_kernel,
+        out_shape=tuple(jax.ShapeDtypeStruct(a.shape, a.dtype) for a in arrays[:6])
+        + tuple(jax.ShapeDtypeStruct(n, F32) for n in small),
+        in_specs=[hbm] * 6 + [vmem],
+        out_specs=(hbm,) * 6 + (vmem,) * 9,
+        scratch_shapes=[pltpu.VMEM(a.shape, a.dtype) for a in arrays[:6]] + [pltpu.SemaphoreType.DMA((2, 6))],
+    )(*arrays)
+
+
 def local_fast(
     stream, counts, cotangent, w_qkv, b_qv, w_out, b_out, w_fc1, b_fc1, w_fc2, b_fc2,
     gain_one, shift_one, gain_two, shift_two,
 ):
-    acts, grad_in, p_qkv, p_out, p_up, p_down, sums = block(
-        counts, stream, cotangent, w_qkv, w_out.T, w_fc1, w_fc2.T, b_qv, b_out, b_fc1, b_fc2,
-        gain_one, shift_one, gain_two, shift_two,
-    )
-    place = lax.axis_index("dp") * 2 + lax.axis_index("tensor")
-    vectors = lax.dynamic_slice(sums[:8], (0, place * 32), (8, 32))
-    up = lax.dynamic_slice(sums[8:12].reshape(-1), (place * 128,), (128,))
-    rms = jnp.sqrt(sums[12, :5] / (sums[12, 5] * stream.shape[1]))
+    acts, grad_in, p_qkv, p_out, p_up, p_down, bqv, *rest = close(
+        *block(
+            counts, stream, cotangent, w_qkv, w_out.T, w_fc1, w_fc2.T, b_qv, b_out, b_fc1, b_fc2,
+            gain_one, shift_one, gain_two, shift_two,
+        )
+    )
+    bout, bdown, gain1, shift1, gain2, shift2, bup, rms = (v.reshape(-1) for v in rest[:8])
     return (
-        acts, grad_in, p_qkv, vectors[0:2], p_out.T, vectors[2], p_up, up, p_down.T, vectors[3],
-        vectors[4], vectors[5], vectors[6], vectors[7], rms,
-    )
-
+        acts, grad_in, p_qkv, bqv, p_out.T, bout, p_up, bup, p_down.T, bdown,
+        gain1, shift1, gain2, shift2, rms,
+    )
 
 def layer_norm(values, gain, shift):
     centre = jnp.mean(values, axis=-1, keepdims=True)

time: 208 us -> 188 us (0.904)
  local copies, waits for them, and re-layouts: 10.8 us -> 0 us
  Pallas kernels: 195 us -> 187 us
    pallas_call x1, Pallas kernels: 195 us -> 182 us  [block(): pl.pallas_call(block_kernel, out_shape=(jax.ShapeDtypeStruct((own, width)...]
    unnamed x18 -> x0, local copies, waits for them, and re-layouts: 6.93 us -> none
    pallas_call x0 -> x1, Pallas kernels: none -> 4.64 us  [close(): pl.pallas_call(close_kernel, out_shape=tuple((jax.ShapeDtypeStruct(a.shap...]
    slice x3 -> x0, local copies, waits for them, and re-layouts: 2.69 us -> none  [the longest x1 1.36 us: local_fast(): rms = jnp.sqrt(sums[12, :5] / (sums[12, 5] * stream.shape[1]))]
where the time goes in v5:
time: 188 us; the launch traced here: 187 us
  Pallas kernels  187 us (99%)
    pallas_call x1, Pallas kernels, block(): pl.pallas_call(block_kernel, out_shape=(jax.ShapeDtypeStruct((own, width)...  182 us
    pallas_call x1, Pallas kernels, close(): pl.pallas_call(close_kernel, out_shape=tuple((jax.ShapeDtypeStruct(a.shap...  4.64 us

profile of v5, /device:TPU:0, one launch (start us, length us, event | category | flops | bytes accessed | tf_op | source)
XLA Modules:
  0.0 187.4 jit_solution(13231558353890780681)
XLA Ops:
  0.7 181.9 %shard_map.262 = (bf16[320,1024]{1,0:T(8,128)(2,1)}, f32[320,1024]{1,0:T(8,128)}, f32[3,64,512]{2,1,0:T(8,128)}, f32[64,512]{1,0:T(8,128)}, f32[64,2048]{1,0:T(8...) custom-call(s32[2]{0:T(128)} %counts.1, bf16[320,1024]{1,0:T(8,128)(2,1)} %x_ref.1, bf16[320,1024]{1,0:T(8,128)(2,1)} %cot_ref.1, ...), custom_call_target="tpu_custom_call" | custom-call | tf_op jit(solution)/shard_map/pallas_call | solution.py:1166
  182.6 4.6 %shard_map.263 = (bf16[320,1024]{1,0:T(8,128)(2,1)}, f32[320,1024]{1,0:T(8,128)}, f32[3,64,512]{2,1,0:T(8,128)}, f32[64,512]{1,0:T(8,128)}, f32[64,2048]{1,0:T(8...) custom-call(bf16[320,1024]{1,0:T(8,128)(2,1)} %get-tuple-element.37., ...), custom_call_target="tpu_custom_call" | custom-call | tf_op jit(solution)/shard_map/pallas_call | solution.py:1263
